TPU v7x, 32 devices: a whole 2x2x4 slice. The times are simulated.
32 devices in a mesh: seq: 8 (over z, core), head: 4 (over y, x).
Axes of the slice: x: 2, y: 2, z: 4, core: 2. Of those that a mesh axis runs over, the one named last changes fastest.
Arguments:
- tokens: bfloat16 [64, 512, 1024], P('seq'), may hold values from -36 to 36
- lengths: int32 [64], P('seq'), may hold values from 1 to 512, 16384 in all
- attn_in: float32 [1024, 3, 1024], P(('seq', 'head')), may hold values from -0.4 to 0.4
- attn_out: float32 [1024, 1024], P(None, ('seq', 'head')), may hold values from -0.1875 to 0.1875
- mlp_in: float32 [1024, 4096], P(('seq', 'head')), may hold values from -0.1875 to 0.1875
- mlp_out: float32 [4096, 1024], P(None, ('seq', 'head')), may hold values from -0.09375 to 0.09375
- norm_gain: float32 [2, 1024], replicated, may hold values from 0.5 to 1.5
- norm_shift: float32 [2, 1024], replicated, may hold values from -3 to 3
Outputs:
- encoded: bfloat16 [64, 512, 1024], P('seq', 'head')
- key_cache: bfloat16 [64, 512, 1024], P('seq', None, 'head')
- value_cache: bfloat16 [64, 512, 1024], P('seq', None, 'head')
Inputs may be any that keep to these rules, and one draw needn't show every extreme that they name: `lengths`: some prompt has exactly 512 tokens.
All inputs are finite; a program needn't handle non-finite values. No bound on the sum of `lengths` on one device may be relied on, other than what follows from the above.
Results may differ from a plain program's by a relative error of at most 0.02.
Values may be sent and summed in bfloat16 or wider, within the bound.
No kernel may reach another device: no remote copies, remote signals or barrier semaphores. Data moves between devices by JAX's collectives and lax.ppermute only.
A program may use at most 128 MiB of HBM per device.

v0:
```python
import math

import jax
import jax.numpy as jnp
from jax import lax
from jax.sharding import PartitionSpec as P

DH = 64


EPSILON = 1e-05


def layer_norm(values, gain, shift):
    center = values - jnp.mean(values, axis=-1, keepdims=True)
    spread = jnp.mean(center * center, axis=-1, keepdims=True)
    return center * lax.rsqrt(spread + EPSILON) * gain + shift


def shards(tokens, lengths, attn_in, attn_out, mlp_in, mlp_out, norm_gain, norm_shift):
    heads_axis = lax.axis_size("head")
    head_index = lax.axis_index("head")
    prompts = tokens.shape[0]
    seq_len = tokens.shape[1]
    model_width = tokens.shape[2]
    hidden_width = mlp_in.shape[1]
    block_width = model_width // heads_axis
    hidden_block = hidden_width // heads_axis
    local_heads = block_width // DH
    in_cast = attn_in.astype(jnp.bfloat16)
    up_cast = mlp_in.astype(jnp.bfloat16)
    out_cast = attn_out.astype(jnp.bfloat16)
    down_cast = mlp_out.astype(jnp.bfloat16)
    whole_in, whole_up = (
        lax.all_gather(in_cast, ("seq", "head"), axis=0, tiled=True),
        lax.all_gather(up_cast, ("seq", "head"), axis=0, tiled=True),
    )
    whole_out, whole_down = (
        lax.all_gather(out_cast, ("seq", "head"), axis=1, tiled=True),
        lax.all_gather(down_cast, ("seq", "head"), axis=1, tiled=True),
    )
    qkv_weight = lax.dynamic_slice_in_dim(whole_in, head_index * block_width, block_width, 2)
    up_weight = lax.dynamic_slice_in_dim(whole_up, head_index * hidden_block, hidden_block, 1)
    proj_weight = lax.dynamic_slice_in_dim(whole_out, head_index * block_width, block_width, 0)
    down_weight = lax.dynamic_slice_in_dim(whole_down, head_index * hidden_block, hidden_block, 0)
    projected = jnp.einsum(
        "pld,dte->plte", tokens, qkv_weight, preferred_element_type=jnp.float32
    ).astype(jnp.bfloat16)
    positions = jnp.arange(seq_len, dtype=jnp.int32)
    inside = positions[None, :] < lengths[:, None]
    key_part = projected[:, :, 1]
    value_part = projected[:, :, 2]
    queries = projected[:, :, 0].reshape(prompts, seq_len, local_heads, DH)
    key_heads = key_part.reshape(prompts, seq_len, local_heads, DH)
    value_heads = value_part.reshape(prompts, seq_len, local_heads, DH)
    scores = jnp.einsum(
        "pqhd,pkhd->phqk", queries, key_heads, preferred_element_type=jnp.float32
    ) * (1.0 / math.sqrt(DH))
    scores = jnp.where(inside[:, None, None, :], scores, -1e30)
    row_peak = jnp.max(scores, axis=-1, keepdims=True)
    raised = jnp.exp(scores - row_peak)
    weights = (raised / jnp.sum(raised, axis=-1, keepdims=True)).astype(jnp.bfloat16)
    context = jnp.einsum(
        "phqk,pkhd->pqhd", weights, value_heads, preferred_element_type=jnp.float32
    )
    context = context.astype(jnp.bfloat16).reshape(prompts, seq_len, block_width)
    key_cache = jnp.where(inside[:, :, None], key_part, jnp.zeros_like(key_part))
    value_cache = jnp.where(inside[:, :, None], value_part, jnp.zeros_like(value_part))
    row_count = seq_len // heads_axis
    row_start = head_index * row_count
    attn_partial = jnp.einsum(
        "pld,de->ple", context, proj_weight, preferred_element_type=jnp.float32
    )
    attn_total = lax.psum(attn_partial.astype(jnp.bfloat16), "head").astype(jnp.float32)
    normed = layer_norm(
        tokens.astype(jnp.float32) + attn_total, norm_gain[0], norm_shift[0]
    ).astype(jnp.bfloat16)
    hidden = jax.nn.gelu(
        jnp.einsum("pld,df->plf", normed, up_weight, preferred_element_type=jnp.float32),
        approximate=False,
    ).astype(jnp.bfloat16)
    mlp_partial = jnp.einsum("plf,fe->ple", hidden, down_weight, preferred_element_type=jnp.float32)
    mlp_total = lax.psum(mlp_partial.astype(jnp.bfloat16), "head").astype(jnp.float32)
    mlp_rows = lax.dynamic_slice_in_dim(mlp_total, row_start, row_count, 1)
    normed_rows = lax.dynamic_slice_in_dim(normed, row_start, row_count, 1)
    finished = layer_norm(normed_rows.astype(jnp.float32) + mlp_rows, norm_gain[1], norm_shift[1])
    inside_rows = lax.dynamic_slice_in_dim(inside, row_start, row_count, 1)
    encoded = jnp.where(inside_rows[:, :, None], finished, 0.0).astype(jnp.bfloat16)
    return (encoded, key_cache, value_cache)


def solution(mesh):
    in_specs = (
        P("seq", None, None),
        P("seq"),
        P(("seq", "head"), None, None),
        P(None, ("seq", "head")),
        P(("seq", "head"), None),
        P(None, ("seq", "head")),
        P(),
        P(),
    )
    out_specs = (P("seq", "head", None), P("seq", None, "head"), P("seq", None, "head"))
    return jax.shard_map(shards, mesh=mesh, in_specs=in_specs, out_specs=out_specs, check_vma=False)
```

profile of v0, /device:TPU:15, one launch (start us, length us, event | category | flops | bytes accessed | tf_op | source)
XLA Modules:
  0.0 715.3 jit_solution(17648773107714358465)
XLA Ops:
  7.2 1.7 convert_element_type.55
  9.0 1.5 convert_element_type.61
  10.6 0.7 iota_compare_fusion
  11.3 70.4 %all-gather.5.cloned.1.call-done = bf16[1024,3,1024]{2,0,1:T(8,128)(2,1)} async-done(((bf16[32,3,1024]{2,0,1:T(8,128)(2,1)}), bf16[1024,3,1024]{2,0,1:T(8,128)(2,1)}) %all-gather.5.cloned.1.call-update) | async-done | bytes 6291472 | tf_op jit(solution)/shard_map/all_gather | solution.py:35
  81.7 9.6 %convert_bitcast_fusion = bf16[8,512,3,256]{1,3,0,2:T(8,128)(2,1)S(1)} fusion(bf16[8,512,1024]{2,1,0:T(8,128)(2,1)} %param.8, bf16[1024,3,1024]{2,0,1:T(8,128)(2,1)} %all-gather.5.cloned.1.call-done, s32[]{:T(128)S(6)} %select_n.29), kind=kOutput, calls=%fused_computation.41 | convolution fusion | flops 6445596672 | bytes 16252932 | tf_op jit(solution)/shard_map/pld,dte->plte/dot_general | solution.py:46
  91.4 2.7 copy-done
  94.1 2.4 fusion.92
  96.5 13.5 %fusion.95 = f32[8,4,512]{2,1,0:T(4,128)S(1)} fusion(pred[8,512]{1,0:T(8,128)(4,1)S(1)} %iota_compare_fusion, bf16[8,512,4,64]{1,3,2,0:T(8,128)(2,1)} %bitcast.56, bf16[8,512,4,64]{1,3,2,0:T(8,128)(2,1)S(1)} %bitcast.54), kind=kOutput, calls=%fused_computation.113 | convolution fusion | flops 1107296768 | bytes 4263936 | tf_op jit(solution)/shard_map/sub | solution.py:61
  110.1 16.1 %fusion.43 = bf16[8,4,64,512]{3,2,1,0:T(8,128)(2,1)S(1)} fusion(bf16[8,512,4,64]{1,3,2,0:T(8,128)(2,1)} %bitcast.58, f32[8,4,512]{2,1,0:T(4,128)S(1)} %fusion.95, pred[8,512]{1,0:T(8,128)(4,1)S(1)} %iota_compare_fusion, bf16[8,512,4,64]{1,3,2,0:T(8,128)(2,1)} %bitcast.57, bf16[8,512,4,64]{1,3,2,0:T(8,128)(2,1)} %bitcast.55), kind=kOutput, calls=%fused_computation.59 | convolution fusion | flops 2190492160 | bytes 8458240 | tf_op jit(solution)/shard_map/phqk,pkhd->pqhd/dot_general | solution.py:63
  126.2 12.6 %all-gather.7.cloned.1.call-done = bf16[1024,1024]{0,1:T(8,128)(2,1)} async-done(((bf16[1024,32]{0,1:T(8,128)(2,1)}), bf16[1024,1024]{0,1:T(8,128)(2,1)}) %all-gather.7.cloned.1.call-update) | async-done | bytes 2097168 | tf_op jit(solution)/shard_map/all_gather | solution.py:39
  138.8 6.7 convolution_convert_fusion
  145.6 0.7 convert_element_type.66
  146.3 0.0 all-gather.11.cloned.1.call-start
  146.4 0.7 convert_element_type.68
  147.1 0.0 all-reduce.5.cloned.1.call-start
  147.2 0.6 fusion.93
  147.8 0.6 fusion.94
  148.4 169.2 %all-reduce.3.cloned.1.call-done = bf16[8,512,1024]{2,1,0:T(8,128)(2,1)} async-done(((bf16[8,512,1024]{2,1,0:T(8,128)(2,1)}), bf16[8,512,1024]{2,1,0:T(8,128)(2,1)}) %all-reduce.3.cloned.1.call-update) | async-done | bytes 8388624 | tf_op jit(solution)/shard_map/psum | solution.py:74
  317.6 8.0 %fusion.16 = f32[8,512]{1,0:T(8,128)S(1)} fusion(bf16[8,512,1024]{2,1,0:T(8,128)(2,1)} %all-reduce.3.cloned.1.call-done, bf16[8,512,1024]{2,1,0:T(8,128)(2,1)} %param.8), kind=kLoop, calls=%fused_computation.35 | loop fusion | flops 16773120 | bytes 16793600 | tf_op jit(solution)/shard_map/reduce_sum | solution.py:15
  325.7 9.5 %multiply_reduce_fusion = f32[8,512]{1,0:T(8,128)S(1)} fusion(bf16[8,512,1024]{2,1,0:T(8,128)(2,1)} %all-reduce.3.cloned.1.call-done, bf16[8,512,1024]{2,1,0:T(8,128)(2,1)} %param.8, f32[8,512]{1,0:T(8,128)S(1)} %broadcast_multiply_fusion), kind=kLoop, calls=%fused_computation.28 | loop fusion | flops 25161728 | bytes 16809984 | tf_op jit(solution)/shard_map/reduce_sum | solution.py:16
  335.2 9.3 %add_convert_fusion = bf16[8,512,1024]{2,1,0:T(8,128)(2,1)} fusion(bf16[8,512,1024]{2,1,0:T(8,128)(2,1)S(1)} %bitcast.52, bf16[8,512,1024]{2,1,0:T(8,128)(2,1)} %param.8, f32[1024]{0:T(1024)S(1)} %bitcast.60, f32[1024]{0:T(1024)S(1)} %bitcast.59, f32[8,512]{1,0:T(8,128)S(1)} %add_rsqrt_fusion, f32[8,512]{1,0:T(8,128)S(1)} %broadcast_multiply_fusion), kind=kLoop, calls=%fused_computation.27 | loop fusion | flops 33554432 | bytes 25206784 | tf_op jit(solution)/shard_map/convert_element_type | solution.py:77
  344.6 54.8 %all-gather.9.cloned.1.call-done = bf16[1024,4096]{1,0:T(8,128)(2,1)} async-done(((bf16[32,4096]{1,0:T(8,128)(2,1)}), bf16[1024,4096]{1,0:T(8,128)(2,1)}) %all-gather.9.cloned.1.call-update) | async-done | bytes 8388624 | tf_op jit(solution)/shard_map/all_gather | solution.py:36
  399.4 21.1 %fusion.25 = (u8[512,1024]{1,0:T(8,128)(4,1)S(1)}, u8[512,1024]{1,0:T(8,128)(4,1)S(1)}, f32[8,512,1024]{2,1,0:T(8,128)}) fusion(bf16[8,512,1024]{2,1,0:T(8,128)(2,1)} %add_convert_fusion, bf16[1024,4096]{1,0:T(8,128)(2,1)} %all-gather.9.cloned.1.call-done, s32[]{:T(128)S(6)} %select_n.31), kind=kOutput, calls=%fused_computation.46 | convolution fusion | flops 8643411968 | bytes 28311556 | tf_op jit(solution)/shard_map/pld,df->plf/dot_general | solution.py:79
  420.4 58.8 %all-gather.11.cloned.1.call-done = bf16[4096,1024]{0,1:T(8,128)(2,1)} async-done(((bf16[4096,32]{0,1:T(8,128)(2,1)}), bf16[4096,1024]{0,1:T(8,128)(2,1)}) %all-gather.11.cloned.1.call-update) | async-done | bytes 8388624 | tf_op jit(solution)/shard_map/all_gather | solution.py:40
  479.3 47.6 %fusion.21 = bf16[8,512,1024]{2,1,0:T(8,128)(2,1)} fusion(f32[8,512,1024]{2,1,0:T(8,128)} %get-tuple-element.20, u8[512,1024]{1,0:T(8,128)(4,1)S(1)} %get-tuple-element.10, u8[512,1024]{1,0:T(8,128)(4,1)S(1)} %get-tuple-element.9, bf16[4096,1024]{0,1:T(8,128)(2,1)} %all-gather.11.cloned.1.call-done, s32[]{:T(128)S(6)} %select_n.31), kind=kOutput, calls=%fused_computation.40 | convolution fusion | flops 8887730176 | bytes 28311556 | tf_op jit(solution)/shard_map/plf,fe->ple/dot_general | solution.py:82
  526.9 3.8 bitcast_select_fusion
  530.8 3.9 copy.24
  534.7 2.4 copy.23
  537.1 160.9 %all-reduce.5.cloned.1.call-done = bf16[8,512,1024]{2,1,0:T(8,128)(2,1)} async-done(((bf16[8,512,1024]{2,1,0:T(8,128)(2,1)}), bf16[8,512,1024]{2,1,0:T(8,128)(2,1)}) %all-reduce.5.cloned.1.call-update) | async-done | bytes 8388624 | tf_op jit(solution)/shard_map/psum | solution.py:83
  698.0 2.8 fusion.27
  700.8 3.1 multiply_reduce_fusion.1
  704.0 4.0 select_convert_fusion
  (39 shorter events, 0.4 us)
Async XLA Ops:
  7.2 74.6 %all-gather.5.cloned.1.call-start = ((), (), s32[]{:S(2)}) async-start(), calls=%async_computation | async-start | bytes 6488064 | tf_op jit(solution)/shard_map/all_gather | solution.py:35
  8.9 129.9 %all-gather.7.cloned.1.call-start = ((), (), s32[]{:S(2)}) async-start(), calls=%async_computation.1 | async-start | bytes 2162688 | tf_op jit(solution)/shard_map/all_gather | solution.py:39
  10.6 307.1 %all-reduce.3.cloned.1.call-start = ((), (), s32[]{:S(2)}) async-start(), calls=%async_computation.2 | async-start | bytes 16777216 | tf_op jit(solution)/shard_map/psum | solution.py:74
  11.3 98.7 %copy-start.4 = (pred[8,512]{1,0:T(8,128)(4,1)}, pred[8,512]{1,0:T(8,128)(4,1)S(1)}, u32[]{:S(2)}) copy-start(pred[8,512]{1,0:T(8,128)(4,1)S(1)} %iota_compare_fusion) | copy-start | bytes 12292
  91.4 2.7 copy-start
  96.5 13.6 %copy-start.1 = (bf16[8,512,1,256]{1,3,0,2:T(8,128)(2,1)}, bf16[8,512,1,256]{1,3,0,2:T(8,128)(2,1)S(1)}, u32[]{:S(2)}) copy-start(bf16[8,512,1,256]{1,3,0,2:T(8,128)(2,1)S(1)} %get-tuple-element.13) | copy-start | bytes 6291460
  126.2 19.4 %copy-start.2 = (f32[32,4096]{1,0:T(8,128)S(1)}, f32[32,4096]{1,0:T(8,128)}, u32[]{:S(2)}) copy-start(f32[32,4096]{1,0:T(8,128)} %param.12) | copy-start | bytes 1572868
  126.2 20.2 %copy-start.3 = (f32[4096,32]{0,1:T(8,128)S(1)}, f32[4096,32]{0,1:T(8,128)}, u32[]{:S(2)}) copy-start(f32[4096,32]{0,1:T(8,128)} %param.13) | copy-start | bytes 1572868
  126.2 21.0 %copy-start.8 = (f32[2,1024]{1,0:T(2,128)S(1)}, f32[2,1024]{1,0:T(2,128)}, u32[]{:S(2)}) copy-start(f32[2,1024]{1,0:T(2,128)} %param.14) | copy-start | bytes 24580
  126.2 21.6 %copy-start.9 = (f32[2,1024]{1,0:T(2,128)S(1)}, f32[2,1024]{1,0:T(2,128)}, u32[]{:S(2)}) copy-start(f32[2,1024]{1,0:T(2,128)} %param.15) | copy-start | bytes 24580
  145.5 253.9 %all-gather.9.cloned.1.call-start = ((), (), s32[]{:S(2)}) async-start(), calls=%async_computation.3 | async-start | bytes 8650752 | tf_op jit(solution)/shard_map/all_gather | solution.py:36
  146.3 332.9 %all-gather.11.cloned.1.call-start = ((), (), s32[]{:S(2)}) async-start(), calls=%async_computation.4 | async-start | bytes 8650752 | tf_op jit(solution)/shard_map/all_gather | solution.py:40
  147.1 550.8 %all-reduce.5.cloned.1.call-start = ((), (), s32[]{:S(2)}) async-start(), calls=%async_computation.5 | async-start | bytes 16777216 | tf_op jit(solution)/shard_map/psum | solution.py:83
  325.6 9.6 %slice-start = ((s8[8388608]{0:T(1024)(128)(4,1)}), s8[4194304]{0:T(1024)(128)(4,1)S(1)}, s32[]{:S(2)}) async-start(s8[8388608]{0:T(1024)(128)(4,1)} %bitcast.51), calls=%async_computation.6 | async-start | bytes 8388608
  325.7 9.6 %slice-start.1 = ((s8[8388608]{0:T(1024)(128)(4,1)}), s8[4194304]{0:T(1024)(128)(4,1)S(1)}, s32[]{:S(2)}) async-start(s8[8388608]{0:T(1024)(128)(4,1)} %bitcast.51), calls=%async_computation.7 | async-start | bytes 8388608
  479.3 47.6 %copy-start.5 = (pred[8,512]{1,0:T(8,128)(4,1)S(1)}, pred[8,512]{1,0:T(8,128)(4,1)}, u32[]{:S(2)}) copy-start(pred[8,512]{1,0:T(8,128)(4,1)} %copy-done.4) | copy-start | bytes 12292
  526.9 177.1 %copy-start.6 = (f32[1,1024]{1,0:T(1,128)S(1)}, f32[1,1024]{1,0:T(1,128)}, u32[]{:S(2)}) copy-start(f32[1,1024]{1,0:T(1,128)} %get-tuple-element.17) | copy-start | bytes 12292
  526.9 177.1 %copy-start.7 = (f32[1,1024]{1,0:T(1,128)S(1)}, f32[1,1024]{1,0:T(1,128)}, u32[]{:S(2)}) copy-start(f32[1,1024]{1,0:T(1,128)} %get-tuple-element.19) | copy-start | bytes 12292
Sparse Core Ops, SparseCore 0:
  11.5 70.1 all-gather.4
  84.6 54.1 all-gather.6
  145.6 171.9 all-reduce.2
  321.3 77.9 all-gather.8
  403.1 76.1 all-gather.10
  527.0 170.9 all-reduce.4
where the time goes:
time: 725 us; the launch traced here: 715 us
  waiting for transfers between devices  527 us (73%)
  matrix products  115 us (16%)
  other arithmetic  46.1 us (6%)
  between operations  14.8 us (2%)
  local copies, waits for them, and re-layouts  12.7 us (2%)
    psum x1, waiting for transfers between devices, shards(): lax.psum(attn_partial.astype(jnp.bfloat16), 'head').astype(jnp.float32)  169 us
    psum x1, waiting for transfers between devices, shards(): lax.psum(mlp_partial.astype(jnp.bfloat16), 'head').astype(jnp.float32)  161 us
    all_gather x1, waiting for transfers between devices, shards(): lax.all_gather(in_cast, ('seq', 'head'), axis=0, tiled=True)  70.4 us
    all_gather x1, waiting for transfers between devices, shards(): lax.all_gather(down_cast, ('seq', 'head'), axis=1, tiled=True)  58.8 us
    all_gather x1, waiting for transfers between devices, shards(): lax.all_gather(up_cast, ('seq', 'head'), axis=0, tiled=True)  54.8 us
    dot_general x1, matrix products, shards(): jnp.einsum('plf,fe->ple', hidden, down_weight, preferred_element_type=jnp...  47.6 us
    dot_general x1, matrix products, shards(): jnp.einsum('pld,df->plf', normed, up_weight, preferred_element_type=jnp.f...  21.1 us
    dot_general x1, matrix products, shards(): jnp.einsum('phqk,pkhd->pqhd', weights, value_heads, preferred_element_typ...  16.1 us
  transfers between devices with their start and end apart: 6, of which 6 were waited for; matrix products, arithmetic and copies ran while one was open for 15% of the time, Pallas kernels for 0%

commit v1 on v0

v1 whole, which is shorter than its diff:
```python
import functools
import math

import jax
import jax.numpy as jnp
from jax import lax
from jax.experimental import pallas as pl
from jax.experimental.pallas import tpu as pltpu
from jax.sharding import PartitionSpec as P

DH = 64
EPSILON = 1e-05
TILE = 128
NT = (((1,), (1,)), ((), ()))
MIB = 1024 * 1024


def swap_seq(x, k):
    return lax.ppermute(x, "seq", [(i, i ^ k) for i in range(lax.axis_size("seq"))])


def swap_head(x, k):
    return lax.ppermute(x, "head", [(i, i ^ k) for i in range(lax.axis_size("head"))])


def gather_all(x):
    depths = list(range(0, lax.axis_size("seq"), 2))
    half = len(depths) // 2
    blocks = []
    for depth_list, first, second in ((depths[:half], 1, 2), (depths[half:], 2, 1)):
        own = jnp.concatenate([x if k == 0 else swap_seq(x, k) for k in depth_list], axis=0)
        one = swap_head(own, first)
        two = swap_head(own, second)
        both = swap_head(one, second)
        for block, h in ((own, 0), (one, first), (two, second), (both, 3)):
            blocks.append((block, [(k, h) for k in depth_list]))
    return blocks + [(swap_seq(b, 1), [(s ^ 1, h) for s, h in at]) for b, at in blocks]


def shard_copies(refs, places, place_ref, heads_axis, rows, columns, target, sem):
    copies = []
    for ref, at in zip(refs, places):
        for n, (s, h) in enumerate(at):
            index = (place_ref[0] ^ s) * heads_axis + (place_ref[1] ^ h)
            copies.append(
                pltpu.make_async_copy(
                    ref.at[pl.ds(n * rows, rows), pl.ds(columns[0], columns[1])],
                    target.at[pl.ds(pl.multiple_of(index * rows, rows), rows), :],
                    sem.at[len(copies)],
                )
            )
    return copies


def attention_kernel(places, heads_axis, rows, *refs):
    lengths_ref, place_ref, tokens_ref = refs[:3]
    weight_refs = refs[3 : 3 + len(places)]
    key_ref, value_ref = refs[3 + len(places) : 5 + len(places)]
    context_refs = refs[5 + len(places) : 5 + len(places) + heads_axis]
    weight, held, sem = refs[5 + len(places) + heads_axis :]
    prompt = pl.program_id(0)
    width = key_ref.shape[2]
    seq_len = key_ref.shape[1]
    row_count = context_refs[0].shape[1]

    @pl.when(prompt == 0)
    def _():
        copies = []
        for n, (ref, s) in enumerate(zip(weight_refs, places)):
            start = pl.multiple_of((place_ref[0] ^ s) * rows, rows)
            copies.append(pltpu.make_async_copy(ref, weight.at[pl.ds(start, rows), :], sem.at[n]))
        for copy in copies:
            copy.start()
        for copy in copies:
            copy.wait()

    length = lengths_ref[prompt]
    filled = (length + TILE - 1) // TILE
    lanes = lax.broadcasted_iota(jnp.int32, (1, width), 1) // DH

    def part(tiles):
        span = tiles * TILE
        projected = jnp.dot(tokens_ref[0, :span, :], weight[...], preferred_element_type=jnp.float32)
        queries = (projected[:, :width] * (math.log2(math.e) / math.sqrt(DH))).astype(jnp.bfloat16)
        keys = projected[:, width : 2 * width].astype(jnp.bfloat16)
        values = projected[:, 2 * width :].astype(jnp.bfloat16)
        inside = lax.broadcasted_iota(jnp.int32, (span, 1), 0) < length
        key_ref[0, :span, :] = jnp.where(inside, keys, jnp.zeros_like(keys))
        value_ref[0, :span, :] = jnp.where(inside, values, jnp.zeros_like(values))
        if span < seq_len:
            rest = jnp.zeros((seq_len - span, width), jnp.bfloat16)
            key_ref[0, span:, :] = rest
            value_ref[0, span:, :] = rest
            held[span:, :] = rest
        column = lax.broadcasted_iota(jnp.int32, (1, span), 1) < length
        context = jnp.zeros((span, width), jnp.float32)
        for head in range(width // DH):
            mine = lanes == head
            query = jnp.where(mine, queries, jnp.zeros_like(queries))
            scores = lax.dot_general(query, keys, NT, preferred_element_type=jnp.float32)
            scores = jnp.where(column, scores, -1e30)
            raised = jnp.exp2(scores - jnp.max(scores, axis=-1, keepdims=True))
            total = jnp.sum(raised, axis=-1, keepdims=True)
            out = jnp.dot(raised.astype(jnp.bfloat16), values, preferred_element_type=jnp.float32)
            context = jnp.where(mine, out * (1.0 / total), context)
        held[:span, :] = context.astype(jnp.bfloat16)

    for tiles in range(1, seq_len // TILE + 1):
        pl.when(filled == tiles)(functools.partial(part, tiles))
    for k, ref in enumerate(context_refs):
        start = pl.multiple_of((place_ref[1] ^ k) * row_count, row_count)
        ref[0] = held[pl.ds(start, row_count), :]


def attention(lengths, place, tokens, weight_blocks, heads_axis):
    prompts, seq_len, model_width = tokens.shape
    width = model_width // heads_axis
    row_count = seq_len // heads_axis
    rows = weight_blocks[0][0].shape[0]
    cache = jax.ShapeDtypeStruct((prompts, seq_len, width), jnp.bfloat16)
    piece = jax.ShapeDtypeStruct((prompts, row_count, width), jnp.bfloat16)
    by_prompt = lambda p, *_: (p, 0, 0)
    return pl.pallas_call(
        functools.partial(attention_kernel, [s for _, s in weight_blocks], heads_axis, rows),
        out_shape=[cache, cache] + [piece] * heads_axis,
        grid_spec=pltpu.PrefetchScalarGridSpec(
            num_scalar_prefetch=2,
            grid=(prompts,),
            in_specs=[pl.BlockSpec((1, seq_len, model_width), by_prompt)]
            + [pl.BlockSpec(memory_space=pl.ANY)] * len(weight_blocks),
            out_specs=[pl.BlockSpec((1, seq_len, width), by_prompt)] * 2
            + [pl.BlockSpec((1, row_count, width), by_prompt)] * heads_axis,
            scratch_shapes=[
                pltpu.VMEM((model_width, 3 * width), jnp.bfloat16),
                pltpu.VMEM((seq_len, width), jnp.bfloat16),
                pltpu.SemaphoreType.DMA((len(weight_blocks),)),
            ],
        ),
        compiler_params=pltpu.CompilerParams(vmem_limit_bytes=40 * MIB),
        cost_estimate=pl.CostEstimate(
            flops=2 * prompts * seq_len * model_width * 3 * width + 8 * prompts * seq_len * seq_len * width,
            bytes_accessed=4 * prompts * seq_len * model_width,
            transcendentals=prompts * seq_len * seq_len * width // DH,
        ),
        name="attention",
    )(lengths, place, tokens, *[block for block, _ in weight_blocks])


def normalize(values, gain, shift):
    center = values - jnp.mean(values, axis=-1, keepdims=True)
    spread = jnp.mean(center * center, axis=-1, keepdims=True)
    return center * lax.rsqrt(spread + EPSILON) * gain + shift


def project_kernel(places, heads_axis, rows, *refs):
    place_ref, tokens_ref = refs[:2]
    context_refs = refs[2 : 2 + heads_axis]
    weight_refs = refs[2 + heads_axis : 2 + heads_axis + len(places)]
    gain_ref, shift_ref, out_ref, weight, sem = refs[2 + heads_axis + len(places) :]

    @pl.when(pl.program_id(0) == 0)
    def _():
        copies = shard_copies(
            weight_refs, places, place_ref, heads_axis, rows, (0, weight.shape[1]), weight, sem
        )
        for copy in copies:
            copy.start()
        for copy in copies:
            copy.wait()

    count = out_ref.shape[0] * out_ref.shape[1]
    model_width = out_ref.shape[2]
    total = tokens_ref[...].reshape(count, model_width).astype(jnp.float32)
    for k, ref in enumerate(context_refs):
        width = ref.shape[2]
        start = pl.multiple_of((place_ref[1] ^ k) * width, width)
        total = total + lax.dot_general(
            ref[...].reshape(count, width),
            weight[:, pl.ds(start, width)],
            NT,
            preferred_element_type=jnp.float32,
        )
    normed = normalize(total, gain_ref[0:1, :], shift_ref[0:1, :])
    out_ref[...] = normed.astype(jnp.bfloat16).reshape(out_ref.shape)


def project(place, tokens, contexts, blocks, gain, shift, rows, steps):
    prompts, seq_len, model_width = tokens.shape
    heads_axis = len(contexts)
    row_count, width = contexts[0].shape[1:]
    group = prompts // steps
    places = [at for _, at in blocks]
    copies = sum(len(at) for at in places)
    return pl.pallas_call(
        functools.partial(project_kernel, places, heads_axis, rows),
        out_shape=jax.ShapeDtypeStruct((prompts, row_count, model_width), jnp.bfloat16),
        grid_spec=pltpu.PrefetchScalarGridSpec(
            num_scalar_prefetch=1,
            grid=(steps,),
            in_specs=[pl.BlockSpec((group, row_count, model_width), lambda p, place: (p, place[1], 0))]
            + [pl.BlockSpec((group, row_count, width), lambda p, place: (p, 0, 0))] * heads_axis
            + [pl.BlockSpec(memory_space=pl.ANY)] * len(blocks)
            + [pl.BlockSpec(gain.shape, lambda p, place: (0, 0))] * 2,
            out_specs=pl.BlockSpec((group, row_count, model_width), lambda p, place: (p, 0, 0)),
            scratch_shapes=[
                pltpu.VMEM((model_width, model_width), jnp.bfloat16),
                pltpu.SemaphoreType.DMA((copies,)),
            ],
        ),
        compiler_params=pltpu.CompilerParams(vmem_limit_bytes=40 * MIB),
        cost_estimate=pl.CostEstimate(
            flops=2 * prompts * row_count * model_width * model_width,
            bytes_accessed=8 * prompts * row_count * model_width,
            transcendentals=0,
        ),
        name="project",
    )(place, tokens, *contexts, *[block for block, _ in blocks], gain, shift)


def expand_kernel(places, heads_axis, rows, start_column, *refs):
    place_ref, normed_ref = refs[:2]
    weight_refs = refs[2 : 2 + len(places)]
    out_ref, weight, product, sem = refs[2 + len(places) :]
    step = pl.program_id(0)
    last = pl.num_programs(0) - 1
    chunk = out_ref.shape[1]

    @pl.when(step == 0)
    def _():
        copies = shard_copies(
            weight_refs, places, place_ref, heads_axis, rows, (start_column, weight.shape[1]), weight, sem
        )
        for copy in copies:
            copy.start()
        for copy in copies:
            copy.wait()

    def multiply():
        at = pl.multiple_of(step * chunk, chunk)
        product[lax.rem(step, 2)] = jnp.dot(
            normed_ref[...], weight[:, pl.ds(at, chunk)], preferred_element_type=jnp.float32
        )

    def activate():
        values = product[lax.rem(step + 1, 2)]
        out_ref[...] = (0.5 * values * (1.0 + lax.erf(values * math.sqrt(0.5)))).astype(jnp.bfloat16)

    @pl.when(step == 0)
    def _():
        multiply()

    @pl.when((step > 0) & (step < last))
    def _():
        multiply()
        activate()

    @pl.when(step == last)
    def _():
        activate()


def expand(place, normed, blocks, rows, start_column, hidden_width, heads_axis, chunk):
    count, model_width = normed.shape
    places = [at for _, at in blocks]
    copies = sum(len(at) for at in places)
    steps = hidden_width // chunk
    return pl.pallas_call(
        functools.partial(expand_kernel, places, heads_axis, rows, start_column),
        out_shape=jax.ShapeDtypeStruct((count, hidden_width), jnp.bfloat16),
        grid_spec=pltpu.PrefetchScalarGridSpec(
            num_scalar_prefetch=1,
            grid=(steps + 1,),
            in_specs=[pl.BlockSpec((count, model_width), lambda n, place: (0, 0))]
            + [pl.BlockSpec(memory_space=pl.ANY)] * len(blocks),
            out_specs=pl.BlockSpec((count, chunk), lambda n, place: (0, jnp.maximum(n - 1, 0))),
            scratch_shapes=[
                pltpu.VMEM((model_width, hidden_width), jnp.bfloat16),
                pltpu.VMEM((2, count, chunk), jnp.float32),
                pltpu.SemaphoreType.DMA((copies,)),
            ],
        ),
        compiler_params=pltpu.CompilerParams(vmem_limit_bytes=48 * MIB),
        cost_estimate=pl.CostEstimate(
            flops=2 * count * model_width * hidden_width,
            bytes_accessed=2 * (count + model_width) * hidden_width,
            transcendentals=count * hidden_width,
        ),
        name="expand",
    )(place, normed, *[block for block, _ in blocks])


def contract_kernel(lengths_ref, place_ref, hidden_ref, weight_ref, normed_ref, gain_ref, shift_ref, out_ref, total):
    step = pl.program_id(0)
    partial = lax.dot_general(hidden_ref[...], weight_ref[...], NT, preferred_element_type=jnp.float32)

    @pl.when(step == 0)
    def _():
        total[...] = partial

    @pl.when(step > 0)
    def _():
        total[...] += partial

    @pl.when(step == pl.num_programs(0) - 1)
    def _():
        prompts, row_count, _ = out_ref.shape
        for p in range(prompts):
            rows = slice(p * row_count, (p + 1) * row_count)
            finished = normalize(
                normed_ref[rows, :].astype(jnp.float32) + total[rows, :], gain_ref[1:2, :], shift_ref[1:2, :]
            )
            position = place_ref[1] * row_count + lax.broadcasted_iota(jnp.int32, (row_count, 1), 0)
            out_ref[p] = jnp.where(position < lengths_ref[p], finished, 0.0).astype(jnp.bfloat16)


def contract(lengths, place, hidden, weight, normed, gain, shift, prompts, steps):
    count, model_width = normed.shape
    chunk = hidden.shape[1] // steps
    row_count = count // prompts
    return pl.pallas_call(
        contract_kernel,
        out_shape=jax.ShapeDtypeStruct((prompts, row_count, model_width), jnp.bfloat16),
        grid_spec=pltpu.PrefetchScalarGridSpec(
            num_scalar_prefetch=2,
            grid=(steps,),
            in_specs=[
                pl.BlockSpec((count, chunk), lambda n, *_: (0, n)),
                pl.BlockSpec((model_width, chunk), lambda n, *_: (0, n)),
                pl.BlockSpec((count, model_width), lambda n, *_: (0, 0)),
                pl.BlockSpec(gain.shape, lambda n, *_: (0, 0)),
                pl.BlockSpec(gain.shape, lambda n, *_: (0, 0)),
            ],
            out_specs=pl.BlockSpec((prompts, row_count, model_width), lambda n, *_: (0, 0, 0)),
            scratch_shapes=[pltpu.VMEM((count, model_width), jnp.float32)],
        ),
        compiler_params=pltpu.CompilerParams(vmem_limit_bytes=48 * MIB),
        cost_estimate=pl.CostEstimate(
            flops=2 * count * model_width * hidden.shape[1],
            bytes_accessed=2 * (count + model_width) * hidden.shape[1],
            transcendentals=0,
        ),
        name="contract",
    )(lengths, place, hidden, weight, normed, gain, shift)


def shards(tokens, lengths, attn_in, attn_out, mlp_in, mlp_out, norm_gain, norm_shift):
    heads_axis = lax.axis_size("head")
    prompts, seq_len, model_width = tokens.shape
    hidden_width = mlp_in.shape[1]
    width = model_width // heads_axis
    row_count = seq_len // heads_axis
    rows = mlp_in.shape[0]
    place = jnp.stack([lax.axis_index("seq"), lax.axis_index("head")]).astype(jnp.int32)

    down_weight = lax.all_gather(mlp_out.T.astype(jnp.bfloat16), ("seq", "head"), axis=0, tiled=True)

    in_cast = attn_in.astype(jnp.bfloat16).reshape(rows, 3, heads_axis, width)
    in_cast = in_cast.transpose(2, 0, 1, 3).reshape(heads_axis, rows, 3 * width)
    in_rows = lax.all_to_all(in_cast, "head", 0, 0).reshape(heads_axis * rows, 3 * width)
    in_blocks = [(in_rows if s == 0 else swap_seq(in_rows, s), s) for s in range(0, lax.axis_size("seq"), 2)]
    in_blocks = in_blocks + [(swap_seq(block, 1), s ^ 1) for block, s in in_blocks]

    out_up = jnp.concatenate([attn_out.T, mlp_in], axis=1).astype(jnp.bfloat16)
    blocks = gather_all(out_up)

    key_cache, value_cache, *contexts = attention(lengths, place, tokens, in_blocks, heads_axis)
    contexts = [contexts[0]] + [swap_head(contexts[k], k) for k in range(1, heads_axis)]
    normed = project(place, tokens, contexts, blocks, norm_gain, norm_shift, rows, 2)
    normed = normed.reshape(prompts * row_count, model_width)
    hidden = expand(place, normed, blocks, rows, model_width, hidden_width, heads_axis, 512)
    encoded = contract(lengths, place, hidden, down_weight, normed, norm_gain, norm_shift, prompts, 4)
    return (encoded, key_cache, value_cache)


def solution(mesh):
    in_specs = (
        P("seq", None, None),
        P("seq"),
        P(("seq", "head"), None, None),
        P(None, ("seq", "head")),
        P(("seq", "head"), None),
        P(None, ("seq", "head")),
        P(),
        P(),
    )
    out_specs = (P("seq", "head", None), P("seq", None, "head"), P("seq", None, "head"))
    return jax.shard_map(shards, mesh=mesh, in_specs=in_specs, out_specs=out_specs, check_vma=False)
```

time: 725 us -> 217 us (0.30); the launches traced: 715 us -> 215 us
  waiting for transfers between devices: 527 us -> 104 us
  matrix products: 115 us -> 0 us
  Pallas kernels: 0 us -> 63.5 us
  other arithmetic: 46.1 us -> 3.95 us
  starting transfers between devices: 0.25 us -> 24.9 us
  local copies, waits for them, and re-layouts: 12.7 us -> 4.68 us
    psum x2 -> x0, waiting for transfers between devices: 330 us -> none  [the longest x1 169 us: shards(): lax.psum(attn_partial.astype(jnp.bfloat16), 'head').astype(jnp.float32)]
    all_gather x4 -> x1, waiting for transfers between devices: 197 us -> 0.02 us  [shards(): lax.all_gather(mlp_out.T.astype(jnp.bfloat16), ('seq', 'head'), axis=0, t...]
    ppermute x0 -> x27, waiting for transfers between devices: none -> 102 us  [the longest x9 53.2 us: swap_head(): lax.ppermute(x, 'head', [(i, i ^ k) for i in range(lax.axis_size('head'))])]
    dot_general x5 -> x0, matrix products: 101 us -> none  [the longest x1 47.6 us: shards(): jnp.einsum('plf,fe->ple', hidden, down_weight, preferred_element_type=jnp...]
    pallas_call x0 -> x4, Pallas kernels: none -> 63.5 us  [the longest x1 22.1 us: expand(): pl.pallas_call(functools.partial(expand_kernel, places, heads_axis, rows,...]
    reduce_sum x4 -> x0, other arithmetic: 23.5 us -> none  [the longest x2 12.6 us: layer_norm(): spread = jnp.mean(center * center, axis=-1, keepdims=True)]
    ppermute x0 -> x27, starting transfers between devices: none -> 21.2 us  [the longest x18 15.6 us: swap_seq(): lax.ppermute(x, 'seq', [(i, i ^ k) for i in range(lax.axis_size('seq'))])]
    convert_element_type x6 -> x2, other arithmetic: 18 us -> 1.83 us  [the longest x1 1.8 us: shards(): mlp_out.T.astype(jnp.bfloat16)]
  transfers between devices with their start and end apart: 6 -> 29, of which waited for: 6 -> 13; matrix products, arithmetic and copies ran while one was open for 15% -> 2% of each run, Pallas kernels for 0% -> 22%
where the time goes in v1:
time: 217 us; the launch traced here: 215 us
  waiting for transfers between devices  104 us (48%)
  Pallas kernels  63.5 us (29%)
  starting transfers between devices  24.9 us (11%)
  between operations  14.3 us (7%)
  local copies, waits for them, and re-layouts  4.68 us (2%)
  other arithmetic  3.95 us (2%)
    ppermute x9, waiting for transfers between devices, swap_head(): lax.ppermute(x, 'head', [(i, i ^ k) for i in range(lax.axis_size('head'))])  53.2 us
    ppermute x18, waiting for transfers between devices, swap_seq(): lax.ppermute(x, 'seq', [(i, i ^ k) for i in range(lax.axis_size('seq'))])  49.1 us
    pallas_call x1, Pallas kernels, expand(): pl.pallas_call(functools.partial(expand_kernel, places, heads_axis, rows,...  22.1 us
    pallas_call x1, Pallas kernels, attention(): pl.pallas_call(functools.partial(attention_kernel, [s for _, s in weight_...  16.9 us
    pallas_call x1, Pallas kernels, contract(): pl.pallas_call(contract_kernel, out_shape=jax.ShapeDtypeStruct((prompts,...  16.8 us
    ppermute x18, starting transfers between devices, swap_seq(): lax.ppermute(x, 'seq', [(i, i ^ k) for i in range(lax.axis_size('seq'))])  15.6 us
    pallas_call x1, Pallas kernels, project(): pl.pallas_call(functools.partial(project_kernel, places, heads_axis, rows...  7.78 us
    ppermute x9, starting transfers between devices, swap_head(): lax.ppermute(x, 'head', [(i, i ^ k) for i in range(lax.axis_size('head'))])  5.56 us
  transfers between devices with their start and end apart: 29, of which 13 were waited for; matrix products, arithmetic and copies ran while one was open for 2% of the time, Pallas kernels for 22%

profile of v1, /device:TPU:15, one launch (start us, length us, event | category | flops | bytes accessed | tf_op | source)
XLA Modules:
  0.0 215.1 jit_solution(4847085959097734370)
XLA Ops:
  7.2 1.8 convert_bitcast_fusion
  9.0 1.1 convert.8
  10.1 0.9 convert_bitcast_fusion.1
  11.1 2.4 %collective-permute-start.14 = (bf16[32,5120]{1,0:T(8,128)(2,1)S(1)}, bf16[32,5120]{1,0:T(8,128)(2,1)S(1)}, u32[]{:S(2)}, u32[]{:S(2)}) collective-permute-start(bf16[32,5120]{1,0:T(8,128)(2,1)S(1)} %pad_maximum_fusion.1), channel_id=1, source_target_pairs={{0,16},{4,20},{8,24},{12,28},{16,0},{20,4},{24,8},{28,12},{1,17},{... | collective-permute-start | bytes 983048 | tf_op jit(solution)/shard_map/ppermute | solution.py:19
  14.7 3.6 %all-to-all-start = ((bf16[4,32,768]{2,1,0:T(8,128)(2,1)}), bf16[4,32,768]{2,1,0:T(8,128)(2,1)S(1)}, u32[]{:S(2)}, u32[]{:S(2)}) async-start(bf16[4,32,768]{2,1,0:T(8,128)(2,1)} %reshape.19), calls=%async_computation | async-start | bytes 393216 | tf_op jit(solution)/shard_map/all_to_all | solution.py:359
  18.3 1.2 collective-permute-start.10
  19.6 1.5 all-to-all-done
  21.1 0.9 collective-permute-start.1
  22.0 16.4 %collective-permute-done.14 = bf16[32,5120]{1,0:T(8,128)(2,1)S(1)} collective-permute-done((bf16[32,5120]{1,0:T(8,128)(2,1)S(1)}, bf16[32,5120]{1,0:T(8,128)(2,1)S(1)}, u32[]{:S(2)}, u32[]{:S(2)}) %collective-permute-start.14) | collective-permute-done | bytes 327712 | tf_op jit(solution)/shard_map/ppermute | solution.py:19
  38.5 17.3 %collective-permute-done.15 = bf16[32,5120]{1,0:T(8,128)(2,1)S(1)} collective-permute-done((bf16[32,5120]{1,0:T(8,128)(2,1)S(1)}, bf16[32,5120]{1,0:T(8,128)(2,1)S(1)}, u32[]{:S(2)}, u32[]{:S(2)}) %collective-permute-start.15) | collective-permute-done | bytes 327712 | tf_op jit(solution)/shard_map/ppermute | solution.py:19
  56.2 1.8 collective-permute-start.3
  58.2 1.9 collective-permute-done.1.refs_5_
  60.6 9.0 %collective-permute-done.2.refs_6_ = bf16[128,768]{1,0:T(8,128)(2,1)S(1)} collective-permute-done((bf16[128,768]{1,0:T(8,128)(2,1)S(1)}, bf16[128,768]{1,0:T(8,128)(2,1)S(1)}, u32[]{:S(2)}, u32[]{:S(2)}) %collective-permute-start.2) | collective-permute-done | bytes 196640 | tf_op jit(solution)/shard_map/ppermute | solution.py:19
  69.6 1.2 collective-permute-start.6
  71.1 1.6 collective-permute-start.11
  72.9 1.5 collective-permute-done.16.refs_11_.refs_7_
  74.4 3.5 %collective-permute-start.19 = (bf16[64,5120]{1,0:T(8,128)(2,1)S(1)}, bf16[64,5120]{1,0:T(8,128)(2,1)S(1)}, u32[]{:S(2)}, u32[]{:S(2)}) collective-permute-start(bf16[64,5120]{1,0:T(8,128)(2,1)S(1)} %pad_maximum_fusion.refs_6_.refs_2_), channel_id=1, source_target_pairs={{0,4},{4,0},{8,12},{12,8},{16,20},{20,16},{24,28},{28,24},{1,5},{5... | collective-permute-start | bytes 1966088 | tf_op jit(solution)/shard_map/ppermute | solution.py:19
  77.9 3.4 %copy-done = bf16[8,512,1024]{2,1,0:T(8,128)(2,1)S(1)} copy-done((bf16[8,512,1024]{2,1,0:T(8,128)(2,1)S(1)}, bf16[8,512,1024]{2,1,0:T(8,128)(2,1)}, u32[]{:S(2)}) %copy-start) | copy-done | bytes 8388632
  81.2 16.9 %attention.1 = (bf16[8,512,256]{2,1,0:T(8,128)(2,1)}, bf16[8,512,256]{2,1,0:T(8,128)(2,1)}, bf16[8,128,256]{2,1,0:T(8,128)(2,1)S(1)}, bf16[8,128,256]{2,1,0:T(8,...) custom-call(s32[8]{0:T(128)S(1)} %copy-done.11, ...), custom_call_target="tpu_custom_call" | custom-call | flops 10737418240 | bytes 16777216 | tf_op jit(solution)/shard_map/attention/pallas_call | solution.py:123
  98.1 14.8 %collective-permute-done.11.refs_7_.refs_3_ = bf16[64,5120]{1,0:T(8,128)(2,1)S(1)} collective-permute-done((bf16[64,5120]{1,0:T(8,128)(2,1)S(1)}, bf16[64,5120]{1,0:T(8,128)(2,1)S(1)}, u32[]{:S(2)}, u32[]{:S(2)}) %collective-permute-start.11) | collective-permute-done | bytes 655392 | tf_op jit(solution)/shard_map/ppermute | solution.py:23
  112.9 1.5 collective-permute-start.18
  114.4 2.0 collective-permute-start.24
  116.5 1.4 collective-permute-start.8
  117.9 9.0 %collective-permute-done.7.refs_3_ = bf16[8,128,256]{2,1,0:T(8,128)(2,1)S(1)} collective-permute-done((bf16[8,128,256]{2,1,0:T(8,128)(2,1)S(1)}, bf16[8,128,256]{2,1,0:T(8,128)(2,1)S(1)}, u32[]{:S(2)}, u32[]{:S(2)}) %collective-permute-start.7) | collective-permute-done | bytes 524320 | tf_op jit(solution)/shard_map/ppermute | solution.py:23
  127.4 27.8 %collective-permute-done.8.refs_4_ = bf16[8,128,256]{2,1,0:T(8,128)(2,1)S(1)} collective-permute-done((bf16[8,128,256]{2,1,0:T(8,128)(2,1)S(1)}, bf16[8,128,256]{2,1,0:T(8,128)(2,1)S(1)}, u32[]{:S(2)}, u32[]{:S(2)}) %collective-permute-start.8) | collective-permute-done | bytes 524320 | tf_op jit(solution)/shard_map/ppermute | solution.py:23
  157.1 1.6 collective-permute-done.25.refs_20_.refs_16_
  158.7 0.9 collective-permute-done.21.refs_16_.refs_12_
  159.7 0.9 collective-permute-done.26.refs_21_.refs_17_
  160.6 0.9 collective-permute-done.22.refs_17_.refs_13_
  161.5 7.8 %project.1 = bf16[8,128,1024]{2,1,0:T(8,128)(2,1)} custom-call(s32[2]{0:T(128)S(1)} %pad_add_fusion.refs_1_.refs_0_.place_ref, bf16[8,512,1024]{2,1,0:T(8,128)(2,1)} %refs_1_.1, bf16[8,128,256]{2,1,0:T(8,128)(2,1)S(1)} %get-tuple-element.9.refs_2_, bf16[8,128,256]{2,1,0:T(8,128)(2,1)S(1)} %collective-permute-done.7.refs_3_, ...), custom_call_target="tpu_custom_call" | custom-call | flops 2147483648 | bytes 8388608 | tf_op jit(solution)/shard_map/project/pallas_call | solution.py:194
  169.4 22.1 %expand.1.hidden_ref = bf16[1024,4096]{1,0:T(8,128)(2,1)} custom-call(s32[2]{0:T(128)S(1)} %pad_add_fusion.refs_1_.refs_0_.place_ref, bf16[1024,1024]{1,0:T(8,128)(2,1)} %bitcast.13, bf16[64,5120]{1,0:T(8,128)(2,1)S(1)} %pad_maximum_fusion.refs_6_.refs_2_, bf16[64,5120]{1,0:T(8,128)(2,1)S(1)} %collective-permute-done.11.refs_7_.refs_3_, ...), custom_call_target="tpu_custom_call" | custom-call | flops 8589934592 | bytes 16777216 | tf_op jit(solution)/shard_map/expand/pallas_call | solution.py:267
  191.5 16.8 %contract.1 = bf16[8,128,1024]{2,1,0:T(8,128)(2,1)} custom-call(s32[8]{0:T(128)S(1)} %copy-done.11, s32[2]{0:T(128)S(1)} %pad_add_fusion.refs_1_.refs_0_.place_ref, bf16[1024,4096]{1,0:T(8,128)(2,1)} %expand.1.hidden_ref, bf16[1024,4096]{1,0:T(8,128)(2,1)} %all-gather.2.cloned.1.call-done.weight_ref, bf16[1024,1024]{1,0:T(8,128)(2,1)S(1)} %bitcast.14, ...), custom_call_target="tpu_custom_call" | custom-call | flops 8589934592 | bytes 16777216 | tf_op jit(solution)/shard_map/contract/pallas_call | solution.py:320
  (69 shorter events, 5.3 us)
Async XLA Ops:
  7.2 184.3 %all-gather.2.cloned.1.call-start = ((), (), s32[]{:S(2)}) async-start(), calls=%async_computation.1 | async-start | bytes 8650752 | tf_op jit(solution)/shard_map/all_gather | solution.py:355
  11.1 27.4 %collective-permute-start.14 = (bf16[32,5120]{1,0:T(8,128)(2,1)S(1)}, bf16[32,5120]{1,0:T(8,128)(2,1)S(1)}, u32[]{:S(2)}, u32[]{:S(2)}) collective-permute-start(bf16[32,5120]{1,0:T(8,128)(2,1)S(1)} %pad_maximum_fusion.1), channel_id=1, source_target_pairs={{0,16},{4,20},{8,24},{12,28},{16,0},{20,4},{24,8},{28,12},{1,17},{... | collective-permute-start | bytes 983048 | tf_op jit(solution)/shard_map/ppermute | solution.py:19
  13.5 64.4 %copy-start.11 = (s32[8]{0:T(128)S(1)}, s32[8]{0:T(128)}, u32[]{:S(2)}) copy-start(s32[8]{0:T(128)} %lengths_ref.1) | copy-start | bytes 100
  14.7 6.4 %all-to-all-start = ((bf16[4,32,768]{2,1,0:T(8,128)(2,1)}), bf16[4,32,768]{2,1,0:T(8,128)(2,1)S(1)}, u32[]{:S(2)}, u32[]{:S(2)}) async-start(bf16[4,32,768]{2,1,0:T(8,128)(2,1)} %reshape.19), calls=%async_computation | async-start | bytes 393216 | tf_op jit(solution)/shard_map/all_to_all | solution.py:359
  18.3 37.5 %collective-permute-start.15 = (bf16[32,5120]{1,0:T(8,128)(2,1)S(1)}, bf16[32,5120]{1,0:T(8,128)(2,1)S(1)}, u32[]{:S(2)}, u32[]{:S(2)}) collective-permute-start(bf16[32,5120]{1,0:T(8,128)(2,1)S(1)} %pad_maximum_fusion.1), channel_id=1, source_target_pairs={{0,24},{4,28},{8,16},{12,20},{16,8},{20,12},{24,0},{28,4},{1,25},{... | collective-permute-start | bytes 983048 | tf_op jit(solution)/shard_map/ppermute | solution.py:19
  18.3 37.9 %collective-permute-start.10 = (bf16[32,5120]{1,0:T(8,128)(2,1)S(1)}, bf16[32,5120]{1,0:T(8,128)(2,1)S(1)}, u32[]{:S(2)}, u32[]{:S(2)}) collective-permute-start(bf16[32,5120]{1,0:T(8,128)(2,1)S(1)} %pad_maximum_fusion.1), channel_id=1, source_target_pairs={{0,8},{4,12},{8,0},{12,4},{16,24},{20,28},{24,16},{28,20},{1,9},{5... | collective-permute-start | bytes 983048 | tf_op jit(solution)/shard_map/ppermute | solution.py:19
  21.1 37.0 %collective-permute-start = (bf16[128,768]{1,0:T(8,128)(2,1)S(1)}, bf16[128,768]{1,0:T(8,128)(2,1)S(1)}, u32[]{:S(2)}, u32[]{:S(2)}) collective-permute-start(bf16[128,768]{1,0:T(8,128)(2,1)S(1)} %bitcast.15), channel_id=1, source_target_pairs={{0,8},{4,12},{8,0},{12,4},{16,24},{20,28},{24,16},{28,20},{1,9},{5... | collective-permute-start | bytes 589832 | tf_op jit(solution)/shard_map/ppermute | solution.py:19
  21.1 38.9 %collective-permute-start.1 = (bf16[128,768]{1,0:T(8,128)(2,1)S(1)}, bf16[128,768]{1,0:T(8,128)(2,1)S(1)}, u32[]{:S(2)}, u32[]{:S(2)}) collective-permute-start(bf16[128,768]{1,0:T(8,128)(2,1)S(1)} %bitcast.16), channel_id=1, source_target_pairs={{0,16},{4,20},{8,24},{12,28},{16,0},{20,4},{24,8},{28,12},{1,17},{... | collective-permute-start | bytes 589832 | tf_op jit(solution)/shard_map/ppermute | solution.py:19
  38.5 31.1 %collective-permute-start.2 = (bf16[128,768]{1,0:T(8,128)(2,1)S(1)}, bf16[128,768]{1,0:T(8,128)(2,1)S(1)}, u32[]{:S(2)}, u32[]{:S(2)}) collective-permute-start(bf16[128,768]{1,0:T(8,128)(2,1)S(1)} %bitcast.17), channel_id=1, source_target_pairs={{0,24},{4,28},{8,16},{12,20},{16,8},{20,12},{24,0},{28,4},{1,25},{... | collective-permute-start | bytes 589832 | tf_op jit(solution)/shard_map/ppermute | solution.py:19
  55.9 18.5 %collective-permute-start.16 = (bf16[64,5120]{1,0:T(8,128)(2,1)S(1)}, bf16[64,5120]{1,0:T(8,128)(2,1)S(1)}, u32[]{:S(2)}, u32[]{:S(2)}) collective-permute-start(bf16[64,5120]{1,0:T(8,128)(2,1)S(1)} %constant_dynamic-update-slice_fusion.refs_10_.refs_6_), channel_id=1, source_target_pairs={{0,2},{1,3},{2,0},{3,1},{4,6},{5,7},{6,4},{7,5},{8,10},{9,11},{10,... | collective-permute-start | bytes 1966088 | tf_op jit(solution)/shard_map/ppermute | solution.py:23
  56.2 14.6 %collective-permute-start.3 = (bf16[128,768]{1,0:T(8,128)(2,1)S(1)}, bf16[128,768]{1,0:T(8,128)(2,1)S(1)}, u32[]{:S(2)}, u32[]{:S(2)}) collective-permute-start(bf16[128,768]{1,0:T(8,128)(2,1)S(1)} %bitcast.18), channel_id=1, source_target_pairs={{0,4},{4,0},{8,12},{12,8},{16,20},{20,16},{24,28},{28,24},{1,5},{5... | collective-permute-start | bytes 589832 | tf_op jit(solution)/shard_map/ppermute | solution.py:19
  58.1 12.9 %collective-permute-start.4 = (bf16[128,768]{1,0:T(8,128)(2,1)S(1)}, bf16[128,768]{1,0:T(8,128)(2,1)S(1)}, u32[]{:S(2)}, u32[]{:S(2)}) collective-permute-start(bf16[128,768]{1,0:T(8,128)(2,1)S(1)} %collective-permute-done.refs_4_), channel_id=1, source_target_pairs={{0,4},{4,0},{8,12},{12,8},{16,20},{20,16},{24,28},{28,24},{1,5},{5... | collective-permute-start | bytes 589832 | tf_op jit(solution)/shard_map/ppermute | solution.py:19
  60.1 11.0 %collective-permute-start.5 = (bf16[128,768]{1,0:T(8,128)(2,1)S(1)}, bf16[128,768]{1,0:T(8,128)(2,1)S(1)}, u32[]{:S(2)}, u32[]{:S(2)}) collective-permute-start(bf16[128,768]{1,0:T(8,128)(2,1)S(1)} %collective-permute-done.1.refs_5_), channel_id=1, source_target_pairs={{0,4},{4,0},{8,12},{12,8},{16,20},{20,16},{24,28},{28,24},{1,5},{5... | collective-permute-start | bytes 589832 | tf_op jit(solution)/shard_map/ppermute | solution.py:19
  69.6 3.1 %collective-permute-start.6 = (bf16[128,768]{1,0:T(8,128)(2,1)S(1)}, bf16[128,768]{1,0:T(8,128)(2,1)S(1)}, u32[]{:S(2)}, u32[]{:S(2)}) collective-permute-start(bf16[128,768]{1,0:T(8,128)(2,1)S(1)} %collective-permute-done.2.refs_6_), channel_id=1, source_target_pairs={{0,4},{4,0},{8,12},{12,8},{16,20},{20,16},{24,28},{28,24},{1,5},{5... | collective-permute-start | bytes 589832 | tf_op jit(solution)/shard_map/ppermute | solution.py:19
  70.8 90.7 %copy-start.9 = (f32[2,1024]{1,0:T(2,128)S(1)}, f32[2,1024]{1,0:T(2,128)}, u32[]{:S(2)}) copy-start(f32[2,1024]{1,0:T(2,128)} %gain_ref.1) | copy-start | bytes 24580
  70.8 90.7 %copy-start.10 = (f32[2,1024]{1,0:T(2,128)S(1)}, f32[2,1024]{1,0:T(2,128)}, u32[]{:S(2)}) copy-start(f32[2,1024]{1,0:T(2,128)} %shift_ref.1) | copy-start | bytes 24580
  70.9 42.1 %collective-permute-start.17 = (bf16[64,5120]{1,0:T(8,128)(2,1)S(1)}, bf16[64,5120]{1,0:T(8,128)(2,1)S(1)}, u32[]{:S(2)}, u32[]{:S(2)}) collective-permute-start(bf16[64,5120]{1,0:T(8,128)(2,1)S(1)} %constant_dynamic-update-slice_fusion.refs_10_.refs_6_), channel_id=1, source_target_pairs={{0,1},{1,0},{2,3},{3,2},{4,5},{5,4},{6,7},{7,6},{8,9},{9,8},{10,11... | collective-permute-start | bytes 1966088 | tf_op jit(solution)/shard_map/ppermute | solution.py:23
  71.0 43.4 %collective-permute-start.23 = (bf16[64,5120]{1,0:T(8,128)(2,1)S(1)}, bf16[64,5120]{1,0:T(8,128)(2,1)S(1)}, u32[]{:S(2)}, u32[]{:S(2)}) collective-permute-start(bf16[64,5120]{1,0:T(8,128)(2,1)S(1)} %constant_dynamic-update-slice_fusion.refs_10_.refs_6_), channel_id=1, source_target_pairs={{0,4},{4,0},{8,12},{12,8},{16,20},{20,16},{24,28},{28,24},{1,5},{5... | collective-permute-start | bytes 1966088 | tf_op jit(solution)/shard_map/ppermute | solution.py:19
  71.1 41.9 %collective-permute-start.11 = (bf16[64,5120]{1,0:T(8,128)(2,1)S(1)}, bf16[64,5120]{1,0:T(8,128)(2,1)S(1)}, u32[]{:S(2)}, u32[]{:S(2)}) collective-permute-start(bf16[64,5120]{1,0:T(8,128)(2,1)S(1)} %pad_maximum_fusion.refs_6_.refs_2_), channel_id=1, source_target_pairs={{0,1},{1,0},{2,3},{3,2},{4,5},{5,4},{6,7},{7,6},{8,9},{9,8},{10,11... | collective-permute-start | bytes 1966088 | tf_op jit(solution)/shard_map/ppermute | solution.py:23
  72.7 43.7 %collective-permute-start.12 = (bf16[64,5120]{1,0:T(8,128)(2,1)S(1)}, bf16[64,5120]{1,0:T(8,128)(2,1)S(1)}, u32[]{:S(2)}, u32[]{:S(2)}) collective-permute-start(bf16[64,5120]{1,0:T(8,128)(2,1)S(1)} %pad_maximum_fusion.refs_6_.refs_2_), channel_id=1, source_target_pairs={{0,2},{1,3},{2,0},{3,1},{4,6},{5,7},{6,4},{7,5},{8,10},{9,11},{10,... | collective-permute-start | bytes 1966088 | tf_op jit(solution)/shard_map/ppermute | solution.py:23
  74.4 42.1 %collective-permute-start.19 = (bf16[64,5120]{1,0:T(8,128)(2,1)S(1)}, bf16[64,5120]{1,0:T(8,128)(2,1)S(1)}, u32[]{:S(2)}, u32[]{:S(2)}) collective-permute-start(bf16[64,5120]{1,0:T(8,128)(2,1)S(1)} %pad_maximum_fusion.refs_6_.refs_2_), channel_id=1, source_target_pairs={{0,4},{4,0},{8,12},{12,8},{16,20},{20,16},{24,28},{28,24},{1,5},{5... | collective-permute-start | bytes 1966088 | tf_op jit(solution)/shard_map/ppermute | solution.py:19
  112.9 14.0 %collective-permute-start.7 = (bf16[8,128,256]{2,1,0:T(8,128)(2,1)S(1)}, bf16[8,128,256]{2,1,0:T(8,128)(2,1)S(1)}, u32[]{:S(2)}, u32[]{:S(2)}) collective-permute-start(bf16[8,128,256]{2,1,0:T(8,128)(2,1)S(1)} %get-tuple-element.10), channel_id=1, source_target_pairs={{0,1},{1,0},{2,3},{3,2},{4,5},{5,4},{6,7},{7,6},{8,9},{9,8},{10,11... | collective-permute-start | bytes 1572872 | tf_op jit(solution)/shard_map/ppermute | solution.py:23
  112.9 43.1 %collective-permute-start.18 = (bf16[64,5120]{1,0:T(8,128)(2,1)S(1)}, bf16[64,5120]{1,0:T(8,128)(2,1)S(1)}, u32[]{:S(2)}, u32[]{:S(2)}) collective-permute-start(bf16[64,5120]{1,0:T(8,128)(2,1)S(1)} %collective-permute-done.16.refs_11_.refs_7_), channel_id=1, source_target_pairs={{0,1},{1,0},{2,3},{3,2},{4,5},{5,4},{6,7},{7,6},{8,9},{9,8},{10,11... | collective-permute-start | bytes 1966088 | tf_op jit(solution)/shard_map/ppermute | solution.py:23
  114.4 42.2 %collective-permute-start.24 = (bf16[64,5120]{1,0:T(8,128)(2,1)S(1)}, bf16[64,5120]{1,0:T(8,128)(2,1)S(1)}, u32[]{:S(2)}, u32[]{:S(2)}) collective-permute-start(bf16[64,5120]{1,0:T(8,128)(2,1)S(1)} %collective-permute-done.16.refs_11_.refs_7_), channel_id=1, source_target_pairs={{0,4},{4,0},{8,12},{12,8},{16,20},{20,16},{24,28},{28,24},{1,5},{5... | collective-permute-start | bytes 1966088 | tf_op jit(solution)/shard_map/ppermute | solution.py:19
  116.4 40.2 %collective-permute-start.13 = (bf16[64,5120]{1,0:T(8,128)(2,1)S(1)}, bf16[64,5120]{1,0:T(8,128)(2,1)S(1)}, u32[]{:S(2)}, u32[]{:S(2)}) collective-permute-start(bf16[64,5120]{1,0:T(8,128)(2,1)S(1)} %collective-permute-done.11.refs_7_.refs_3_), channel_id=1, source_target_pairs={{0,2},{1,3},{2,0},{3,1},{4,6},{5,7},{6,4},{7,5},{8,10},{9,11},{10,... | collective-permute-start | bytes 1966088 | tf_op jit(solution)/shard_map/ppermute | solution.py:23
  116.5 38.7 %collective-permute-start.8 = (bf16[8,128,256]{2,1,0:T(8,128)(2,1)S(1)}, bf16[8,128,256]{2,1,0:T(8,128)(2,1)S(1)}, u32[]{:S(2)}, u32[]{:S(2)}) collective-permute-start(bf16[8,128,256]{2,1,0:T(8,128)(2,1)S(1)} %get-tuple-element.11), channel_id=1, source_target_pairs={{0,2},{1,3},{2,0},{3,1},{4,6},{5,7},{6,4},{7,5},{8,10},{9,11},{10,... | collective-permute-start | bytes 1572872 | tf_op jit(solution)/shard_map/ppermute | solution.py:23
  126.9 29.1 %collective-permute-start.9 = (bf16[8,128,256]{2,1,0:T(8,128)(2,1)S(1)}, bf16[8,128,256]{2,1,0:T(8,128)(2,1)S(1)}, u32[]{:S(2)}, u32[]{:S(2)}) collective-permute-start(bf16[8,128,256]{2,1,0:T(8,128)(2,1)S(1)} %get-tuple-element.12), channel_id=1, source_target_pairs={{0,3},{1,2},{2,1},{3,0},{4,7},{5,6},{6,5},{7,4},{8,11},{9,10},{10,... | collective-permute-start | bytes 1572872 | tf_op jit(solution)/shard_map/ppermute | solution.py:23
  155.2 3.5 %collective-permute-start.20 = (bf16[64,5120]{1,0:T(8,128)(2,1)S(1)}, bf16[64,5120]{1,0:T(8,128)(2,1)S(1)}, u32[]{:S(2)}, u32[]{:S(2)}) collective-permute-start(bf16[64,5120]{1,0:T(8,128)(2,1)S(1)} %collective-permute-done.11.refs_7_.refs_3_), channel_id=1, source_target_pairs={{0,4},{4,0},{8,12},{12,8},{16,20},{20,16},{24,28},{28,24},{1,5},{5... | collective-permute-start | bytes 1966088 | tf_op jit(solution)/shard_map/ppermute | solution.py:19
  156.1 2.7 %collective-permute-start.25 = (bf16[64,5120]{1,0:T(8,128)(2,1)S(1)}, bf16[64,5120]{1,0:T(8,128)(2,1)S(1)}, u32[]{:S(2)}, u32[]{:S(2)}) collective-permute-start(bf16[64,5120]{1,0:T(8,128)(2,1)S(1)} %collective-permute-done.17.refs_12_.refs_8_), channel_id=1, source_target_pairs={{0,4},{4,0},{8,12},{12,8},{16,20},{20,16},{24,28},{28,24},{1,5},{5... | collective-permute-start | bytes 1966088 | tf_op jit(solution)/shard_map/ppermute | solution.py:19
  156.1 3.6 %collective-permute-start.21 = (bf16[64,5120]{1,0:T(8,128)(2,1)S(1)}, bf16[64,5120]{1,0:T(8,128)(2,1)S(1)}, u32[]{:S(2)}, u32[]{:S(2)}) collective-permute-start(bf16[64,5120]{1,0:T(8,128)(2,1)S(1)} %collective-permute-done.12.refs_8_.refs_4_), channel_id=1, source_target_pairs={{0,4},{4,0},{8,12},{12,8},{16,20},{20,16},{24,28},{28,24},{1,5},{5... | collective-permute-start | bytes 1966088 | tf_op jit(solution)/shard_map/ppermute | solution.py:19
  156.6 4.0 %collective-permute-start.26 = (bf16[64,5120]{1,0:T(8,128)(2,1)S(1)}, bf16[64,5120]{1,0:T(8,128)(2,1)S(1)}, u32[]{:S(2)}, u32[]{:S(2)}) collective-permute-start(bf16[64,5120]{1,0:T(8,128)(2,1)S(1)} %collective-permute-done.18.refs_13_.refs_9_), channel_id=1, source_target_pairs={{0,4},{4,0},{8,12},{12,8},{16,20},{20,16},{24,28},{28,24},{1,5},{5... | collective-permute-start | bytes 1966088 | tf_op jit(solution)/shard_map/ppermute | solution.py:19
  156.7 4.9 %collective-permute-start.22 = (bf16[64,5120]{1,0:T(8,128)(2,1)S(1)}, bf16[64,5120]{1,0:T(8,128)(2,1)S(1)}, u32[]{:S(2)}, u32[]{:S(2)}) collective-permute-start(bf16[64,5120]{1,0:T(8,128)(2,1)S(1)} %collective-permute-done.13.refs_9_.refs_5_), channel_id=1, source_target_pairs={{0,4},{4,0},{8,12},{12,8},{16,20},{20,16},{24,28},{28,24},{1,5},{5... | collective-permute-start | bytes 1966088 | tf_op jit(solution)/shard_map/ppermute | solution.py:19
  (10 other events, 147.1 us)
Sparse Core Ops, SparseCore 0:
  10.9 119.2 all-gather.1

commit v2 on v1

v2 whole, which is shorter than its diff:
```python
import functools
import math

import jax
import jax.numpy as jnp
from jax import lax
from jax.experimental import pallas as pl
from jax.experimental.pallas import tpu as pltpu
from jax.sharding import PartitionSpec as P

DH = 64
EPSILON = 1e-05
TILE = 128
NT = (((1,), (1,)), ((), ()))
MIB = 1024 * 1024
ATTENTION_CALLS = 1


def swap_seq(x, k):
    return lax.ppermute(x, "seq", [(i, i ^ k) for i in range(lax.axis_size("seq"))])


def swap_head(x, k):
    return lax.ppermute(x, "head", [(i, i ^ k) for i in range(lax.axis_size("head"))])


def depths():
    return list(range(0, lax.axis_size("seq"), 2))


def after(x, *done):
    return lax.optimization_barrier((x, done))[0]


def along_depth(x):
    groups = [[d + core for d in depths()] for core in range(2)]
    return lax.all_gather(x, "seq", axis=0, tiled=True, axis_index_groups=groups)


def by_depth(x):
    return [x] + [swap_seq(x, k) for k in depths()[1:]]


def across_first(parts):
    half = len(parts) // 2
    lower, upper = jnp.concatenate(parts[:half], axis=0), jnp.concatenate(parts[half:], axis=0)
    return [[lower, swap_head(lower, 1), swap_head(lower, 2)], [upper, swap_head(upper, 2), swap_head(upper, 1)]]


def across_second(first):
    half = len(depths()) // 2
    blocks = []
    for (own, one, two), (a, b), at in zip(first, ((1, 2), (2, 1)), (depths()[:half], depths()[half:])):
        for block, h in ((own, 0), (one, a), (two, b), (swap_head(one, b), 3)):
            blocks.append((block, [(-1, s, h) for s in at]))
    return blocks


def cycle():
    seq = list(range(lax.axis_size("seq")))
    order = []
    for n in range(len(seq) // 2):
        for h in across_order()[:: 1 if n % 2 == 0 else -1]:
            order.extend([(2 * n, h), (2 * n + 1, h)])
    return order


def across_order():
    return [n ^ (n >> 1) for n in range(lax.axis_size("head"))]


def gather_cycle(x):
    heads = lax.axis_size("head")
    group = [s * heads + h for s, h in cycle()]
    return lax.all_gather(x, ("seq", "head"), axis=0, tiled=True, axis_index_groups=[group])


def other_core(blocks):
    return blocks + [(swap_seq(b, 1), [(m, s ^ 1, h) for m, s, h in at]) for b, at in blocks]


def shard_copies(refs, places, place_ref, heads_axis, rows, start, target, sem):
    copies = []
    for ref, at in zip(refs, places):
        for n, (mask, s, h) in enumerate(at):
            index = s * heads_axis + h if mask is None else (place_ref[0] & mask ^ s) * heads_axis + (place_ref[1] ^ h)
            copies.append(
                pltpu.make_async_copy(
                    ref.at[pl.ds(n * rows, rows), pl.ds(start, target.shape[1])],
                    target.at[pl.ds(index * rows if mask is None else pl.multiple_of(index * rows, rows), rows), :],
                    sem.at[len(copies)],
                )
            )
    return copies


def attention_kernel(places, heads_axis, rows, first, aliases, *refs):
    lengths_ref, place_ref, tokens_ref = refs[:3]
    weight_refs = refs[3 : 3 + len(places)]
    refs = refs[:3] + weight_refs + refs[3 + len(places) + aliases :]
    key_ref, value_ref = refs[3 + len(places) : 5 + len(places)]
    context_refs = refs[5 + len(places) : 5 + len(places) + heads_axis]
    weight, held, sem = refs[5 + len(places) + heads_axis :]
    prompt = pl.program_id(0)
    width = key_ref.shape[2]
    seq_len = key_ref.shape[1]
    row_count = context_refs[0].shape[1]

    @pl.when(prompt == 0)
    def _():
        copies = []
        for core, ref in zip(places, weight_refs):
            for depth in range(ref.shape[0] // rows):
                start = pl.multiple_of((place_ref[0] ^ (2 * depth + core)) * rows, rows)
                copies.append(
                    pltpu.make_async_copy(
                        ref.at[pl.ds(depth * rows, rows), :],
                        weight.at[pl.ds(start, rows), :],
                        sem.at[len(copies)],
                    )
                )
        for copy in copies:
            copy.start()
        for copy in copies:
            copy.wait()

    length = lengths_ref[first + prompt]
    filled = (length + TILE - 1) // TILE
    lanes = lax.broadcasted_iota(jnp.int32, (1, width), 1) // DH

    def part(tiles):
        span = tiles * TILE
        projected = jnp.dot(tokens_ref[0, :span, :], weight[...], preferred_element_type=jnp.float32)
        queries = (projected[:, :width] * (math.log2(math.e) / math.sqrt(DH))).astype(jnp.bfloat16)
        keys = projected[:, width : 2 * width].astype(jnp.bfloat16)
        values = projected[:, 2 * width :].astype(jnp.bfloat16)
        inside = lax.broadcasted_iota(jnp.int32, (span, 1), 0) < length
        key_ref[0, :span, :] = jnp.where(inside, keys, jnp.zeros_like(keys))
        value_ref[0, :span, :] = jnp.where(inside, values, jnp.zeros_like(values))
        if span < seq_len:
            rest = jnp.zeros((seq_len - span, width), jnp.bfloat16)
            key_ref[0, span:, :] = rest
            value_ref[0, span:, :] = rest
            held[span:, :] = rest
        column = lax.broadcasted_iota(jnp.int32, (1, span), 1) < length
        context = jnp.zeros((span, width), jnp.float32)
        for head in range(width // DH):
            mine = lanes == head
            query = jnp.where(mine, queries, jnp.zeros_like(queries))
            scores = lax.dot_general(query, keys, NT, preferred_element_type=jnp.float32)
            scores = jnp.where(column, scores, -1e30)
            raised = jnp.exp2(scores - jnp.max(scores, axis=-1, keepdims=True))
            total = jnp.sum(raised, axis=-1, keepdims=True)
            out = jnp.dot(raised.astype(jnp.bfloat16), values, preferred_element_type=jnp.float32)
            context = jnp.where(mine, out * (1.0 / total), context)
        held[:span, :] = context.astype(jnp.bfloat16)

    for tiles in range(1, seq_len // TILE + 1):
        pl.when(filled == tiles)(functools.partial(part, tiles))
    for k, ref in enumerate(context_refs):
        start = pl.multiple_of((place_ref[1] ^ k) * row_count, row_count)
        ref[0] = held[pl.ds(start, row_count), :]


def attention(lengths, place, tokens, weight_blocks, heads_axis, first, count, caches):
    prompts, seq_len, model_width = tokens.shape
    width = model_width // heads_axis
    row_count = seq_len // heads_axis
    rows = model_width // lax.axis_size("seq")
    cache = jax.ShapeDtypeStruct((prompts, seq_len, width), jnp.bfloat16)
    piece = jax.ShapeDtypeStruct((count, row_count, width), jnp.bfloat16)
    by_prompt = lambda p, *_: (p, 0, 0)
    shifted = lambda p, *_: (first + p, 0, 0)
    return pl.pallas_call(
        functools.partial(attention_kernel, [s for _, s in weight_blocks], heads_axis, rows, first, len(caches)),
        out_shape=[cache, cache] + [piece] * heads_axis,
        grid_spec=pltpu.PrefetchScalarGridSpec(
            num_scalar_prefetch=2,
            grid=(count,),
            in_specs=[pl.BlockSpec((1, seq_len, model_width), shifted)]
            + [pl.BlockSpec(memory_space=pl.ANY)] * (len(weight_blocks) + len(caches)),
            out_specs=[pl.BlockSpec((1, seq_len, width), shifted)] * 2
            + [pl.BlockSpec((1, row_count, width), by_prompt)] * heads_axis,
            scratch_shapes=[
                pltpu.VMEM((model_width, 3 * width), jnp.bfloat16),
                pltpu.VMEM((seq_len, width), jnp.bfloat16),
                pltpu.SemaphoreType.DMA((model_width // rows,)),
            ],
        ),
        input_output_aliases={3 + len(weight_blocks) + n: n for n in range(len(caches))},
        compiler_params=pltpu.CompilerParams(vmem_limit_bytes=62 * MIB),
        cost_estimate=pl.CostEstimate(
            flops=2 * count * seq_len * model_width * 3 * width + 8 * count * seq_len * seq_len * width,
            bytes_accessed=4 * count * seq_len * model_width,
            transcendentals=count * seq_len * seq_len * width // DH,
        ),
        name="attention",
    )(lengths, place, tokens, *[block for block, _ in weight_blocks], *caches)


def normalize(values, gain, shift):
    center = values - jnp.mean(values, axis=-1, keepdims=True)
    spread = jnp.mean(center * center, axis=-1, keepdims=True)
    return center * lax.rsqrt(spread + EPSILON) * gain + shift


def project_kernel(places, heads_axis, rows, start_column, *refs):
    place_ref, tokens_ref = refs[:2]
    halves = (len(refs) - 2 - len(places) - 5) // heads_axis
    context_refs = refs[2 : 2 + halves * heads_axis]
    weight_refs = refs[2 + halves * heads_axis : 2 + halves * heads_axis + len(places)]
    gain_ref, shift_ref, out_ref, weight, sem = refs[2 + halves * heads_axis + len(places) :]

    @pl.when(pl.program_id(0) == 0)
    def _():
        if places[0] is None:
            columns = pl.ds(start_column, weight.shape[1])
            copies = [pltpu.make_async_copy(weight_refs[0].at[:, columns], weight, sem.at[0])]
        else:
            copies = shard_copies(weight_refs, places, place_ref, heads_axis, rows, start_column, weight, sem)
        for copy in copies:
            copy.start()
        for copy in copies:
            copy.wait()

    count = out_ref.shape[0] * out_ref.shape[1]
    model_width = out_ref.shape[2]

    def half(own_refs):
        total = tokens_ref[...].reshape(count, model_width).astype(jnp.float32)
        for k, ref in enumerate(own_refs):
            width = ref.shape[2]
            start = pl.multiple_of((place_ref[1] ^ k) * width, width)
            total = total + lax.dot_general(
                ref[...].reshape(count, width),
                weight[:, pl.ds(start, width)],
                NT,
                preferred_element_type=jnp.float32,
            )
        normed = normalize(total, gain_ref[0:1, :], shift_ref[0:1, :])
        out_ref[...] = normed.astype(jnp.bfloat16).reshape(out_ref.shape)

    for n in range(halves):
        own_refs = context_refs[n * heads_axis : (n + 1) * heads_axis]
        pl.when(pl.program_id(0) * halves // pl.num_programs(0) == n)(functools.partial(half, own_refs))


def project(place, tokens, contexts, blocks, gain, shift, rows, start_column):
    prompts, seq_len, model_width = tokens.shape
    heads_axis = len(contexts[0])
    row_count, width = contexts[0][0].shape[1:]
    group = max(prompts // 4, 1)
    steps = prompts // group
    share = contexts[0][0].shape[0] // group
    places = [at for _, at in blocks]
    copies = 1 if places[0] is None else sum(len(at) for at in places)
    return pl.pallas_call(
        functools.partial(project_kernel, places, heads_axis, rows, start_column),
        out_shape=jax.ShapeDtypeStruct((prompts, row_count, model_width), jnp.bfloat16),
        grid_spec=pltpu.PrefetchScalarGridSpec(
            num_scalar_prefetch=1,
            grid=(steps,),
            in_specs=[pl.BlockSpec((group, row_count, model_width), lambda p, place: (p, place[1], 0))]
            + [pl.BlockSpec((group, row_count, width), lambda p, place: (lax.rem(p, share), 0, 0))] * (len(contexts) * heads_axis)
            + [pl.BlockSpec(memory_space=pl.ANY)] * len(blocks)
            + [pl.BlockSpec(gain.shape, lambda p, place: (0, 0))] * 2,
            out_specs=pl.BlockSpec((group, row_count, model_width), lambda p, place: (p, 0, 0)),
            scratch_shapes=[
                pltpu.VMEM((model_width, model_width), jnp.bfloat16),
                pltpu.SemaphoreType.DMA((copies,)),
            ],
        ),
        compiler_params=pltpu.CompilerParams(vmem_limit_bytes=40 * MIB),
        cost_estimate=pl.CostEstimate(
            flops=2 * prompts * row_count * model_width * model_width,
            bytes_accessed=8 * prompts * row_count * model_width,
            transcendentals=0,
        ),
        name="project",
    )(place, tokens, *[c for half in contexts for c in half], *[block for block, _ in blocks], gain, shift)


def mlp_kernel(
    order, rows, chunk, lengths_ref, place_ref, normed_ref, whole_ref, gain_ref, shift_ref, out_ref, *scratch
):
    up_weight, down_weight, products, total, sem = scratch
    step = pl.program_id(0)
    parts = pl.num_programs(0) - 1
    hidden_width = whole_ref.shape[1] // 2

    def fetch(kind, n):
        slot = lax.rem(n, 2)
        start = pl.multiple_of(kind * hidden_width + n * chunk, chunk)
        target = (up_weight, down_weight)[kind]
        return [
            pltpu.make_async_copy(
                whole_ref.at[pl.ds(k * rows, rows), pl.ds(start, chunk)],
                target.at[slot, pl.ds(index * rows, rows), :],
                sem.at[kind, slot, k],
            )
            for k, index in enumerate(order)
        ]

    def start(kind, n):
        for copy in fetch(kind, n):
            copy.start()

    def wait(kind, n):
        for copy in fetch(kind, n):
            copy.wait()

    pl.when(step == 0)(lambda: start(0, step))
    pl.when(step + 1 < parts)(lambda: start(0, step + 1))
    pl.when(step < parts)(lambda: start(1, step))
    pl.when(step < parts)(lambda: wait(0, step))
    pl.when(step > 0)(lambda: wait(1, step - 1))

    def up():
        slot = lax.rem(step, 2)
        products[slot] = jnp.dot(normed_ref[...], up_weight[slot], preferred_element_type=jnp.float32)

    def down(at):
        slot = lax.rem(step + 1, 2)
        values = products[slot, at, :]
        hidden = (0.5 * values * (1.0 + lax.erf(values * math.sqrt(0.5)))).astype(jnp.bfloat16)
        return lax.dot_general(hidden, down_weight[slot], NT, preferred_element_type=jnp.float32)

    everything = slice(0, normed_ref.shape[0])

    @pl.when(step == 0)
    def _():
        up()

    @pl.when(step == 1)
    def _():
        up()
        total[...] = down(everything)

    @pl.when((step > 1) & (step < parts))
    def _():
        up()
        total[...] += down(everything)

    @pl.when(step == parts)
    def _():
        prompts, row_count, _ = out_ref.shape
        position = place_ref[1] * row_count + lax.broadcasted_iota(jnp.int32, (row_count, 1), 0)
        pair = 2 if prompts % 2 == 0 else 1
        for p in range(0, prompts, pair):
            at = slice(p * row_count, (p + pair) * row_count)
            summed = normed_ref[at, :].astype(jnp.float32) + total[at, :] + down(at)
            finished = normalize(summed, gain_ref[1:2, :], shift_ref[1:2, :])
            for n in range(pair):
                part = finished[n * row_count : (n + 1) * row_count, :]
                inside = position < lengths_ref[p + n]
                out_ref[p + n] = jnp.where(inside, part, 0.0).astype(jnp.bfloat16)


def mlp(lengths, place, normed, whole, order, rows, gain, shift, prompts, chunk):
    count, model_width = normed.shape
    hidden_width = whole.shape[1] // 2
    row_count = count // prompts
    constant = lambda n, *_: (0, 0)
    return pl.pallas_call(
        functools.partial(mlp_kernel, order, rows, chunk),
        out_shape=jax.ShapeDtypeStruct((prompts, row_count, model_width), jnp.bfloat16),
        grid_spec=pltpu.PrefetchScalarGridSpec(
            num_scalar_prefetch=2,
            grid=(hidden_width // chunk + 1,),
            in_specs=[
                pl.BlockSpec((count, model_width), constant),
                pl.BlockSpec(memory_space=pl.ANY),
                pl.BlockSpec(gain.shape, constant),
                pl.BlockSpec(gain.shape, constant),
            ],
            out_specs=pl.BlockSpec((prompts, row_count, model_width), lambda n, *_: (0, 0, 0)),
            scratch_shapes=[
                pltpu.VMEM((2, model_width, chunk), jnp.bfloat16),
                pltpu.VMEM((2, model_width, chunk), jnp.bfloat16),
                pltpu.VMEM((2, count, chunk), jnp.float32),
                pltpu.VMEM((count, model_width), jnp.float32),
                pltpu.SemaphoreType.DMA((2, 2, len(order))),
            ],
        ),
        compiler_params=pltpu.CompilerParams(vmem_limit_bytes=60 * MIB),
        cost_estimate=pl.CostEstimate(
            flops=4 * count * model_width * hidden_width,
            bytes_accessed=4 * model_width * hidden_width + 6 * count * model_width,
            transcendentals=count * hidden_width,
        ),
        name="mlp",
    )(lengths, place, normed, whole, gain, shift)


def shards(tokens, lengths, attn_in, attn_out, mlp_in, mlp_out, norm_gain, norm_shift):
    heads_axis = lax.axis_size("head")
    prompts, seq_len, model_width = tokens.shape
    hidden_width = mlp_in.shape[1]
    width = model_width // heads_axis
    row_count = seq_len // heads_axis
    rows = mlp_in.shape[0]
    place = jnp.stack([lax.axis_index("seq"), lax.axis_index("head")]).astype(jnp.int32)
    half = hidden_width // 2
    quarter = hidden_width // 4

    def both(start, stop):
        return [mlp_in[:, start:stop], mlp_out.T[:, start:stop]]

    def packed(pieces):
        return jnp.concatenate(pieces, axis=1).astype(jnp.bfloat16)

    in_cast = attn_in.astype(jnp.bfloat16).reshape(rows, 3, heads_axis, width)
    in_cast = in_cast.transpose(2, 0, 1, 3).reshape(heads_axis, rows, 3 * width)
    in_rows = lax.all_to_all(in_cast, "head", 0, 0).reshape(heads_axis * rows, 3 * width)

    whole = gather_cycle(packed(both(0, hidden_width)))
    in_depth = jnp.concatenate(by_depth(in_rows), axis=0)
    out_parts = by_depth(after(attn_out.T.astype(jnp.bfloat16), in_depth))
    in_blocks = [(in_depth, 0), (swap_seq(in_depth, 1), 1)]

    contexts, caches, count = [], [], prompts // ATTENTION_CALLS
    for start in range(0, prompts, count):
        *caches, own, one, two, three = attention(
            lengths, place, tokens, in_blocks, heads_axis, start, count, caches
        )
        contexts.append([own, swap_head(one, 1), swap_head(two, 2), swap_head(three, 3)])
    out_blocks = other_core(across_second(across_first(out_parts)))
    normed = project(place, tokens, contexts, out_blocks, norm_gain, norm_shift, rows, 0)
    normed = normed.reshape(prompts * row_count, model_width)
    whole = after(whole, normed)
    order = [s * heads_axis + h for s, h in cycle()]
    encoded = mlp(lengths, place, normed, whole, order, rows, norm_gain, norm_shift, prompts, hidden_width // 4)
    return (encoded, caches[0], caches[1])


def solution(mesh):
    in_specs = (
        P("seq", None, None),
        P("seq"),
        P(("seq", "head"), None, None),
        P(None, ("seq", "head")),
        P(("seq", "head"), None),
        P(None, ("seq", "head")),
        P(),
        P(),
    )
    out_specs = (P("seq", "head", None), P("seq", None, "head"), P("seq", None, "head"))
    return jax.shard_map(shards, mesh=mesh, in_specs=in_specs, out_specs=out_specs, check_vma=False)
```

time: 217 us -> 193 us (0.89)
  waiting for transfers between devices: 104 us -> 71.2 us
  starting transfers between devices: 24.9 us -> 40.3 us
  Pallas kernels: 63.5 us -> 52.1 us
  blocking collectives: 0 us -> 5.93 us
    ppermute x18 -> x15, waiting for transfers between devices: 49.1 us -> 21.4 us  [swap_seq(): lax.ppermute(x, 'seq', [(i, i ^ k) for i in range(lax.axis_size('seq'))])]
    ppermute x9, waiting for transfers between devices: 53.2 us -> 30.4 us  [swap_head(): lax.ppermute(x, 'head', [(i, i ^ k) for i in range(lax.axis_size('head'))])]
    all_gather x1, waiting for transfers between devices: 0.02 us -> 19.4 us  [gather_cycle(): lax.all_gather(x, ('seq', 'head'), axis=0, tiled=True, axis_index_groups=...]
    ppermute x9, starting transfers between devices: 5.56 us -> 21.2 us  [swap_head(): lax.ppermute(x, 'head', [(i, i ^ k) for i in range(lax.axis_size('head'))])]
    pallas_call x2 -> x1, Pallas kernels: 38.8 us -> 27.5 us  [mlp(): pl.pallas_call(functools.partial(mlp_kernel, order, rows, chunk), out_sha...]
    all_to_all x0 -> x1, blocking collectives: none -> 5.93 us  [shards(): lax.all_to_all(in_cast, 'head', 0, 0).reshape(heads_axis * rows, 3 * width)]
    all_to_all x1 -> x0, starting transfers between devices: 3.63 us -> none  [shards(): lax.all_to_all(in_cast, 'head', 0, 0).reshape(heads_axis * rows, 3 * width)]
    ppermute x18 -> x15, starting transfers between devices: 15.6 us -> 19 us  [swap_seq(): lax.ppermute(x, 'seq', [(i, i ^ k) for i in range(lax.axis_size('seq'))])]
  transfers between devices with their start and end apart: 29 -> 25, of which waited for: 13 -> 17; matrix products, arithmetic and copies ran while one was open for 2% -> 1% of each run, Pallas kernels for 22% -> 13%
where the time goes in v2:
time: 193 us; the launch traced here: 191 us
  waiting for transfers between devices  71.2 us (37%)
  Pallas kernels  52.1 us (27%)
  starting transfers between devices  40.3 us (21%)
  between operations  14.2 us (7%)
  blocking collectives  5.93 us (3%)
  local copies, waits for them, and re-layouts  3.87 us (2%)
  other arithmetic  3.68 us (2%)
    ppermute x9, waiting for transfers between devices, swap_head(): lax.ppermute(x, 'head', [(i, i ^ k) for i in range(lax.axis_size('head'))])  30.4 us
    pallas_call x1, Pallas kernels, mlp(): pl.pallas_call(functools.partial(mlp_kernel, order, rows, chunk), out_sha...  27.5 us
    ppermute x15, waiting for transfers between devices, swap_seq(): lax.ppermute(x, 'seq', [(i, i ^ k) for i in range(lax.axis_size('seq'))])  21.4 us
    ppermute x9, starting transfers between devices, swap_head(): lax.ppermute(x, 'head', [(i, i ^ k) for i in range(lax.axis_size('head'))])  21.2 us
    all_gather x1, waiting for transfers between devices, gather_cycle(): lax.all_gather(x, ('seq', 'head'), axis=0, tiled=True, axis_index_groups=...  19.4 us
    ppermute x15, starting transfers between devices, swap_seq(): lax.ppermute(x, 'seq', [(i, i ^ k) for i in range(lax.axis_size('seq'))])  19 us
    pallas_call x1, Pallas kernels, attention(): pl.pallas_call(functools.partial(attention_kernel, [s for _, s in weight_...  15.1 us
    pallas_call x1, Pallas kernels, project(): pl.pallas_call(functools.partial(project_kernel, places, heads_axis, rows...  9.51 us
  transfers between devices with their start and end apart: 25, of which 17 were waited for; matrix products, arithmetic and copies ran while one was open for 1% of the time, Pallas kernels for 13%

profile of v2, /device:TPU:15, one launch (start us, length us, event | category | flops | bytes accessed | tf_op | source)
XLA Modules:
  0.0 191.4 jit_solution(17791043909980085152)
XLA Ops:
  7.2 1.1 convert.7
  8.3 1.1 convert_bitcast_fusion
  10.9 5.9 %all_to_all.5 = bf16[4,32,768]{2,1,0:T(8,128)(2,1)S(1)} all-to-all(bf16[4,32,768]{2,1,0:T(8,128)(2,1)S(1)} %reshape.19), channel_id=1, replica_groups=mesh['seq'=8,'head'=4] {'head'}, dimensions={0} | all-to-all | bytes 393216 | tf_op jit(solution)/shard_map/all_to_all | solution.py:414
  17.0 2.3 %collective-permute-start.1 = (bf16[128,768]{1,0:T(8,128)(2,1)S(1)}, bf16[128,768]{1,0:T(8,128)(2,1)S(1)}, u32[]{:S(2)}, u32[]{:S(2)}) collective-permute-start(bf16[128,768]{1,0:T(8,128)(2,1)S(1)} %bitcast.16), channel_id=1, source_target_pairs={{0,16},{4,20},{8,24},{12,28},{16,0},{20,4},{24,8},{28,12},{1,17},{... | collective-permute-start | bytes 589832 | tf_op jit(solution)/shard_map/ppermute | solution.py:20
  19.4 2.3 %collective-permute-done = bf16[128,768]{1,0:T(8,128)(2,1)S(1)} collective-permute-done((bf16[128,768]{1,0:T(8,128)(2,1)S(1)}, bf16[128,768]{1,0:T(8,128)(2,1)S(1)}, u32[]{:S(2)}, u32[]{:S(2)}) %collective-permute-start) | collective-permute-done | bytes 196640 | tf_op jit(solution)/shard_map/ppermute | solution.py:20
  21.7 4.5 %collective-permute-done.1 = bf16[128,768]{1,0:T(8,128)(2,1)S(1)} collective-permute-done((bf16[128,768]{1,0:T(8,128)(2,1)S(1)}, bf16[128,768]{1,0:T(8,128)(2,1)S(1)}, u32[]{:S(2)}, u32[]{:S(2)}) %collective-permute-start.1) | collective-permute-done | bytes 196640 | tf_op jit(solution)/shard_map/ppermute | solution.py:20
  26.2 9.1 %collective-permute-done.2 = bf16[128,768]{1,0:T(8,128)(2,1)S(1)} collective-permute-done((bf16[128,768]{1,0:T(8,128)(2,1)S(1)}, bf16[128,768]{1,0:T(8,128)(2,1)S(1)}, u32[]{:S(2)}, u32[]{:S(2)}) %collective-permute-start.2) | collective-permute-done | bytes 196640 | tf_op jit(solution)/shard_map/ppermute | solution.py:20
  35.4 2.7 %collective-permute-start.3 = (bf16[512,768]{1,0:T(8,128)(2,1)S(1)}, bf16[512,768]{1,0:T(8,128)(2,1)S(1)}, u32[]{:S(2)}, u32[]{:S(2)}) collective-permute-start(bf16[512,768]{1,0:T(8,128)(2,1)S(1)} %pad_maximum_fusion.refs_3_), channel_id=1, source_target_pairs={{0,4},{4,0},{8,12},{12,8},{16,20},{20,16},{24,28},{28,24},{1,5},{5... | collective-permute-start | bytes 2359304 | tf_op jit(solution)/shard_map/ppermute | solution.py:20
  38.8 1.3 collective-permute-start.12
  40.1 2.2 %collective-permute-start.7 = (bf16[32,1024]{1,0:T(8,128)(2,1)S(1)}, bf16[32,1024]{1,0:T(8,128)(2,1)S(1)}, u32[]{:S(2)}, u32[]{:S(2)}) collective-permute-start(bf16[32,1024]{1,0:T(8,128)(2,1)S(1)} %convert_bitcast_fusion.1), channel_id=1, source_target_pairs={{0,8},{4,12},{8,0},{12,4},{16,24},{20,28},{24,16},{28,20},{1,9},{5... | collective-permute-start | bytes 196616 | tf_op jit(solution)/shard_map/ppermute | solution.py:20
  42.8 2.7 %collective-permute-done.12 = bf16[32,1024]{1,0:T(8,128)(2,1)S(1)} collective-permute-done((bf16[32,1024]{1,0:T(8,128)(2,1)S(1)}, bf16[32,1024]{1,0:T(8,128)(2,1)S(1)}, u32[]{:S(2)}, u32[]{:S(2)}) %collective-permute-start.12) | collective-permute-done | bytes 65568 | tf_op jit(solution)/shard_map/ppermute | solution.py:20
  45.6 14.4 %collective-permute-start.13 = (bf16[64,1024]{1,0:T(8,128)(2,1)S(1)}, bf16[64,1024]{1,0:T(8,128)(2,1)S(1)}, u32[]{:S(2)}, u32[]{:S(2)}) collective-permute-start(bf16[64,1024]{1,0:T(8,128)(2,1)S(1)} %constant_dynamic-update-slice_fusion.2.refs_10_), channel_id=1, source_target_pairs={{0,2},{1,3},{2,0},{3,1},{4,6},{5,7},{6,4},{7,5},{8,10},{9,11},{10,... | collective-permute-start | bytes 393224 | tf_op jit(solution)/shard_map/ppermute | solution.py:24
  60.0 2.2 %collective-permute-start.14 = (bf16[64,1024]{1,0:T(8,128)(2,1)S(1)}, bf16[64,1024]{1,0:T(8,128)(2,1)S(1)}, u32[]{:S(2)}, u32[]{:S(2)}) collective-permute-start(bf16[64,1024]{1,0:T(8,128)(2,1)S(1)} %constant_dynamic-update-slice_fusion.2.refs_10_), channel_id=1, source_target_pairs={{0,1},{1,0},{2,3},{3,2},{4,5},{5,4},{6,7},{7,6},{8,9},{9,8},{10,11... | collective-permute-start | bytes 393224 | tf_op jit(solution)/shard_map/ppermute | solution.py:24
  62.4 3.6 %collective-permute-done.13.refs_11_ = bf16[64,1024]{1,0:T(8,128)(2,1)S(1)} collective-permute-done((bf16[64,1024]{1,0:T(8,128)(2,1)S(1)}, bf16[64,1024]{1,0:T(8,128)(2,1)S(1)}, u32[]{:S(2)}, u32[]{:S(2)}) %collective-permute-start.13) | collective-permute-done | bytes 131104 | tf_op jit(solution)/shard_map/ppermute | solution.py:24
  66.0 1.5 collective-permute-start.20
  67.5 0.9 copy-done.8
  68.4 15.1 %attention.1 = (bf16[8,512,256]{2,1,0:T(8,128)(2,1)}, bf16[8,512,256]{2,1,0:T(8,128)(2,1)}, bf16[8,128,256]{2,1,0:T(8,128)(2,1)}, bf16[8,128,256]{2,1,0:T(8,128)...) custom-call(s32[8]{0:T(128)} %lengths_ref.1, s32[2]{0:T(128)} %pad_add_fusion.refs_1_.refs_0_.place_ref, ...), custom_call_target="tpu_custom_call" | custom-call | flops 10737418240 | bytes 16777216 | tf_op jit(solution)/shard_map/attention/pallas_call | solution.py:174
  83.6 1.7 collective-permute-start.10
  85.4 1.1 collective-permute-start.5
  86.5 1.5 collective-permute-start.6
  88.0 2.6 %collective-permute-done.15.refs_13_ = bf16[64,1024]{1,0:T(8,128)(2,1)S(1)} collective-permute-done((bf16[64,1024]{1,0:T(8,128)(2,1)S(1)}, bf16[64,1024]{1,0:T(8,128)(2,1)S(1)}, u32[]{:S(2)}, u32[]{:S(2)}) %collective-permute-start.15) | collective-permute-done | bytes 131104 | tf_op jit(solution)/shard_map/ppermute | solution.py:24
  90.6 6.3 %collective-permute-start.21 = (bf16[64,1024]{1,0:T(8,128)(2,1)S(1)}, bf16[64,1024]{1,0:T(8,128)(2,1)S(1)}, u32[]{:S(2)}, u32[]{:S(2)}) collective-permute-start(bf16[64,1024]{1,0:T(8,128)(2,1)S(1)} %collective-permute-done.13.refs_11_), channel_id=1, source_target_pairs={{0,4},{4,0},{8,12},{12,8},{16,20},{20,16},{24,28},{28,24},{1,5},{5... | collective-permute-start | bytes 393224 | tf_op jit(solution)/shard_map/ppermute | solution.py:20
  96.9 0.9 collective-permute-start.17
  100.6 0.9 collective-permute-done.19.refs_17_
  101.5 11.5 %collective-permute-done.4.refs_3_ = bf16[8,128,256]{2,1,0:T(8,128)(2,1)S(1)} collective-permute-done((bf16[8,128,256]{2,1,0:T(8,128)(2,1)}, bf16[8,128,256]{2,1,0:T(8,128)(2,1)S(1)}, u32[]{:S(2)}, u32[]{:S(2)}) %collective-permute-start.4) | collective-permute-done | bytes 524320 | tf_op jit(solution)/shard_map/ppermute | solution.py:24
  112.9 11.5 %collective-permute-done.5.refs_4_ = bf16[8,128,256]{2,1,0:T(8,128)(2,1)S(1)} collective-permute-done((bf16[8,128,256]{2,1,0:T(8,128)(2,1)}, bf16[8,128,256]{2,1,0:T(8,128)(2,1)S(1)}, u32[]{:S(2)}, u32[]{:S(2)}) %collective-permute-start.5) | collective-permute-done | bytes 524320 | tf_op jit(solution)/shard_map/ppermute | solution.py:24
  124.4 1.3 collective-permute-done.6.refs_5_
  125.7 1.0 copy-done.1
  126.7 9.5 %project.1 = bf16[8,128,1024]{2,1,0:T(8,128)(2,1)S(1)} custom-call(s32[2]{0:T(128)S(1)} %copy-done.4, bf16[8,512,1024]{2,1,0:T(8,128)(2,1)} %refs_1_.1, bf16[8,128,256]{2,1,0:T(8,128)(2,1)S(1)} %copy-done.1, bf16[8,128,256]{2,1,0:T(8,128)(2,1)S(1)} %collective-permute-done.4.refs_3_, bf16[8,128,256]{2,1,0:T(8,128)(2,1)S(1)} %collective-permute-done.5.refs_4_, ...), custom_call_target="tpu_custom_call" | custom-call | flops 2147483648 | bytes 8388608 | tf_op jit(solution)/shard_map/project/pallas_call | solution.py:257
  136.3 1.3 copy-done
  137.6 19.4 %all-gather.2.cloned.1.call-done.whole_ref = bf16[1024,8192]{1,0:T(8,128)(2,1)} async-done(((bf16[32,8192]{1,0:T(8,128)(2,1)}), bf16[1024,8192]{1,0:T(8,128)(2,1)}) %all-gather.2.cloned.1.call-update) | async-done | bytes 16777232 | tf_op jit(solution)/shard_map/all_gather | solution.py:75
  157.0 27.5 %mlp.1 = bf16[8,128,1024]{2,1,0:T(8,128)(2,1)} custom-call(s32[8]{0:T(128)} %lengths_ref.1, s32[2]{0:T(128)} %pad_add_fusion.refs_1_.refs_0_.place_ref, bf16[1024,1024]{1,0:T(8,128)(2,1)} %bitcast.13, bf16[1024,8192]{1,0:T(8,128)(2,1)} %all-gather.2.cloned.1.call-done.whole_ref, f32[2,1024]{1,0:T(2,128)} %gain_ref.1, f32[2,1024]{1,0:T(2,128)} %shift_ref.1), custom_call_target="tpu_custom_call" | custom-call | flops 17179869184 | bytes 23068672 | tf_op jit(solution)/shard_map/mlp/pallas_call | solution.py:364
  (55 shorter events, 6.2 us)
Async XLA Ops:
  7.2 3.1 %copy-start.6 = (f32[32,3,1024]{2,0,1:T(8,128)S(1)}, f32[32,3,1024]{2,0,1:T(8,128)}, u32[]{:S(2)}) copy-start(f32[32,3,1024]{2,0,1:T(8,128)} %param.10) | copy-start | bytes 1179652
  7.2 149.8 %all-gather.2.cloned.1.call-start = ((), (), s32[]{:S(2)}) async-start(), calls=%async_computation.1 | async-start | bytes 17301504 | tf_op jit(solution)/shard_map/all_gather | solution.py:75
  10.3 27.8 %copy-start.7 = (f32[1024,32]{0,1:T(8,128)S(1)}, f32[1024,32]{0,1:T(8,128)}, u32[]{:S(2)}) copy-start(f32[1024,32]{0,1:T(8,128)} %param.11) | copy-start | bytes 393220
  16.8 4.9 %collective-permute-start = (bf16[128,768]{1,0:T(8,128)(2,1)S(1)}, bf16[128,768]{1,0:T(8,128)(2,1)S(1)}, u32[]{:S(2)}, u32[]{:S(2)}) collective-permute-start(bf16[128,768]{1,0:T(8,128)(2,1)S(1)} %bitcast.15), channel_id=1, source_target_pairs={{0,8},{4,12},{8,0},{12,4},{16,24},{20,28},{24,16},{28,20},{1,9},{5... | collective-permute-start | bytes 589832 | tf_op jit(solution)/shard_map/ppermute | solution.py:20
  17.0 9.3 %collective-permute-start.1 = (bf16[128,768]{1,0:T(8,128)(2,1)S(1)}, bf16[128,768]{1,0:T(8,128)(2,1)S(1)}, u32[]{:S(2)}, u32[]{:S(2)}) collective-permute-start(bf16[128,768]{1,0:T(8,128)(2,1)S(1)} %bitcast.16), channel_id=1, source_target_pairs={{0,16},{4,20},{8,24},{12,28},{16,0},{20,4},{24,8},{28,12},{1,17},{... | collective-permute-start | bytes 589832 | tf_op jit(solution)/shard_map/ppermute | solution.py:20
  19.3 16.0 %collective-permute-start.2 = (bf16[128,768]{1,0:T(8,128)(2,1)S(1)}, bf16[128,768]{1,0:T(8,128)(2,1)S(1)}, u32[]{:S(2)}, u32[]{:S(2)}) collective-permute-start(bf16[128,768]{1,0:T(8,128)(2,1)S(1)} %bitcast.17), channel_id=1, source_target_pairs={{0,24},{4,28},{8,16},{12,20},{16,8},{20,12},{24,0},{28,4},{1,25},{... | collective-permute-start | bytes 589832 | tf_op jit(solution)/shard_map/ppermute | solution.py:20
  35.4 33.0 %copy-start.5 = (bf16[512,768]{1,0:T(8,128)(2,1)}, bf16[512,768]{1,0:T(8,128)(2,1)S(1)}, u32[]{:S(2)}) copy-start(bf16[512,768]{1,0:T(8,128)(2,1)S(1)} %pad_maximum_fusion.refs_3_) | copy-start | bytes 2359300
  35.4 32.1 %collective-permute-start.3 = (bf16[512,768]{1,0:T(8,128)(2,1)S(1)}, bf16[512,768]{1,0:T(8,128)(2,1)S(1)}, u32[]{:S(2)}, u32[]{:S(2)}) collective-permute-start(bf16[512,768]{1,0:T(8,128)(2,1)S(1)} %pad_maximum_fusion.refs_3_), channel_id=1, source_target_pairs={{0,4},{4,0},{8,12},{12,8},{16,20},{20,16},{24,28},{28,24},{1,5},{5... | collective-permute-start | bytes 2359304 | tf_op jit(solution)/shard_map/ppermute | solution.py:20
  38.1 4.7 %collective-permute-start.11 = (bf16[32,1024]{1,0:T(8,128)(2,1)S(1)}, bf16[32,1024]{1,0:T(8,128)(2,1)S(1)}, u32[]{:S(2)}, u32[]{:S(2)}) collective-permute-start(bf16[32,1024]{1,0:T(8,128)(2,1)S(1)} %convert_bitcast_fusion.1), channel_id=1, source_target_pairs={{0,16},{4,20},{8,24},{12,28},{16,0},{20,4},{24,8},{28,12},{1,17},{... | collective-permute-start | bytes 196616 | tf_op jit(solution)/shard_map/ppermute | solution.py:20
  38.8 6.8 %collective-permute-start.12 = (bf16[32,1024]{1,0:T(8,128)(2,1)S(1)}, bf16[32,1024]{1,0:T(8,128)(2,1)S(1)}, u32[]{:S(2)}, u32[]{:S(2)}) collective-permute-start(bf16[32,1024]{1,0:T(8,128)(2,1)S(1)} %convert_bitcast_fusion.1), channel_id=1, source_target_pairs={{0,24},{4,28},{8,16},{12,20},{16,8},{20,12},{24,0},{28,4},{1,25},{... | collective-permute-start | bytes 196616 | tf_op jit(solution)/shard_map/ppermute | solution.py:20
  40.1 22.1 %collective-permute-start.7 = (bf16[32,1024]{1,0:T(8,128)(2,1)S(1)}, bf16[32,1024]{1,0:T(8,128)(2,1)S(1)}, u32[]{:S(2)}, u32[]{:S(2)}) collective-permute-start(bf16[32,1024]{1,0:T(8,128)(2,1)S(1)} %convert_bitcast_fusion.1), channel_id=1, source_target_pairs={{0,8},{4,12},{8,0},{12,4},{16,24},{20,28},{24,16},{28,20},{1,9},{5... | collective-permute-start | bytes 196616 | tf_op jit(solution)/shard_map/ppermute | solution.py:20
  45.6 20.4 %collective-permute-start.13 = (bf16[64,1024]{1,0:T(8,128)(2,1)S(1)}, bf16[64,1024]{1,0:T(8,128)(2,1)S(1)}, u32[]{:S(2)}, u32[]{:S(2)}) collective-permute-start(bf16[64,1024]{1,0:T(8,128)(2,1)S(1)} %constant_dynamic-update-slice_fusion.2.refs_10_), channel_id=1, source_target_pairs={{0,2},{1,3},{2,0},{3,1},{4,6},{5,7},{6,4},{7,5},{8,10},{9,11},{10,... | collective-permute-start | bytes 393224 | tf_op jit(solution)/shard_map/ppermute | solution.py:24
  60.0 23.6 %collective-permute-start.14 = (bf16[64,1024]{1,0:T(8,128)(2,1)S(1)}, bf16[64,1024]{1,0:T(8,128)(2,1)S(1)}, u32[]{:S(2)}, u32[]{:S(2)}) collective-permute-start(bf16[64,1024]{1,0:T(8,128)(2,1)S(1)} %constant_dynamic-update-slice_fusion.2.refs_10_), channel_id=1, source_target_pairs={{0,1},{1,0},{2,3},{3,2},{4,5},{5,4},{6,7},{7,6},{8,9},{9,8},{10,11... | collective-permute-start | bytes 393224 | tf_op jit(solution)/shard_map/ppermute | solution.py:24
  62.2 63.5 %copy-start.2 = (f32[2,1024]{1,0:T(2,128)S(1)}, f32[2,1024]{1,0:T(2,128)}, u32[]{:S(2)}) copy-start(f32[2,1024]{1,0:T(2,128)} %gain_ref.1) | copy-start | bytes 24580
  62.2 63.5 %copy-start.3 = (f32[2,1024]{1,0:T(2,128)S(1)}, f32[2,1024]{1,0:T(2,128)}, u32[]{:S(2)}) copy-start(f32[2,1024]{1,0:T(2,128)} %shift_ref.1) | copy-start | bytes 24580
  62.2 63.5 %copy-start.4 = (s32[2]{0:T(128)S(1)}, s32[2]{0:T(128)}, u32[]{:S(2)}) copy-start(s32[2]{0:T(128)} %pad_add_fusion.refs_1_.refs_0_.place_ref) | copy-start | bytes 28
  62.2 21.3 %collective-permute-start.8 = (bf16[64,1024]{1,0:T(8,128)(2,1)S(1)}, bf16[64,1024]{1,0:T(8,128)(2,1)S(1)}, u32[]{:S(2)}, u32[]{:S(2)}) collective-permute-start(bf16[64,1024]{1,0:T(8,128)(2,1)S(1)} %constant_dynamic-update-slice_fusion.refs_6_), channel_id=1, source_target_pairs={{0,1},{1,0},{2,3},{3,2},{4,5},{5,4},{6,7},{7,6},{8,9},{9,8},{10,11... | collective-permute-start | bytes 393224 | tf_op jit(solution)/shard_map/ppermute | solution.py:24
  62.3 23.0 %collective-permute-start.9 = (bf16[64,1024]{1,0:T(8,128)(2,1)S(1)}, bf16[64,1024]{1,0:T(8,128)(2,1)S(1)}, u32[]{:S(2)}, u32[]{:S(2)}) collective-permute-start(bf16[64,1024]{1,0:T(8,128)(2,1)S(1)} %constant_dynamic-update-slice_fusion.refs_6_), channel_id=1, source_target_pairs={{0,2},{1,3},{2,0},{3,1},{4,6},{5,7},{6,4},{7,5},{8,10},{9,11},{10,... | collective-permute-start | bytes 393224 | tf_op jit(solution)/shard_map/ppermute | solution.py:24
  66.0 19.4 %collective-permute-start.20 = (bf16[64,1024]{1,0:T(8,128)(2,1)S(1)}, bf16[64,1024]{1,0:T(8,128)(2,1)S(1)}, u32[]{:S(2)}, u32[]{:S(2)}) collective-permute-start(bf16[64,1024]{1,0:T(8,128)(2,1)S(1)} %constant_dynamic-update-slice_fusion.2.refs_10_), channel_id=1, source_target_pairs={{0,4},{4,0},{8,12},{12,8},{16,20},{20,16},{24,28},{28,24},{1,5},{5... | collective-permute-start | bytes 393224 | tf_op jit(solution)/shard_map/ppermute | solution.py:20
  68.4 18.1 %collective-permute-start.16 = (bf16[64,1024]{1,0:T(8,128)(2,1)S(1)}, bf16[64,1024]{1,0:T(8,128)(2,1)S(1)}, u32[]{:S(2)}, u32[]{:S(2)}) collective-permute-start(bf16[64,1024]{1,0:T(8,128)(2,1)S(1)} %constant_dynamic-update-slice_fusion.refs_6_), channel_id=1, source_target_pairs={{0,4},{4,0},{8,12},{12,8},{16,20},{20,16},{24,28},{28,24},{1,5},{5... | collective-permute-start | bytes 393224 | tf_op jit(solution)/shard_map/ppermute | solution.py:20
  83.5 7.1 %collective-permute-start.15 = (bf16[64,1024]{1,0:T(8,128)(2,1)S(1)}, bf16[64,1024]{1,0:T(8,128)(2,1)S(1)}, u32[]{:S(2)}, u32[]{:S(2)}) collective-permute-start(bf16[64,1024]{1,0:T(8,128)(2,1)S(1)} %collective-permute-done.13.refs_11_), channel_id=1, source_target_pairs={{0,1},{1,0},{2,3},{3,2},{4,5},{5,4},{6,7},{7,6},{8,9},{9,8},{10,11... | collective-permute-start | bytes 393224 | tf_op jit(solution)/shard_map/ppermute | solution.py:24
  83.6 13.3 %collective-permute-start.10 = (bf16[64,1024]{1,0:T(8,128)(2,1)S(1)}, bf16[64,1024]{1,0:T(8,128)(2,1)S(1)}, u32[]{:S(2)}, u32[]{:S(2)}) collective-permute-start(bf16[64,1024]{1,0:T(8,128)(2,1)S(1)} %collective-permute-done.8.refs_7_), channel_id=1, source_target_pairs={{0,2},{1,3},{2,0},{3,1},{4,6},{5,7},{6,4},{7,5},{8,10},{9,11},{10,... | collective-permute-start | bytes 393224 | tf_op jit(solution)/shard_map/ppermute | solution.py:24
  85.3 27.6 %collective-permute-start.4 = (bf16[8,128,256]{2,1,0:T(8,128)(2,1)}, bf16[8,128,256]{2,1,0:T(8,128)(2,1)S(1)}, u32[]{:S(2)}, u32[]{:S(2)}) collective-permute-start(bf16[8,128,256]{2,1,0:T(8,128)(2,1)} %get-tuple-element.12), channel_id=1, source_target_pairs={{0,1},{1,0},{2,3},{3,2},{4,5},{5,4},{6,7},{7,6},{8,9},{9,8},{10,11... | collective-permute-start | bytes 1572872 | tf_op jit(solution)/shard_map/ppermute | solution.py:24
  85.4 39.0 %collective-permute-start.5 = (bf16[8,128,256]{2,1,0:T(8,128)(2,1)}, bf16[8,128,256]{2,1,0:T(8,128)(2,1)S(1)}, u32[]{:S(2)}, u32[]{:S(2)}) collective-permute-start(bf16[8,128,256]{2,1,0:T(8,128)(2,1)} %get-tuple-element.13), channel_id=1, source_target_pairs={{0,2},{1,3},{2,0},{3,1},{4,6},{5,7},{6,4},{7,5},{8,10},{9,11},{10,... | collective-permute-start | bytes 1572872 | tf_op jit(solution)/shard_map/ppermute | solution.py:24
  86.5 39.2 %collective-permute-start.6 = (bf16[8,128,256]{2,1,0:T(8,128)(2,1)}, bf16[8,128,256]{2,1,0:T(8,128)(2,1)S(1)}, u32[]{:S(2)}, u32[]{:S(2)}) collective-permute-start(bf16[8,128,256]{2,1,0:T(8,128)(2,1)} %get-tuple-element.14), channel_id=1, source_target_pairs={{0,3},{1,2},{2,1},{3,0},{4,7},{5,6},{6,5},{7,4},{8,11},{9,10},{10,... | collective-permute-start | bytes 1572872 | tf_op jit(solution)/shard_map/ppermute | solution.py:24
  90.6 7.3 %collective-permute-start.21 = (bf16[64,1024]{1,0:T(8,128)(2,1)S(1)}, bf16[64,1024]{1,0:T(8,128)(2,1)S(1)}, u32[]{:S(2)}, u32[]{:S(2)}) collective-permute-start(bf16[64,1024]{1,0:T(8,128)(2,1)S(1)} %collective-permute-done.13.refs_11_), channel_id=1, source_target_pairs={{0,4},{4,0},{8,12},{12,8},{16,20},{20,16},{24,28},{28,24},{1,5},{5... | collective-permute-start | bytes 393224 | tf_op jit(solution)/shard_map/ppermute | solution.py:20
  96.9 1.9 collective-permute-start.17
  97.9 1.3 collective-permute-start.22
  98.8 1.3 collective-permute-start.18
  99.2 1.3 collective-permute-start.23
  100.1 1.3 collective-permute-start.19
  136.3 1.3 copy-start
  (2 other events, 2.0 us)
Sparse Core Ops, SparseCore 0:
  10.4 146.5 all-gather.1

commit v3 on v2

--- a/solution.py
+++ b/solution.py
@@ -414,8 +414,10 @@
     in_rows = lax.all_to_all(in_cast, "head", 0, 0).reshape(heads_axis * rows, 3 * width)
 
     whole = gather_cycle(packed(both(0, hidden_width)))
-    in_depth = jnp.concatenate(by_depth(in_rows), axis=0)
-    out_parts = by_depth(after(attn_out.T.astype(jnp.bfloat16), in_depth))
+    out_parts = by_depth(attn_out.T.astype(jnp.bfloat16))
+    in_parts = by_depth(after(in_rows, out_parts))
+    in_parts, out_first = lax.optimization_barrier((in_parts, across_first(out_parts)))
+    in_depth = jnp.concatenate(in_parts, axis=0)
     in_blocks = [(in_depth, 0), (swap_seq(in_depth, 1), 1)]
 
     contexts, caches, count = [], [], prompts // ATTENTION_CALLS
@@ -424,7 +426,7 @@
             lengths, place, tokens, in_blocks, heads_axis, start, count, caches
         )
         contexts.append([own, swap_head(one, 1), swap_head(two, 2), swap_head(three, 3)])
-    out_blocks = other_core(across_second(across_first(out_parts)))
+    out_blocks = other_core(across_second(out_first))
     normed = project(place, tokens, contexts, out_blocks, norm_gain, norm_shift, rows, 0)
     normed = normed.reshape(prompts * row_count, model_width)
     whole = after(whole, normed)

time: 193 us -> 185 us (0.959)
  starting transfers between devices: 40.3 us -> 31.5 us
  blocking collectives: 5.93 us -> 0 us
  Pallas kernels: 52.1 us -> 57.5 us
  waiting for transfers between devices: 71.2 us -> 68.4 us
  local copies, waits for them, and re-layouts: 3.87 us -> 6.42 us
    ppermute x15, waiting for transfers between devices: 21.4 us -> 9.28 us  [swap_seq(): lax.ppermute(x, 'seq', [(i, i ^ k) for i in range(lax.axis_size('seq'))])]
    ppermute x9, waiting for transfers between devices: 30.4 us -> 40.3 us  [swap_head(): lax.ppermute(x, 'head', [(i, i ^ k) for i in range(lax.axis_size('head'))])]
    ppermute x15, starting transfers between devices: 19 us -> 11.3 us  [swap_seq(): lax.ppermute(x, 'seq', [(i, i ^ k) for i in range(lax.axis_size('seq'))])]
    all_to_all x1 -> x0, blocking collectives: 5.93 us -> none  [shards(): lax.all_to_all(in_cast, 'head', 0, 0).reshape(heads_axis * rows, 3 * width)]
    pallas_call x1, Pallas kernels: 15.1 us -> 20.5 us  [attention(): pl.pallas_call(functools.partial(attention_kernel, [s for _, s in weight_...]
    ppermute x9, starting transfers between devices: 21.2 us -> 16.6 us  [swap_head(): lax.ppermute(x, 'head', [(i, i ^ k) for i in range(lax.axis_size('head'))])]
    all_gather x1, waiting for transfers between devices: 19.4 us -> 15.5 us  [gather_cycle(): lax.all_gather(x, ('seq', 'head'), axis=0, tiled=True, axis_index_groups=...]
    all_to_all x0 -> x1, starting transfers between devices: none -> 3.63 us  [shards(): lax.all_to_all(in_cast, 'head', 0, 0).reshape(heads_axis * rows, 3 * width)]
  transfers between devices with their start and end apart: 25 -> 26, of which waited for: 17 -> 15; matrix products, arithmetic and copies ran while one was open for 1% -> 3% of each run, Pallas kernels for 13% -> 17%
where the time goes in v3:
time: 185 us; the launch traced here: 182 us
  waiting for transfers between devices  68.4 us (37%)
  Pallas kernels  57.5 us (31%)
  starting transfers between devices  31.5 us (17%)
  between operations  14.2 us (8%)
  local copies, waits for them, and re-layouts  6.42 us (3%)
  other arithmetic  3.65 us (2%)
    ppermute x9, waiting for transfers between devices, swap_head(): lax.ppermute(x, 'head', [(i, i ^ k) for i in range(lax.axis_size('head'))])  40.3 us
    pallas_call x1, Pallas kernels, mlp(): pl.pallas_call(functools.partial(mlp_kernel, order, rows, chunk), out_sha...  27.5 us
    pallas_call x1, Pallas kernels, attention(): pl.pallas_call(functools.partial(attention_kernel, [s for _, s in weight_...  20.5 us
    ppermute x9, starting transfers between devices, swap_head(): lax.ppermute(x, 'head', [(i, i ^ k) for i in range(lax.axis_size('head'))])  16.6 us
    all_gather x1, waiting for transfers between devices, gather_cycle(): lax.all_gather(x, ('seq', 'head'), axis=0, tiled=True, axis_index_groups=...  15.5 us
    ppermute x15, starting transfers between devices, swap_seq(): lax.ppermute(x, 'seq', [(i, i ^ k) for i in range(lax.axis_size('seq'))])  11.3 us
    pallas_call x1, Pallas kernels, project(): pl.pallas_call(functools.partial(project_kernel, places, heads_axis, rows...  9.52 us
    ppermute x15, waiting for transfers between devices, swap_seq(): lax.ppermute(x, 'seq', [(i, i ^ k) for i in range(lax.axis_size('seq'))])  9.28 us
  transfers between devices with their start and end apart: 26, of which 15 were waited for; matrix products, arithmetic and copies ran while one was open for 3% of the time, Pallas kernels for 17%

profile of v3, /device:TPU:15, one launch (start us, length us, event | category | flops | bytes accessed | tf_op | source)
XLA Modules:
  0.0 181.7 jit_solution(13190815695047540660)
XLA Ops:
  7.2 1.1 convert.7
  8.4 1.1 convert_bitcast_fusion
  9.4 0.8 pad_maximum_fusion
  10.3 2.4 %collective-permute-start.1 = (bf16[32,1024]{1,0:T(8,128)(2,1)S(1)}, bf16[32,1024]{1,0:T(8,128)(2,1)S(1)}, u32[]{:S(2)}, u32[]{:S(2)}) collective-permute-start(bf16[32,1024]{1,0:T(8,128)(2,1)S(1)} %convert_bitcast_fusion.1), channel_id=1, source_target_pairs={{0,16},{4,20},{8,24},{12,28},{16,0},{20,4},{24,8},{28,12},{1,17},{... | collective-permute-start | bytes 196616 | tf_op jit(solution)/shard_map/ppermute | solution.py:20
  13.4 0.9 reshape.19
  14.3 3.6 %all-to-all-start = ((bf16[4,32,768]{2,1,0:T(8,128)(2,1)}), bf16[4,32,768]{2,1,0:T(8,128)(2,1)S(1)}, u32[]{:S(2)}, u32[]{:S(2)}) async-start(bf16[4,32,768]{2,1,0:T(8,128)(2,1)} %reshape.19), calls=%async_computation | async-start | bytes 393216 | tf_op jit(solution)/shard_map/all_to_all | solution.py:414
  18.6 3.3 %all-to-all-done = bf16[4,32,768]{2,1,0:T(8,128)(2,1)S(1)} async-done(((bf16[4,32,768]{2,1,0:T(8,128)(2,1)}), bf16[4,32,768]{2,1,0:T(8,128)(2,1)S(1)}, u32[]{:S(2)}, u32[]{:S(2)}) %all-to-all-start) | async-done | bytes 196640 | tf_op jit(solution)/shard_map/all_to_all | solution.py:414
  21.9 1.6 collective-permute-start.3
  23.5 2.0 %collective-permute-start.4 = (bf16[128,768]{1,0:T(8,128)(2,1)S(1)}, bf16[128,768]{1,0:T(8,128)(2,1)S(1)}, u32[]{:S(2)}, u32[]{:S(2)}) collective-permute-start(bf16[128,768]{1,0:T(8,128)(2,1)S(1)} %bitcast.16), channel_id=1, source_target_pairs={{0,16},{4,20},{8,24},{12,28},{16,0},{20,4},{24,8},{28,12},{1,17},{... | collective-permute-start | bytes 589832 | tf_op jit(solution)/shard_map/ppermute | solution.py:20
  25.8 1.9 %collective-permute-done.8.refs_11_ = bf16[64,1024]{1,0:T(8,128)(2,1)S(1)} collective-permute-done((bf16[64,1024]{1,0:T(8,128)(2,1)S(1)}, bf16[64,1024]{1,0:T(8,128)(2,1)S(1)}, u32[]{:S(2)}, u32[]{:S(2)}) %collective-permute-start.8) | collective-permute-done | bytes 131104 | tf_op jit(solution)/shard_map/ppermute | solution.py:24
  27.7 0.9 collective-permute-done.9.refs_12_
  28.8 6.6 %collective-permute-done.6.refs_7_ = bf16[64,1024]{1,0:T(8,128)(2,1)S(1)} collective-permute-done((bf16[64,1024]{1,0:T(8,128)(2,1)S(1)}, bf16[64,1024]{1,0:T(8,128)(2,1)S(1)}, u32[]{:S(2)}, u32[]{:S(2)}) %collective-permute-start.6) | collective-permute-done | bytes 131104 | tf_op jit(solution)/shard_map/ppermute | solution.py:24
  35.6 6.2 %collective-permute-done.5 = bf16[128,768]{1,0:T(8,128)(2,1)S(1)} collective-permute-done((bf16[128,768]{1,0:T(8,128)(2,1)S(1)}, bf16[128,768]{1,0:T(8,128)(2,1)S(1)}, u32[]{:S(2)}, u32[]{:S(2)}) %collective-permute-start.5) | collective-permute-done | bytes 196640 | tf_op jit(solution)/shard_map/ppermute | solution.py:20
  41.9 0.7 constant_dynamic-update-slice_fusion.5
  42.6 0.7 constant_dynamic-update-slice_fusion.4
  44.6 2.4 %collective-permute-start.10 = (bf16[512,768]{1,0:T(8,128)(2,1)}, bf16[512,768]{1,0:T(8,128)(2,1)}, u32[]{:S(2)}, u32[]{:S(2)}) collective-permute-start(bf16[512,768]{1,0:T(8,128)(2,1)} %constant_dynamic-update-slice_fusion.2.refs_3_), channel_id=1, source_target_pairs={{0,4},{4,0},{8,12},{12,8},{16,20},{20,16},{24,28},{28,24},{1,5},{5... | collective-permute-start | bytes 2359304 | tf_op jit(solution)/shard_map/ppermute | solution.py:20
  47.6 10.8 %collective-permute-start.14 = (bf16[64,1024]{1,0:T(8,128)(2,1)S(1)}, bf16[64,1024]{1,0:T(8,128)(2,1)S(1)}, u32[]{:S(2)}, u32[]{:S(2)}) collective-permute-start(bf16[64,1024]{1,0:T(8,128)(2,1)S(1)} %collective-permute-done.6.refs_7_), channel_id=1, source_target_pairs={{0,2},{1,3},{2,0},{3,1},{4,6},{5,7},{6,4},{7,5},{8,10},{9,11},{10,... | collective-permute-start | bytes 393224 | tf_op jit(solution)/shard_map/ppermute | solution.py:24
  58.7 2.4 %collective-permute-start.15 = (bf16[64,1024]{1,0:T(8,128)(2,1)S(1)}, bf16[64,1024]{1,0:T(8,128)(2,1)S(1)}, u32[]{:S(2)}, u32[]{:S(2)}) collective-permute-start(bf16[64,1024]{1,0:T(8,128)(2,1)S(1)} %collective-permute-done.8.refs_11_), channel_id=1, source_target_pairs={{0,1},{1,0},{2,3},{3,2},{4,5},{5,4},{6,7},{7,6},{8,9},{9,8},{10,11... | collective-permute-start | bytes 393224 | tf_op jit(solution)/shard_map/ppermute | solution.py:24
  61.6 20.5 %attention.1 = (bf16[8,512,256]{2,1,0:T(8,128)(2,1)}, bf16[8,512,256]{2,1,0:T(8,128)(2,1)}, bf16[8,128,256]{2,1,0:T(8,128)(2,1)}, bf16[8,128,256]{2,1,0:T(8,128)...) custom-call(s32[8]{0:T(128)} %lengths_ref.1, s32[2]{0:T(128)} %pad_add_fusion.refs_1_.refs_0_.place_ref, ...), custom_call_target="tpu_custom_call" | custom-call | flops 10737418240 | bytes 16777216 | tf_op jit(solution)/shard_map/attention/pallas_call | solution.py:174
  82.1 1.0 collective-permute-start.12
  83.2 1.6 collective-permute-start.13
  85.3 1.0 collective-permute-done.18.refs_16_
  86.8 0.8 collective-permute-done.21.refs_19_
  88.2 0.8 collective-permute-done.19.refs_17_
  89.2 18.0 %collective-permute-done.11.refs_3_ = bf16[8,128,256]{2,1,0:T(8,128)(2,1)S(1)} collective-permute-done((bf16[8,128,256]{2,1,0:T(8,128)(2,1)}, bf16[8,128,256]{2,1,0:T(8,128)(2,1)S(1)}, u32[]{:S(2)}, u32[]{:S(2)}) %collective-permute-start.11) | collective-permute-done | bytes 524320 | tf_op jit(solution)/shard_map/ppermute | solution.py:24
  107.2 11.6 %collective-permute-done.12.refs_4_ = bf16[8,128,256]{2,1,0:T(8,128)(2,1)S(1)} collective-permute-done((bf16[8,128,256]{2,1,0:T(8,128)(2,1)}, bf16[8,128,256]{2,1,0:T(8,128)(2,1)S(1)}, u32[]{:S(2)}, u32[]{:S(2)}) %collective-permute-start.12) | collective-permute-done | bytes 524320 | tf_op jit(solution)/shard_map/ppermute | solution.py:24
  118.9 1.0 collective-permute-done.13.refs_5_
  119.9 1.1 copy-done.1
  121.0 9.5 %project.1 = bf16[8,128,1024]{2,1,0:T(8,128)(2,1)S(1)} custom-call(s32[2]{0:T(128)S(1)} %copy-done.4, bf16[8,512,1024]{2,1,0:T(8,128)(2,1)} %refs_1_.1, bf16[8,128,256]{2,1,0:T(8,128)(2,1)S(1)} %copy-done.1, bf16[8,128,256]{2,1,0:T(8,128)(2,1)S(1)} %collective-permute-done.11.refs_3_, bf16[8,128,256]{2,1,0:T(8,128)(2,1)S(1)} %collective-permute-done.12.refs_4_, ...), custom_call_target="tpu_custom_call" | custom-call | flops 2147483648 | bytes 8388608 | tf_op jit(solution)/shard_map/project/pallas_call | solution.py:257
  130.5 1.3 copy-done
  131.9 15.5 %all-gather.2.cloned.1.call-done.whole_ref = bf16[1024,8192]{1,0:T(8,128)(2,1)} async-done(((bf16[32,8192]{1,0:T(8,128)(2,1)}), bf16[1024,8192]{1,0:T(8,128)(2,1)}) %all-gather.2.cloned.1.call-update) | async-done | bytes 16777232 | tf_op jit(solution)/shard_map/all_gather | solution.py:75
  147.4 27.5 %mlp.1 = bf16[8,128,1024]{2,1,0:T(8,128)(2,1)} custom-call(s32[8]{0:T(128)} %lengths_ref.1, s32[2]{0:T(128)} %pad_add_fusion.refs_1_.refs_0_.place_ref, bf16[1024,1024]{1,0:T(8,128)(2,1)} %bitcast.13, bf16[1024,8192]{1,0:T(8,128)(2,1)} %all-gather.2.cloned.1.call-done.whole_ref, f32[2,1024]{1,0:T(2,128)} %gain_ref.1, f32[2,1024]{1,0:T(2,128)} %shift_ref.1), custom_call_target="tpu_custom_call" | custom-call | flops 17179869184 | bytes 23068672 | tf_op jit(solution)/shard_map/mlp/pallas_call | solution.py:364
  (54 shorter events, 6.8 us)
Async XLA Ops:
  7.2 3.1 %copy-start.6 = (f32[1024,32]{0,1:T(8,128)S(1)}, f32[1024,32]{0,1:T(8,128)}, u32[]{:S(2)}) copy-start(f32[1024,32]{0,1:T(8,128)} %param.11) | copy-start | bytes 393220
  7.2 5.9 %copy-start.5 = (f32[32,3,1024]{2,0,1:T(8,128)S(1)}, f32[32,3,1024]{2,0,1:T(8,128)}, u32[]{:S(2)}) copy-start(f32[32,3,1024]{2,0,1:T(8,128)} %param.10) | copy-start | bytes 1179652
  7.2 140.2 %all-gather.2.cloned.1.call-start = ((), (), s32[]{:S(2)}) async-start(), calls=%async_computation.1 | async-start | bytes 17301504 | tf_op jit(solution)/shard_map/all_gather | solution.py:75
  10.3 7.6 %collective-permute-start.1 = (bf16[32,1024]{1,0:T(8,128)(2,1)S(1)}, bf16[32,1024]{1,0:T(8,128)(2,1)S(1)}, u32[]{:S(2)}, u32[]{:S(2)}) collective-permute-start(bf16[32,1024]{1,0:T(8,128)(2,1)S(1)} %convert_bitcast_fusion.1), channel_id=1, source_target_pairs={{0,16},{4,20},{8,24},{12,28},{16,0},{20,4},{24,8},{28,12},{1,17},{... | collective-permute-start | bytes 196616 | tf_op jit(solution)/shard_map/ppermute | solution.py:20
  12.7 5.9 %collective-permute-start = (bf16[32,1024]{1,0:T(8,128)(2,1)S(1)}, bf16[32,1024]{1,0:T(8,128)(2,1)S(1)}, u32[]{:S(2)}, u32[]{:S(2)}) collective-permute-start(bf16[32,1024]{1,0:T(8,128)(2,1)S(1)} %convert_bitcast_fusion.1), channel_id=1, source_target_pairs={{0,8},{4,12},{8,0},{12,4},{16,24},{20,28},{24,16},{28,20},{1,9},{5... | collective-permute-start | bytes 196616 | tf_op jit(solution)/shard_map/ppermute | solution.py:20
  12.9 5.2 %collective-permute-start.2 = (bf16[32,1024]{1,0:T(8,128)(2,1)S(1)}, bf16[32,1024]{1,0:T(8,128)(2,1)S(1)}, u32[]{:S(2)}, u32[]{:S(2)}) collective-permute-start(bf16[32,1024]{1,0:T(8,128)(2,1)S(1)} %convert_bitcast_fusion.1), channel_id=1, source_target_pairs={{0,24},{4,28},{8,16},{12,20},{16,8},{20,12},{24,0},{28,4},{1,25},{... | collective-permute-start | bytes 196616 | tf_op jit(solution)/shard_map/ppermute | solution.py:20
  14.3 7.6 %all-to-all-start = ((bf16[4,32,768]{2,1,0:T(8,128)(2,1)}), bf16[4,32,768]{2,1,0:T(8,128)(2,1)S(1)}, u32[]{:S(2)}, u32[]{:S(2)}) async-start(bf16[4,32,768]{2,1,0:T(8,128)(2,1)} %reshape.19), calls=%async_computation | async-start | bytes 393216 | tf_op jit(solution)/shard_map/all_to_all | solution.py:414
  18.1 9.6 %collective-permute-start.8 = (bf16[64,1024]{1,0:T(8,128)(2,1)S(1)}, bf16[64,1024]{1,0:T(8,128)(2,1)S(1)}, u32[]{:S(2)}, u32[]{:S(2)}) collective-permute-start(bf16[64,1024]{1,0:T(8,128)(2,1)S(1)} %constant_dynamic-update-slice_fusion.refs_10_), channel_id=1, source_target_pairs={{0,2},{1,3},{2,0},{3,1},{4,6},{5,7},{6,4},{7,5},{8,10},{9,11},{10,... | collective-permute-start | bytes 393224 | tf_op jit(solution)/shard_map/ppermute | solution.py:24
  18.4 10.2 %collective-permute-start.9 = (bf16[64,1024]{1,0:T(8,128)(2,1)S(1)}, bf16[64,1024]{1,0:T(8,128)(2,1)S(1)}, u32[]{:S(2)}, u32[]{:S(2)}) collective-permute-start(bf16[64,1024]{1,0:T(8,128)(2,1)S(1)} %constant_dynamic-update-slice_fusion.refs_10_), channel_id=1, source_target_pairs={{0,1},{1,0},{2,3},{3,2},{4,5},{5,4},{6,7},{7,6},{8,9},{9,8},{10,11... | collective-permute-start | bytes 393224 | tf_op jit(solution)/shard_map/ppermute | solution.py:24
  21.9 13.7 %collective-permute-start.3 = (bf16[128,768]{1,0:T(8,128)(2,1)S(1)}, bf16[128,768]{1,0:T(8,128)(2,1)S(1)}, u32[]{:S(2)}, u32[]{:S(2)}) collective-permute-start(bf16[128,768]{1,0:T(8,128)(2,1)S(1)} %bitcast.15), channel_id=1, source_target_pairs={{0,8},{4,12},{8,0},{12,4},{16,24},{20,28},{24,16},{28,20},{1,9},{5... | collective-permute-start | bytes 589832 | tf_op jit(solution)/shard_map/ppermute | solution.py:20
  23.5 12.2 %collective-permute-start.4 = (bf16[128,768]{1,0:T(8,128)(2,1)S(1)}, bf16[128,768]{1,0:T(8,128)(2,1)S(1)}, u32[]{:S(2)}, u32[]{:S(2)}) collective-permute-start(bf16[128,768]{1,0:T(8,128)(2,1)S(1)} %bitcast.16), channel_id=1, source_target_pairs={{0,16},{4,20},{8,24},{12,28},{16,0},{20,4},{24,8},{28,12},{1,17},{... | collective-permute-start | bytes 589832 | tf_op jit(solution)/shard_map/ppermute | solution.py:20
  25.5 16.4 %collective-permute-start.5 = (bf16[128,768]{1,0:T(8,128)(2,1)S(1)}, bf16[128,768]{1,0:T(8,128)(2,1)S(1)}, u32[]{:S(2)}, u32[]{:S(2)}) collective-permute-start(bf16[128,768]{1,0:T(8,128)(2,1)S(1)} %bitcast.17), channel_id=1, source_target_pairs={{0,24},{4,28},{8,16},{12,20},{16,8},{20,12},{24,0},{28,4},{1,25},{... | collective-permute-start | bytes 589832 | tf_op jit(solution)/shard_map/ppermute | solution.py:20
  27.7 7.7 %collective-permute-start.6 = (bf16[64,1024]{1,0:T(8,128)(2,1)S(1)}, bf16[64,1024]{1,0:T(8,128)(2,1)S(1)}, u32[]{:S(2)}, u32[]{:S(2)}) collective-permute-start(bf16[64,1024]{1,0:T(8,128)(2,1)S(1)} %pad_maximum_fusion.1.refs_6_), channel_id=1, source_target_pairs={{0,1},{1,0},{2,3},{3,2},{4,5},{5,4},{6,7},{7,6},{8,9},{9,8},{10,11... | collective-permute-start | bytes 393224 | tf_op jit(solution)/shard_map/ppermute | solution.py:24
  28.6 7.1 %collective-permute-start.7 = (bf16[64,1024]{1,0:T(8,128)(2,1)S(1)}, bf16[64,1024]{1,0:T(8,128)(2,1)S(1)}, u32[]{:S(2)}, u32[]{:S(2)}) collective-permute-start(bf16[64,1024]{1,0:T(8,128)(2,1)S(1)} %pad_maximum_fusion.1.refs_6_), channel_id=1, source_target_pairs={{0,2},{1,3},{2,0},{3,1},{4,6},{5,7},{6,4},{7,5},{8,10},{9,11},{10,... | collective-permute-start | bytes 393224 | tf_op jit(solution)/shard_map/ppermute | solution.py:24
  44.6 16.9 %collective-permute-start.10 = (bf16[512,768]{1,0:T(8,128)(2,1)}, bf16[512,768]{1,0:T(8,128)(2,1)}, u32[]{:S(2)}, u32[]{:S(2)}) collective-permute-start(bf16[512,768]{1,0:T(8,128)(2,1)} %constant_dynamic-update-slice_fusion.2.refs_3_), channel_id=1, source_target_pairs={{0,4},{4,0},{8,12},{12,8},{16,20},{20,16},{24,28},{28,24},{1,5},{5... | collective-permute-start | bytes 2359304 | tf_op jit(solution)/shard_map/ppermute | solution.py:20
  47.6 72.3 %copy-start.2 = (f32[2,1024]{1,0:T(2,128)S(1)}, f32[2,1024]{1,0:T(2,128)}, u32[]{:S(2)}) copy-start(f32[2,1024]{1,0:T(2,128)} %gain_ref.1) | copy-start | bytes 24580
  47.6 72.3 %copy-start.3 = (f32[2,1024]{1,0:T(2,128)S(1)}, f32[2,1024]{1,0:T(2,128)}, u32[]{:S(2)}) copy-start(f32[2,1024]{1,0:T(2,128)} %shift_ref.1) | copy-start | bytes 24580
  47.6 72.3 %copy-start.4 = (s32[2]{0:T(128)S(1)}, s32[2]{0:T(128)}, u32[]{:S(2)}) copy-start(s32[2]{0:T(128)} %pad_add_fusion.refs_1_.refs_0_.place_ref) | copy-start | bytes 28
  47.6 34.5 %collective-permute-start.14 = (bf16[64,1024]{1,0:T(8,128)(2,1)S(1)}, bf16[64,1024]{1,0:T(8,128)(2,1)S(1)}, u32[]{:S(2)}, u32[]{:S(2)}) collective-permute-start(bf16[64,1024]{1,0:T(8,128)(2,1)S(1)} %collective-permute-done.6.refs_7_), channel_id=1, source_target_pairs={{0,2},{1,3},{2,0},{3,1},{4,6},{5,7},{6,4},{7,5},{8,10},{9,11},{10,... | collective-permute-start | bytes 393224 | tf_op jit(solution)/shard_map/ppermute | solution.py:24
  58.4 26.7 %collective-permute-start.17 = (bf16[64,1024]{1,0:T(8,128)(2,1)S(1)}, bf16[64,1024]{1,0:T(8,128)(2,1)S(1)}, u32[]{:S(2)}, u32[]{:S(2)}) collective-permute-start(bf16[64,1024]{1,0:T(8,128)(2,1)S(1)} %collective-permute-done.6.refs_7_), channel_id=1, source_target_pairs={{0,4},{4,0},{8,12},{12,8},{16,20},{20,16},{24,28},{28,24},{1,5},{5... | collective-permute-start | bytes 393224 | tf_op jit(solution)/shard_map/ppermute | solution.py:20
  58.7 24.5 %collective-permute-start.15 = (bf16[64,1024]{1,0:T(8,128)(2,1)S(1)}, bf16[64,1024]{1,0:T(8,128)(2,1)S(1)}, u32[]{:S(2)}, u32[]{:S(2)}) collective-permute-start(bf16[64,1024]{1,0:T(8,128)(2,1)S(1)} %collective-permute-done.8.refs_11_), channel_id=1, source_target_pairs={{0,1},{1,0},{2,3},{3,2},{4,5},{5,4},{6,7},{7,6},{8,9},{9,8},{10,11... | collective-permute-start | bytes 393224 | tf_op jit(solution)/shard_map/ppermute | solution.py:24
  61.1 23.7 %collective-permute-start.16 = (bf16[64,1024]{1,0:T(8,128)(2,1)S(1)}, bf16[64,1024]{1,0:T(8,128)(2,1)S(1)}, u32[]{:S(2)}, u32[]{:S(2)}) collective-permute-start(bf16[64,1024]{1,0:T(8,128)(2,1)S(1)} %pad_maximum_fusion.1.refs_6_), channel_id=1, source_target_pairs={{0,4},{4,0},{8,12},{12,8},{16,20},{20,16},{24,28},{28,24},{1,5},{5... | collective-permute-start | bytes 393224 | tf_op jit(solution)/shard_map/ppermute | solution.py:20
  82.1 25.2 %collective-permute-start.11 = (bf16[8,128,256]{2,1,0:T(8,128)(2,1)}, bf16[8,128,256]{2,1,0:T(8,128)(2,1)S(1)}, u32[]{:S(2)}, u32[]{:S(2)}) collective-permute-start(bf16[8,128,256]{2,1,0:T(8,128)(2,1)} %get-tuple-element.27), channel_id=1, source_target_pairs={{0,1},{1,0},{2,3},{3,2},{4,5},{5,4},{6,7},{7,6},{8,9},{9,8},{10,11... | collective-permute-start | bytes 1572872 | tf_op jit(solution)/shard_map/ppermute | solution.py:24
  82.1 36.7 %collective-permute-start.12 = (bf16[8,128,256]{2,1,0:T(8,128)(2,1)}, bf16[8,128,256]{2,1,0:T(8,128)(2,1)S(1)}, u32[]{:S(2)}, u32[]{:S(2)}) collective-permute-start(bf16[8,128,256]{2,1,0:T(8,128)(2,1)} %get-tuple-element.28), channel_id=1, source_target_pairs={{0,2},{1,3},{2,0},{3,1},{4,6},{5,7},{6,4},{7,5},{8,10},{9,11},{10,... | collective-permute-start | bytes 1572872 | tf_op jit(solution)/shard_map/ppermute | solution.py:24
  83.2 36.7 %collective-permute-start.13 = (bf16[8,128,256]{2,1,0:T(8,128)(2,1)}, bf16[8,128,256]{2,1,0:T(8,128)(2,1)S(1)}, u32[]{:S(2)}, u32[]{:S(2)}) collective-permute-start(bf16[8,128,256]{2,1,0:T(8,128)(2,1)} %get-tuple-element.29), channel_id=1, source_target_pairs={{0,3},{1,2},{2,1},{3,0},{4,7},{5,6},{6,5},{7,4},{8,11},{9,10},{10,... | collective-permute-start | bytes 1572872 | tf_op jit(solution)/shard_map/ppermute | solution.py:24
  84.8 1.5 collective-permute-start.18
  85.2 1.3 collective-permute-start.20
  86.3 1.3 collective-permute-start.21
  86.5 1.3 collective-permute-start.22
  87.6 1.3 collective-permute-start.19
  87.9 1.3 collective-permute-start.23
  130.5 1.3 copy-start
  (1 other events, 1.1 us)
Sparse Core Ops, SparseCore 0:
  10.4 136.8 all-gather.1

commit v4 on v3

--- a/solution.py
+++ b/solution.py
@@ -30,11 +30,6 @@
 
 def after(x, *done):
     return lax.optimization_barrier((x, done))[0]
-
-
-def along_depth(x):
-    groups = [[d + core for d in depths()] for core in range(2)]
-    return lax.all_gather(x, "seq", axis=0, tiled=True, axis_index_groups=groups)
 
 
 def by_depth(x):
@@ -400,8 +395,6 @@
     row_count = seq_len // heads_axis
     rows = mlp_in.shape[0]
     place = jnp.stack([lax.axis_index("seq"), lax.axis_index("head")]).astype(jnp.int32)
-    half = hidden_width // 2
-    quarter = hidden_width // 4
 
     def both(start, stop):
         return [mlp_in[:, start:stop], mlp_out.T[:, start:stop]]
@@ -416,7 +409,9 @@
     whole = gather_cycle(packed(both(0, hidden_width)))
     out_parts = by_depth(attn_out.T.astype(jnp.bfloat16))
     in_parts = by_depth(after(in_rows, out_parts))
-    in_parts, out_first = lax.optimization_barrier((in_parts, across_first(out_parts)))
+    out_blocks = across_second(across_first(out_parts))
+    in_parts, arrived = lax.optimization_barrier((in_parts, [block for block, _ in out_blocks]))
+    out_blocks = [(block, at) for block, (_, at) in zip(arrived, out_blocks)]
     in_depth = jnp.concatenate(in_parts, axis=0)
     in_blocks = [(in_depth, 0), (swap_seq(in_depth, 1), 1)]
 
@@ -426,7 +421,7 @@
             lengths, place, tokens, in_blocks, heads_axis, start, count, caches
         )
         contexts.append([own, swap_head(one, 1), swap_head(two, 2), swap_head(three, 3)])
-    out_blocks = other_core(across_second(out_first))
+    out_blocks = other_core(out_blocks)
     normed = project(place, tokens, contexts, out_blocks, norm_gain, norm_shift, rows, 0)
     normed = normed.reshape(prompts * row_count, model_width)
     whole = after(whole, normed)

time: 185 us -> 181 us (0.978); the launches traced: 182 us -> 181 us
    ppermute x9, waiting for transfers between devices: 40.3 us -> 44 us  [swap_head(): lax.ppermute(x, 'head', [(i, i ^ k) for i in range(lax.axis_size('head'))])]
    all_to_all x1, waiting for transfers between devices: 3.32 us -> 0.78 us  [shards(): lax.all_to_all(in_cast, 'head', 0, 0).reshape(heads_axis * rows, 3 * width)]
  transfers between devices with their start and end apart: 26 -> 26, of which waited for: 15 -> 17; matrix products, arithmetic and copies ran while one was open for 3% -> 3% of each run, Pallas kernels for 17% -> 17%
where the time goes in v4:
time: 181 us
  waiting for transfers between devices  68.8 us (38%)
  Pallas kernels  57.5 us (32%)
  starting transfers between devices  30.2 us (17%)
  between operations  14.2 us (8%)
  local copies, waits for them, and re-layouts  6.38 us (4%)
  other arithmetic  3.65 us (2%)
    ppermute x9, waiting for transfers between devices, swap_head(): lax.ppermute(x, 'head', [(i, i ^ k) for i in range(lax.axis_size('head'))])  44 us
    pallas_call x1, Pallas kernels, mlp(): pl.pallas_call(functools.partial(mlp_kernel, order, rows, chunk), out_sha...  27.5 us
    pallas_call x1, Pallas kernels, attention(): pl.pallas_call(functools.partial(attention_kernel, [s for _, s in weight_...  20.5 us
    ppermute x9, starting transfers between devices, swap_head(): lax.ppermute(x, 'head', [(i, i ^ k) for i in range(lax.axis_size('head'))])  16.2 us
    all_gather x1, waiting for transfers between devices, gather_cycle(): lax.all_gather(x, ('seq', 'head'), axis=0, tiled=True, axis_index_groups=...  15.1 us
    ppermute x15, starting transfers between devices, swap_seq(): lax.ppermute(x, 'seq', [(i, i ^ k) for i in range(lax.axis_size('seq'))])  10.3 us
    pallas_call x1, Pallas kernels, project(): pl.pallas_call(functools.partial(project_kernel, places, heads_axis, rows...  9.52 us
    ppermute x15, waiting for transfers between devices, swap_seq(): lax.ppermute(x, 'seq', [(i, i ^ k) for i in range(lax.axis_size('seq'))])  8.88 us
  transfers between devices with their start and end apart: 26, of which 17 were waited for; matrix products, arithmetic and copies ran while one was open for 3% of the time, Pallas kernels for 17%

profile of v4, /device:TPU:15, one launch (start us, length us, event | category | flops | bytes accessed | tf_op | source)
XLA Modules:
  0.0 180.7 jit_solution(3255933029332366365)
XLA Ops:
  7.2 1.1 convert.7
  8.4 1.1 convert_bitcast_fusion
  9.4 0.8 pad_maximum_fusion
  10.3 2.4 %collective-permute-start.1 = (bf16[32,1024]{1,0:T(8,128)(2,1)S(1)}, bf16[32,1024]{1,0:T(8,128)(2,1)S(1)}, u32[]{:S(2)}, u32[]{:S(2)}) collective-permute-start(bf16[32,1024]{1,0:T(8,128)(2,1)S(1)} %convert_bitcast_fusion.1), channel_id=1, source_target_pairs={{0,16},{4,20},{8,24},{12,28},{16,0},{20,4},{24,8},{28,12},{1,17},{... | collective-permute-start | bytes 196616 | tf_op jit(solution)/shard_map/ppermute | solution.py:20
  13.4 0.9 reshape.19
  14.3 3.6 %all-to-all-start = ((bf16[4,32,768]{2,1,0:T(8,128)(2,1)}), bf16[4,32,768]{2,1,0:T(8,128)(2,1)S(1)}, u32[]{:S(2)}, u32[]{:S(2)}) async-start(bf16[4,32,768]{2,1,0:T(8,128)(2,1)} %reshape.19), calls=%async_computation | async-start | bytes 393216 | tf_op jit(solution)/shard_map/all_to_all | solution.py:407
  18.6 1.3 collective-permute-start.6
  19.9 1.2 collective-permute-start.7
  21.1 0.8 all-to-all-done
  21.9 1.6 collective-permute-start.3
  23.5 4.2 %collective-permute-done.9.refs_11_ = bf16[64,1024]{1,0:T(8,128)(2,1)S(1)} collective-permute-done((bf16[64,1024]{1,0:T(8,128)(2,1)S(1)}, bf16[64,1024]{1,0:T(8,128)(2,1)S(1)}, u32[]{:S(2)}, u32[]{:S(2)}) %collective-permute-start.9) | collective-permute-done | bytes 131104 | tf_op jit(solution)/shard_map/ppermute | solution.py:24
  27.7 3.1 %collective-permute-start.4 = (bf16[128,768]{1,0:T(8,128)(2,1)S(1)}, bf16[128,768]{1,0:T(8,128)(2,1)S(1)}, u32[]{:S(2)}, u32[]{:S(2)}) collective-permute-start(bf16[128,768]{1,0:T(8,128)(2,1)S(1)} %bitcast.16), channel_id=1, source_target_pairs={{0,16},{4,20},{8,24},{12,28},{16,0},{20,4},{24,8},{28,12},{1,17},{... | collective-permute-start | bytes 589832 | tf_op jit(solution)/shard_map/ppermute | solution.py:20
  30.8 3.4 %collective-permute-done.6.refs_7_ = bf16[64,1024]{1,0:T(8,128)(2,1)S(1)} collective-permute-done((bf16[64,1024]{1,0:T(8,128)(2,1)S(1)}, bf16[64,1024]{1,0:T(8,128)(2,1)S(1)}, u32[]{:S(2)}, u32[]{:S(2)}) %collective-permute-start.6) | collective-permute-done | bytes 131104 | tf_op jit(solution)/shard_map/ppermute | solution.py:24
  34.2 1.2 collective-permute-start.11
  35.4 6.2 %collective-permute-done.11.refs_13_ = bf16[64,1024]{1,0:T(8,128)(2,1)S(1)} collective-permute-done((bf16[64,1024]{1,0:T(8,128)(2,1)S(1)}, bf16[64,1024]{1,0:T(8,128)(2,1)S(1)}, u32[]{:S(2)}, u32[]{:S(2)}) %collective-permute-start.11) | collective-permute-done | bytes 131104 | tf_op jit(solution)/shard_map/ppermute | solution.py:24
  41.5 1.1 collective-permute-done.8.refs_9_
  43.2 4.2 %collective-permute-done.5 = bf16[128,768]{1,0:T(8,128)(2,1)S(1)} collective-permute-done((bf16[128,768]{1,0:T(8,128)(2,1)S(1)}, bf16[128,768]{1,0:T(8,128)(2,1)S(1)}, u32[]{:S(2)}, u32[]{:S(2)}) %collective-permute-start.5) | collective-permute-done | bytes 196640 | tf_op jit(solution)/shard_map/ppermute | solution.py:20
  50.2 0.9 collective-permute-start.12
  52.2 1.2 collective-permute-done.12.refs_4_
  53.3 20.5 %attention.1 = (bf16[8,512,256]{2,1,0:T(8,128)(2,1)}, bf16[8,512,256]{2,1,0:T(8,128)(2,1)}, bf16[8,128,256]{2,1,0:T(8,128)(2,1)}, bf16[8,128,256]{2,1,0:T(8,128)...) custom-call(s32[8]{0:T(128)} %lengths_ref.1, s32[2]{0:T(128)} %pad_add_fusion.refs_1_.refs_0_.place_ref, ...), custom_call_target="tpu_custom_call" | custom-call | flops 10737418240 | bytes 16777216 | tf_op jit(solution)/shard_map/attention/pallas_call | solution.py:169
  74.3 10.6 %collective-permute-start.14 = (bf16[8,128,256]{2,1,0:T(8,128)(2,1)}, bf16[8,128,256]{2,1,0:T(8,128)(2,1)S(1)}, u32[]{:S(2)}, u32[]{:S(2)}) collective-permute-start(bf16[8,128,256]{2,1,0:T(8,128)(2,1)} %get-tuple-element.30), channel_id=1, source_target_pairs={{0,2},{1,3},{2,0},{3,1},{4,6},{5,7},{6,4},{7,5},{8,10},{9,11},{10,... | collective-permute-start | bytes 1572872 | tf_op jit(solution)/shard_map/ppermute | solution.py:24
  84.8 1.1 collective-permute-start.15
  86.4 0.8 collective-permute-done.18.refs_16_
  87.8 0.8 collective-permute-done.20.refs_18_
  89.1 0.8 collective-permute-done.22.refs_20_
  90.2 9.2 %collective-permute-done.13.refs_3_ = bf16[8,128,256]{2,1,0:T(8,128)(2,1)S(1)} collective-permute-done((bf16[8,128,256]{2,1,0:T(8,128)(2,1)}, bf16[8,128,256]{2,1,0:T(8,128)(2,1)S(1)}, u32[]{:S(2)}, u32[]{:S(2)}) %collective-permute-start.13) | collective-permute-done | bytes 524320 | tf_op jit(solution)/shard_map/ppermute | solution.py:24
  99.4 19.9 %collective-permute-done.14.refs_4_ = bf16[8,128,256]{2,1,0:T(8,128)(2,1)S(1)} collective-permute-done((bf16[8,128,256]{2,1,0:T(8,128)(2,1)}, bf16[8,128,256]{2,1,0:T(8,128)(2,1)S(1)}, u32[]{:S(2)}, u32[]{:S(2)}) %collective-permute-start.14) | collective-permute-done | bytes 524320 | tf_op jit(solution)/shard_map/ppermute | solution.py:24
  119.3 1.1 copy-done.1
  120.4 9.5 %project.1 = bf16[8,128,1024]{2,1,0:T(8,128)(2,1)S(1)} custom-call(s32[2]{0:T(128)S(1)} %copy-done.4, bf16[8,512,1024]{2,1,0:T(8,128)(2,1)} %refs_1_.1, bf16[8,128,256]{2,1,0:T(8,128)(2,1)S(1)} %copy-done.1, bf16[8,128,256]{2,1,0:T(8,128)(2,1)S(1)} %collective-permute-done.13.refs_3_, bf16[8,128,256]{2,1,0:T(8,128)(2,1)S(1)} %collective-permute-done.14.refs_4_, ...), custom_call_target="tpu_custom_call" | custom-call | flops 2147483648 | bytes 8388608 | tf_op jit(solution)/shard_map/project/pallas_call | solution.py:252
  129.9 1.3 copy-done
  131.3 15.1 %all-gather.2.cloned.1.call-done.whole_ref = bf16[1024,8192]{1,0:T(8,128)(2,1)} async-done(((bf16[32,8192]{1,0:T(8,128)(2,1)}), bf16[1024,8192]{1,0:T(8,128)(2,1)}) %all-gather.2.cloned.1.call-update) | async-done | bytes 16777232 | tf_op jit(solution)/shard_map/all_gather | solution.py:70
  146.4 27.5 %mlp.1 = bf16[8,128,1024]{2,1,0:T(8,128)(2,1)} custom-call(s32[8]{0:T(128)} %lengths_ref.1, s32[2]{0:T(128)} %pad_add_fusion.refs_1_.refs_0_.place_ref, bf16[1024,1024]{1,0:T(8,128)(2,1)} %bitcast.13, bf16[1024,8192]{1,0:T(8,128)(2,1)} %all-gather.2.cloned.1.call-done.whole_ref, f32[2,1024]{1,0:T(2,128)} %gain_ref.1, f32[2,1024]{1,0:T(2,128)} %shift_ref.1), custom_call_target="tpu_custom_call" | custom-call | flops 17179869184 | bytes 23068672 | tf_op jit(solution)/shard_map/mlp/pallas_call | solution.py:359
  (54 shorter events, 8.0 us)
Async XLA Ops:
  7.2 3.1 %copy-start.6 = (f32[1024,32]{0,1:T(8,128)S(1)}, f32[1024,32]{0,1:T(8,128)}, u32[]{:S(2)}) copy-start(f32[1024,32]{0,1:T(8,128)} %param.11) | copy-start | bytes 393220
  7.2 5.9 %copy-start.5 = (f32[32,3,1024]{2,0,1:T(8,128)S(1)}, f32[32,3,1024]{2,0,1:T(8,128)}, u32[]{:S(2)}) copy-start(f32[32,3,1024]{2,0,1:T(8,128)} %param.10) | copy-start | bytes 1179652
  7.2 139.2 %all-gather.2.cloned.1.call-start = ((), (), s32[]{:S(2)}) async-start(), calls=%async_computation.1 | async-start | bytes 17301504 | tf_op jit(solution)/shard_map/all_gather | solution.py:70
  10.3 7.6 %collective-permute-start.1 = (bf16[32,1024]{1,0:T(8,128)(2,1)S(1)}, bf16[32,1024]{1,0:T(8,128)(2,1)S(1)}, u32[]{:S(2)}, u32[]{:S(2)}) collective-permute-start(bf16[32,1024]{1,0:T(8,128)(2,1)S(1)} %convert_bitcast_fusion.1), channel_id=1, source_target_pairs={{0,16},{4,20},{8,24},{12,28},{16,0},{20,4},{24,8},{28,12},{1,17},{... | collective-permute-start | bytes 196616 | tf_op jit(solution)/shard_map/ppermute | solution.py:20
  12.7 5.9 %collective-permute-start = (bf16[32,1024]{1,0:T(8,128)(2,1)S(1)}, bf16[32,1024]{1,0:T(8,128)(2,1)S(1)}, u32[]{:S(2)}, u32[]{:S(2)}) collective-permute-start(bf16[32,1024]{1,0:T(8,128)(2,1)S(1)} %convert_bitcast_fusion.1), channel_id=1, source_target_pairs={{0,8},{4,12},{8,0},{12,4},{16,24},{20,28},{24,16},{28,20},{1,9},{5... | collective-permute-start | bytes 196616 | tf_op jit(solution)/shard_map/ppermute | solution.py:20
  12.9 5.2 %collective-permute-start.2 = (bf16[32,1024]{1,0:T(8,128)(2,1)S(1)}, bf16[32,1024]{1,0:T(8,128)(2,1)S(1)}, u32[]{:S(2)}, u32[]{:S(2)}) collective-permute-start(bf16[32,1024]{1,0:T(8,128)(2,1)S(1)} %convert_bitcast_fusion.1), channel_id=1, source_target_pairs={{0,24},{4,28},{8,16},{12,20},{16,8},{20,12},{24,0},{28,4},{1,25},{... | collective-permute-start | bytes 196616 | tf_op jit(solution)/shard_map/ppermute | solution.py:20
  14.3 7.6 %all-to-all-start = ((bf16[4,32,768]{2,1,0:T(8,128)(2,1)}), bf16[4,32,768]{2,1,0:T(8,128)(2,1)S(1)}, u32[]{:S(2)}, u32[]{:S(2)}) async-start(bf16[4,32,768]{2,1,0:T(8,128)(2,1)} %reshape.19), calls=%async_computation | async-start | bytes 393216 | tf_op jit(solution)/shard_map/all_to_all | solution.py:407
  18.1 9.6 %collective-permute-start.9 = (bf16[64,1024]{1,0:T(8,128)(2,1)S(1)}, bf16[64,1024]{1,0:T(8,128)(2,1)S(1)}, u32[]{:S(2)}, u32[]{:S(2)}) collective-permute-start(bf16[64,1024]{1,0:T(8,128)(2,1)S(1)} %constant_dynamic-update-slice_fusion.refs_10_), channel_id=1, source_target_pairs={{0,2},{1,3},{2,0},{3,1},{4,6},{5,7},{6,4},{7,5},{8,10},{9,11},{10,... | collective-permute-start | bytes 393224 | tf_op jit(solution)/shard_map/ppermute | solution.py:24
  18.4 12.5 %collective-permute-start.10 = (bf16[64,1024]{1,0:T(8,128)(2,1)S(1)}, bf16[64,1024]{1,0:T(8,128)(2,1)S(1)}, u32[]{:S(2)}, u32[]{:S(2)}) collective-permute-start(bf16[64,1024]{1,0:T(8,128)(2,1)S(1)} %constant_dynamic-update-slice_fusion.refs_10_), channel_id=1, source_target_pairs={{0,1},{1,0},{2,3},{3,2},{4,5},{5,4},{6,7},{7,6},{8,9},{9,8},{10,11... | collective-permute-start | bytes 393224 | tf_op jit(solution)/shard_map/ppermute | solution.py:24
  18.6 15.6 %collective-permute-start.6 = (bf16[64,1024]{1,0:T(8,128)(2,1)S(1)}, bf16[64,1024]{1,0:T(8,128)(2,1)S(1)}, u32[]{:S(2)}, u32[]{:S(2)}) collective-permute-start(bf16[64,1024]{1,0:T(8,128)(2,1)S(1)} %pad_maximum_fusion.1.refs_6_), channel_id=1, source_target_pairs={{0,1},{1,0},{2,3},{3,2},{4,5},{5,4},{6,7},{7,6},{8,9},{9,8},{10,11... | collective-permute-start | bytes 393224 | tf_op jit(solution)/shard_map/ppermute | solution.py:24
  19.9 15.5 %collective-permute-start.7 = (bf16[64,1024]{1,0:T(8,128)(2,1)S(1)}, bf16[64,1024]{1,0:T(8,128)(2,1)S(1)}, u32[]{:S(2)}, u32[]{:S(2)}) collective-permute-start(bf16[64,1024]{1,0:T(8,128)(2,1)S(1)} %pad_maximum_fusion.1.refs_6_), channel_id=1, source_target_pairs={{0,2},{1,3},{2,0},{3,1},{4,6},{5,7},{6,4},{7,5},{8,10},{9,11},{10,... | collective-permute-start | bytes 393224 | tf_op jit(solution)/shard_map/ppermute | solution.py:24
  21.9 20.7 %collective-permute-start.3 = (bf16[128,768]{1,0:T(8,128)(2,1)S(1)}, bf16[128,768]{1,0:T(8,128)(2,1)S(1)}, u32[]{:S(2)}, u32[]{:S(2)}) collective-permute-start(bf16[128,768]{1,0:T(8,128)(2,1)S(1)} %bitcast.15), channel_id=1, source_target_pairs={{0,8},{4,12},{8,0},{12,4},{16,24},{20,28},{24,16},{28,20},{1,9},{5... | collective-permute-start | bytes 589832 | tf_op jit(solution)/shard_map/ppermute | solution.py:20
  27.7 15.5 %collective-permute-start.4 = (bf16[128,768]{1,0:T(8,128)(2,1)S(1)}, bf16[128,768]{1,0:T(8,128)(2,1)S(1)}, u32[]{:S(2)}, u32[]{:S(2)}) collective-permute-start(bf16[128,768]{1,0:T(8,128)(2,1)S(1)} %bitcast.16), channel_id=1, source_target_pairs={{0,16},{4,20},{8,24},{12,28},{16,0},{20,4},{24,8},{28,12},{1,17},{... | collective-permute-start | bytes 589832 | tf_op jit(solution)/shard_map/ppermute | solution.py:20
  30.8 16.6 %collective-permute-start.5 = (bf16[128,768]{1,0:T(8,128)(2,1)S(1)}, bf16[128,768]{1,0:T(8,128)(2,1)S(1)}, u32[]{:S(2)}, u32[]{:S(2)}) collective-permute-start(bf16[128,768]{1,0:T(8,128)(2,1)S(1)} %bitcast.17), channel_id=1, source_target_pairs={{0,24},{4,28},{8,16},{12,20},{16,8},{20,12},{24,0},{28,4},{1,25},{... | collective-permute-start | bytes 589832 | tf_op jit(solution)/shard_map/ppermute | solution.py:20
  34.2 7.3 %collective-permute-start.11 = (bf16[64,1024]{1,0:T(8,128)(2,1)S(1)}, bf16[64,1024]{1,0:T(8,128)(2,1)S(1)}, u32[]{:S(2)}, u32[]{:S(2)}) collective-permute-start(bf16[64,1024]{1,0:T(8,128)(2,1)S(1)} %collective-permute-done.9.refs_11_), channel_id=1, source_target_pairs={{0,1},{1,0},{2,3},{3,2},{4,5},{5,4},{6,7},{7,6},{8,9},{9,8},{10,11... | collective-permute-start | bytes 393224 | tf_op jit(solution)/shard_map/ppermute | solution.py:24
  35.4 7.3 %collective-permute-start.8 = (bf16[64,1024]{1,0:T(8,128)(2,1)S(1)}, bf16[64,1024]{1,0:T(8,128)(2,1)S(1)}, u32[]{:S(2)}, u32[]{:S(2)}) collective-permute-start(bf16[64,1024]{1,0:T(8,128)(2,1)S(1)} %collective-permute-done.6.refs_7_), channel_id=1, source_target_pairs={{0,2},{1,3},{2,0},{3,1},{4,6},{5,7},{6,4},{7,5},{8,10},{9,11},{10,... | collective-permute-start | bytes 393224 | tf_op jit(solution)/shard_map/ppermute | solution.py:24
  50.2 3.2 %collective-permute-start.12 = (bf16[512,768]{1,0:T(8,128)(2,1)}, bf16[512,768]{1,0:T(8,128)(2,1)}, u32[]{:S(2)}, u32[]{:S(2)}) collective-permute-start(bf16[512,768]{1,0:T(8,128)(2,1)} %constant_dynamic-update-slice_fusion.2.refs_3_), channel_id=1, source_target_pairs={{0,4},{4,0},{8,12},{12,8},{16,20},{20,16},{24,28},{28,24},{1,5},{5... | collective-permute-start | bytes 2359304 | tf_op jit(solution)/shard_map/ppermute | solution.py:20
  51.7 67.7 %copy-start.2 = (f32[2,1024]{1,0:T(2,128)S(1)}, f32[2,1024]{1,0:T(2,128)}, u32[]{:S(2)}) copy-start(f32[2,1024]{1,0:T(2,128)} %gain_ref.1) | copy-start | bytes 24580
  51.7 67.7 %copy-start.3 = (f32[2,1024]{1,0:T(2,128)S(1)}, f32[2,1024]{1,0:T(2,128)}, u32[]{:S(2)}) copy-start(f32[2,1024]{1,0:T(2,128)} %shift_ref.1) | copy-start | bytes 24580
  51.7 67.7 %copy-start.4 = (s32[2]{0:T(128)S(1)}, s32[2]{0:T(128)}, u32[]{:S(2)}) copy-start(s32[2]{0:T(128)} %pad_add_fusion.refs_1_.refs_0_.place_ref) | copy-start | bytes 28
  51.7 34.2 %collective-permute-start.16 = (bf16[64,1024]{1,0:T(8,128)(2,1)S(1)}, bf16[64,1024]{1,0:T(8,128)(2,1)S(1)}, u32[]{:S(2)}, u32[]{:S(2)}) collective-permute-start(bf16[64,1024]{1,0:T(8,128)(2,1)S(1)} %pad_maximum_fusion.1.refs_6_), channel_id=1, source_target_pairs={{0,4},{4,0},{8,12},{12,8},{16,20},{20,16},{24,28},{28,24},{1,5},{5... | collective-permute-start | bytes 393224 | tf_op jit(solution)/shard_map/ppermute | solution.py:20
  51.7 34.2 %collective-permute-start.17 = (bf16[64,1024]{1,0:T(8,128)(2,1)S(1)}, bf16[64,1024]{1,0:T(8,128)(2,1)S(1)}, u32[]{:S(2)}, u32[]{:S(2)}) collective-permute-start(bf16[64,1024]{1,0:T(8,128)(2,1)S(1)} %collective-permute-done.6.refs_7_), channel_id=1, source_target_pairs={{0,4},{4,0},{8,12},{12,8},{16,20},{20,16},{24,28},{28,24},{1,5},{5... | collective-permute-start | bytes 393224 | tf_op jit(solution)/shard_map/ppermute | solution.py:20
  73.9 25.5 %collective-permute-start.13 = (bf16[8,128,256]{2,1,0:T(8,128)(2,1)}, bf16[8,128,256]{2,1,0:T(8,128)(2,1)S(1)}, u32[]{:S(2)}, u32[]{:S(2)}) collective-permute-start(bf16[8,128,256]{2,1,0:T(8,128)(2,1)} %get-tuple-element.29), channel_id=1, source_target_pairs={{0,1},{1,0},{2,3},{3,2},{4,5},{5,4},{6,7},{7,6},{8,9},{9,8},{10,11... | collective-permute-start | bytes 1572872 | tf_op jit(solution)/shard_map/ppermute | solution.py:24
  74.3 45.0 %collective-permute-start.14 = (bf16[8,128,256]{2,1,0:T(8,128)(2,1)}, bf16[8,128,256]{2,1,0:T(8,128)(2,1)S(1)}, u32[]{:S(2)}, u32[]{:S(2)}) collective-permute-start(bf16[8,128,256]{2,1,0:T(8,128)(2,1)} %get-tuple-element.30), channel_id=1, source_target_pairs={{0,2},{1,3},{2,0},{3,1},{4,6},{5,7},{6,4},{7,5},{8,10},{9,11},{10,... | collective-permute-start | bytes 1572872 | tf_op jit(solution)/shard_map/ppermute | solution.py:24
  84.8 34.5 %collective-permute-start.15 = (bf16[8,128,256]{2,1,0:T(8,128)(2,1)}, bf16[8,128,256]{2,1,0:T(8,128)(2,1)S(1)}, u32[]{:S(2)}, u32[]{:S(2)}) collective-permute-start(bf16[8,128,256]{2,1,0:T(8,128)(2,1)} %get-tuple-element.31), channel_id=1, source_target_pairs={{0,3},{1,2},{2,1},{3,0},{4,7},{5,6},{6,5},{7,4},{8,11},{9,10},{10,... | collective-permute-start | bytes 1572872 | tf_op jit(solution)/shard_map/ppermute | solution.py:24
  85.9 1.3 collective-permute-start.18
  85.9 1.5 collective-permute-start.19
  87.3 1.3 collective-permute-start.20
  87.5 1.3 collective-permute-start.21
  88.6 1.3 collective-permute-start.22
  88.8 1.3 collective-permute-start.23
  129.9 1.3 copy-start
  (1 other events, 1.1 us)
Sparse Core Ops, SparseCore 0:
  10.4 135.9 all-gather.1

commit v5 on v4

--- a/solution.py
+++ b/solution.py
@@ -52,12 +52,12 @@
 
 
 def cycle():
-    seq = list(range(lax.axis_size("seq")))
-    order = []
-    for n in range(len(seq) // 2):
-        for h in across_order()[:: 1 if n % 2 == 0 else -1]:
-            order.extend([(2 * n, h), (2 * n + 1, h)])
-    return order
+    heads = across_order()
+    levels = depths()
+    chips = [(d, heads[0]) for d in levels]
+    for n, d in enumerate(levels[::-1]):
+        chips.extend((d, h) for h in (heads[1:] if n % 2 == 0 else heads[:0:-1]))
+    return [(d + core, h) for d, h in chips for core in range(2)]
 
 
 def across_order():

time: 181 us -> 181 us (level)
  waiting for transfers between devices: 68.8 us -> 72.2 us
  Pallas kernels: 57.5 us -> 54.1 us
    pallas_call x1, Pallas kernels: 20.5 us -> 17.1 us  [attention(): pl.pallas_call(functools.partial(attention_kernel, [s for _, s in weight_...]
    all_gather x1, waiting for transfers between devices: 15.1 us -> 18.4 us  [gather_cycle(): lax.all_gather(x, ('seq', 'head'), axis=0, tiled=True, axis_index_groups=...]
  transfers between devices with their start and end apart: 26 -> 26, of which waited for: 17 -> 16; matrix products, arithmetic and copies ran while one was open for 3% -> 3% of each run, Pallas kernels for 17% -> 15%
where the time goes in v5:
time: 181 us
  waiting for transfers between devices  72.2 us (40%)
  Pallas kernels  54.1 us (30%)
  starting transfers between devices  30.2 us (17%)
  between operations  14.2 us (8%)
  local copies, waits for them, and re-layouts  6.36 us (4%)
  other arithmetic  3.65 us (2%)
    ppermute x9, waiting for transfers between devices, swap_head(): lax.ppermute(x, 'head', [(i, i ^ k) for i in range(lax.axis_size('head'))])  44.1 us
    pallas_call x1, Pallas kernels, mlp(): pl.pallas_call(functools.partial(mlp_kernel, order, rows, chunk), out_sha...  27.5 us
    all_gather x1, waiting for transfers between devices, gather_cycle(): lax.all_gather(x, ('seq', 'head'), axis=0, tiled=True, axis_index_groups=...  18.4 us
    pallas_call x1, Pallas kernels, attention(): pl.pallas_call(functools.partial(attention_kernel, [s for _, s in weight_...  17.1 us
    ppermute x9, starting transfers between devices, swap_head(): lax.ppermute(x, 'head', [(i, i ^ k) for i in range(lax.axis_size('head'))])  16.2 us
    ppermute x15, starting transfers between devices, swap_seq(): lax.ppermute(x, 'seq', [(i, i ^ k) for i in range(lax.axis_size('seq'))])  10.3 us
    pallas_call x1, Pallas kernels, project(): pl.pallas_call(functools.partial(project_kernel, places, heads_axis, rows...  9.5 us
    ppermute x15, waiting for transfers between devices, swap_seq(): lax.ppermute(x, 'seq', [(i, i ^ k) for i in range(lax.axis_size('seq'))])  8.88 us
  transfers between devices with their start and end apart: 26, of which 16 were waited for; matrix products, arithmetic and copies ran while one was open for 3% of the time, Pallas kernels for 15%

profile of v5, /device:TPU:15, one launch (start us, length us, event | category | flops | bytes accessed | tf_op | source)
XLA Modules:
  0.0 180.7 jit_solution(14564584590217235075)
XLA Ops:
  7.2 1.1 convert.7
  8.4 1.1 convert_bitcast_fusion
  9.4 0.8 pad_maximum_fusion
  10.3 2.4 %collective-permute-start.1 = (bf16[32,1024]{1,0:T(8,128)(2,1)S(1)}, bf16[32,1024]{1,0:T(8,128)(2,1)S(1)}, u32[]{:S(2)}, u32[]{:S(2)}) collective-permute-start(bf16[32,1024]{1,0:T(8,128)(2,1)S(1)} %convert_bitcast_fusion.1), channel_id=1, source_target_pairs={{0,16},{4,20},{8,24},{12,28},{16,0},{20,4},{24,8},{28,12},{1,17},{... | collective-permute-start | bytes 196616 | tf_op jit(solution)/shard_map/ppermute | solution.py:20
  13.4 0.9 reshape.19
  14.3 3.6 %all-to-all-start = ((bf16[4,32,768]{2,1,0:T(8,128)(2,1)}), bf16[4,32,768]{2,1,0:T(8,128)(2,1)S(1)}, u32[]{:S(2)}, u32[]{:S(2)}) async-start(bf16[4,32,768]{2,1,0:T(8,128)(2,1)} %reshape.19), calls=%async_computation | async-start | bytes 393216 | tf_op jit(solution)/shard_map/all_to_all | solution.py:407
  18.6 1.3 collective-permute-start.6
  19.9 1.2 collective-permute-start.7
  21.1 0.8 all-to-all-done
  21.9 1.6 collective-permute-start.3
  23.5 4.2 %collective-permute-done.9.refs_11_ = bf16[64,1024]{1,0:T(8,128)(2,1)S(1)} collective-permute-done((bf16[64,1024]{1,0:T(8,128)(2,1)S(1)}, bf16[64,1024]{1,0:T(8,128)(2,1)S(1)}, u32[]{:S(2)}, u32[]{:S(2)}) %collective-permute-start.9) | collective-permute-done | bytes 131104 | tf_op jit(solution)/shard_map/ppermute | solution.py:24
  27.7 3.1 %collective-permute-start.4 = (bf16[128,768]{1,0:T(8,128)(2,1)S(1)}, bf16[128,768]{1,0:T(8,128)(2,1)S(1)}, u32[]{:S(2)}, u32[]{:S(2)}) collective-permute-start(bf16[128,768]{1,0:T(8,128)(2,1)S(1)} %bitcast.16), channel_id=1, source_target_pairs={{0,16},{4,20},{8,24},{12,28},{16,0},{20,4},{24,8},{28,12},{1,17},{... | collective-permute-start | bytes 589832 | tf_op jit(solution)/shard_map/ppermute | solution.py:20
  30.8 3.4 %collective-permute-done.6.refs_7_ = bf16[64,1024]{1,0:T(8,128)(2,1)S(1)} collective-permute-done((bf16[64,1024]{1,0:T(8,128)(2,1)S(1)}, bf16[64,1024]{1,0:T(8,128)(2,1)S(1)}, u32[]{:S(2)}, u32[]{:S(2)}) %collective-permute-start.6) | collective-permute-done | bytes 131104 | tf_op jit(solution)/shard_map/ppermute | solution.py:24
  34.2 1.2 collective-permute-start.11
  35.4 6.2 %collective-permute-done.11.refs_13_ = bf16[64,1024]{1,0:T(8,128)(2,1)S(1)} collective-permute-done((bf16[64,1024]{1,0:T(8,128)(2,1)S(1)}, bf16[64,1024]{1,0:T(8,128)(2,1)S(1)}, u32[]{:S(2)}, u32[]{:S(2)}) %collective-permute-start.11) | collective-permute-done | bytes 131104 | tf_op jit(solution)/shard_map/ppermute | solution.py:24
  41.5 1.1 collective-permute-done.8.refs_9_
  43.2 4.2 %collective-permute-done.5 = bf16[128,768]{1,0:T(8,128)(2,1)S(1)} collective-permute-done((bf16[128,768]{1,0:T(8,128)(2,1)S(1)}, bf16[128,768]{1,0:T(8,128)(2,1)S(1)}, u32[]{:S(2)}, u32[]{:S(2)}) %collective-permute-start.5) | collective-permute-done | bytes 196640 | tf_op jit(solution)/shard_map/ppermute | solution.py:20
  50.2 0.9 collective-permute-start.12
  52.2 1.2 collective-permute-done.12.refs_4_
  53.3 17.1 %attention.1 = (bf16[8,512,256]{2,1,0:T(8,128)(2,1)}, bf16[8,512,256]{2,1,0:T(8,128)(2,1)}, bf16[8,128,256]{2,1,0:T(8,128)(2,1)}, bf16[8,128,256]{2,1,0:T(8,128)...) custom-call(s32[8]{0:T(128)} %lengths_ref.1, s32[2]{0:T(128)} %pad_add_fusion.refs_1_.refs_0_.place_ref, ...), custom_call_target="tpu_custom_call" | custom-call | flops 10737418240 | bytes 16777216 | tf_op jit(solution)/shard_map/attention/pallas_call | solution.py:169
  70.9 10.5 %collective-permute-start.14 = (bf16[8,128,256]{2,1,0:T(8,128)(2,1)}, bf16[8,128,256]{2,1,0:T(8,128)(2,1)S(1)}, u32[]{:S(2)}, u32[]{:S(2)}) collective-permute-start(bf16[8,128,256]{2,1,0:T(8,128)(2,1)} %get-tuple-element.30), channel_id=1, source_target_pairs={{0,2},{1,3},{2,0},{3,1},{4,6},{5,7},{6,4},{7,5},{8,10},{9,11},{10,... | collective-permute-start | bytes 1572872 | tf_op jit(solution)/shard_map/ppermute | solution.py:24
  81.4 1.1 collective-permute-start.15
  83.0 0.8 collective-permute-done.18.refs_16_
  84.4 0.8 collective-permute-done.20.refs_18_
  85.7 0.8 collective-permute-done.22.refs_20_
  86.7 9.0 %collective-permute-done.13.refs_3_ = bf16[8,128,256]{2,1,0:T(8,128)(2,1)S(1)} collective-permute-done((bf16[8,128,256]{2,1,0:T(8,128)(2,1)}, bf16[8,128,256]{2,1,0:T(8,128)(2,1)S(1)}, u32[]{:S(2)}, u32[]{:S(2)}) %collective-permute-start.13) | collective-permute-done | bytes 524320 | tf_op jit(solution)/shard_map/ppermute | solution.py:24
  95.7 20.3 %collective-permute-done.14.refs_4_ = bf16[8,128,256]{2,1,0:T(8,128)(2,1)S(1)} collective-permute-done((bf16[8,128,256]{2,1,0:T(8,128)(2,1)}, bf16[8,128,256]{2,1,0:T(8,128)(2,1)S(1)}, u32[]{:S(2)}, u32[]{:S(2)}) %collective-permute-start.14) | collective-permute-done | bytes 524320 | tf_op jit(solution)/shard_map/ppermute | solution.py:24
  116.0 1.0 copy-done.1
  117.1 9.5 %project.1 = bf16[8,128,1024]{2,1,0:T(8,128)(2,1)S(1)} custom-call(s32[2]{0:T(128)S(1)} %copy-done.4, bf16[8,512,1024]{2,1,0:T(8,128)(2,1)} %refs_1_.1, bf16[8,128,256]{2,1,0:T(8,128)(2,1)S(1)} %copy-done.1, bf16[8,128,256]{2,1,0:T(8,128)(2,1)S(1)} %collective-permute-done.13.refs_3_, bf16[8,128,256]{2,1,0:T(8,128)(2,1)S(1)} %collective-permute-done.14.refs_4_, ...), custom_call_target="tpu_custom_call" | custom-call | flops 2147483648 | bytes 8388608 | tf_op jit(solution)/shard_map/project/pallas_call | solution.py:252
  126.6 1.3 copy-done
  127.9 18.4 %all-gather.2.cloned.1.call-done.whole_ref = bf16[1024,8192]{1,0:T(8,128)(2,1)} async-done(((bf16[32,8192]{1,0:T(8,128)(2,1)}), bf16[1024,8192]{1,0:T(8,128)(2,1)}) %all-gather.2.cloned.1.call-update) | async-done | bytes 16777232 | tf_op jit(solution)/shard_map/all_gather | solution.py:70
  146.4 27.5 %mlp.1 = bf16[8,128,1024]{2,1,0:T(8,128)(2,1)} custom-call(s32[8]{0:T(128)} %lengths_ref.1, s32[2]{0:T(128)} %pad_add_fusion.refs_1_.refs_0_.place_ref, bf16[1024,1024]{1,0:T(8,128)(2,1)} %bitcast.13, bf16[1024,8192]{1,0:T(8,128)(2,1)} %all-gather.2.cloned.1.call-done.whole_ref, f32[2,1024]{1,0:T(2,128)} %gain_ref.1, f32[2,1024]{1,0:T(2,128)} %shift_ref.1), custom_call_target="tpu_custom_call" | custom-call | flops 17179869184 | bytes 23068672 | tf_op jit(solution)/shard_map/mlp/pallas_call | solution.py:359
  (54 shorter events, 8.0 us)
Async XLA Ops:
  7.2 3.1 %copy-start.6 = (f32[1024,32]{0,1:T(8,128)S(1)}, f32[1024,32]{0,1:T(8,128)}, u32[]{:S(2)}) copy-start(f32[1024,32]{0,1:T(8,128)} %param.11) | copy-start | bytes 393220
  7.2 5.9 %copy-start.5 = (f32[32,3,1024]{2,0,1:T(8,128)S(1)}, f32[32,3,1024]{2,0,1:T(8,128)}, u32[]{:S(2)}) copy-start(f32[32,3,1024]{2,0,1:T(8,128)} %param.10) | copy-start | bytes 1179652
  7.2 139.2 %all-gather.2.cloned.1.call-start = ((), (), s32[]{:S(2)}) async-start(), calls=%async_computation.1 | async-start | bytes 17301504 | tf_op jit(solution)/shard_map/all_gather | solution.py:70
  10.3 7.6 %collective-permute-start.1 = (bf16[32,1024]{1,0:T(8,128)(2,1)S(1)}, bf16[32,1024]{1,0:T(8,128)(2,1)S(1)}, u32[]{:S(2)}, u32[]{:S(2)}) collective-permute-start(bf16[32,1024]{1,0:T(8,128)(2,1)S(1)} %convert_bitcast_fusion.1), channel_id=1, source_target_pairs={{0,16},{4,20},{8,24},{12,28},{16,0},{20,4},{24,8},{28,12},{1,17},{... | collective-permute-start | bytes 196616 | tf_op jit(solution)/shard_map/ppermute | solution.py:20
  12.7 5.9 %collective-permute-start = (bf16[32,1024]{1,0:T(8,128)(2,1)S(1)}, bf16[32,1024]{1,0:T(8,128)(2,1)S(1)}, u32[]{:S(2)}, u32[]{:S(2)}) collective-permute-start(bf16[32,1024]{1,0:T(8,128)(2,1)S(1)} %convert_bitcast_fusion.1), channel_id=1, source_target_pairs={{0,8},{4,12},{8,0},{12,4},{16,24},{20,28},{24,16},{28,20},{1,9},{5... | collective-permute-start | bytes 196616 | tf_op jit(solution)/shard_map/ppermute | solution.py:20
  12.9 5.2 %collective-permute-start.2 = (bf16[32,1024]{1,0:T(8,128)(2,1)S(1)}, bf16[32,1024]{1,0:T(8,128)(2,1)S(1)}, u32[]{:S(2)}, u32[]{:S(2)}) collective-permute-start(bf16[32,1024]{1,0:T(8,128)(2,1)S(1)} %convert_bitcast_fusion.1), channel_id=1, source_target_pairs={{0,24},{4,28},{8,16},{12,20},{16,8},{20,12},{24,0},{28,4},{1,25},{... | collective-permute-start | bytes 196616 | tf_op jit(solution)/shard_map/ppermute | solution.py:20
  14.3 7.6 %all-to-all-start = ((bf16[4,32,768]{2,1,0:T(8,128)(2,1)}), bf16[4,32,768]{2,1,0:T(8,128)(2,1)S(1)}, u32[]{:S(2)}, u32[]{:S(2)}) async-start(bf16[4,32,768]{2,1,0:T(8,128)(2,1)} %reshape.19), calls=%async_computation | async-start | bytes 393216 | tf_op jit(solution)/shard_map/all_to_all | solution.py:407
  18.1 9.6 %collective-permute-start.9 = (bf16[64,1024]{1,0:T(8,128)(2,1)S(1)}, bf16[64,1024]{1,0:T(8,128)(2,1)S(1)}, u32[]{:S(2)}, u32[]{:S(2)}) collective-permute-start(bf16[64,1024]{1,0:T(8,128)(2,1)S(1)} %constant_dynamic-update-slice_fusion.refs_10_), channel_id=1, source_target_pairs={{0,2},{1,3},{2,0},{3,1},{4,6},{5,7},{6,4},{7,5},{8,10},{9,11},{10,... | collective-permute-start | bytes 393224 | tf_op jit(solution)/shard_map/ppermute | solution.py:24
  18.4 12.5 %collective-permute-start.10 = (bf16[64,1024]{1,0:T(8,128)(2,1)S(1)}, bf16[64,1024]{1,0:T(8,128)(2,1)S(1)}, u32[]{:S(2)}, u32[]{:S(2)}) collective-permute-start(bf16[64,1024]{1,0:T(8,128)(2,1)S(1)} %constant_dynamic-update-slice_fusion.refs_10_), channel_id=1, source_target_pairs={{0,1},{1,0},{2,3},{3,2},{4,5},{5,4},{6,7},{7,6},{8,9},{9,8},{10,11... | collective-permute-start | bytes 393224 | tf_op jit(solution)/shard_map/ppermute | solution.py:24
  18.6 15.6 %collective-permute-start.6 = (bf16[64,1024]{1,0:T(8,128)(2,1)S(1)}, bf16[64,1024]{1,0:T(8,128)(2,1)S(1)}, u32[]{:S(2)}, u32[]{:S(2)}) collective-permute-start(bf16[64,1024]{1,0:T(8,128)(2,1)S(1)} %pad_maximum_fusion.1.refs_6_), channel_id=1, source_target_pairs={{0,1},{1,0},{2,3},{3,2},{4,5},{5,4},{6,7},{7,6},{8,9},{9,8},{10,11... | collective-permute-start | bytes 393224 | tf_op jit(solution)/shard_map/ppermute | solution.py:24
  19.9 15.5 %collective-permute-start.7 = (bf16[64,1024]{1,0:T(8,128)(2,1)S(1)}, bf16[64,1024]{1,0:T(8,128)(2,1)S(1)}, u32[]{:S(2)}, u32[]{:S(2)}) collective-permute-start(bf16[64,1024]{1,0:T(8,128)(2,1)S(1)} %pad_maximum_fusion.1.refs_6_), channel_id=1, source_target_pairs={{0,2},{1,3},{2,0},{3,1},{4,6},{5,7},{6,4},{7,5},{8,10},{9,11},{10,... | collective-permute-start | bytes 393224 | tf_op jit(solution)/shard_map/ppermute | solution.py:24
  21.9 20.7 %collective-permute-start.3 = (bf16[128,768]{1,0:T(8,128)(2,1)S(1)}, bf16[128,768]{1,0:T(8,128)(2,1)S(1)}, u32[]{:S(2)}, u32[]{:S(2)}) collective-permute-start(bf16[128,768]{1,0:T(8,128)(2,1)S(1)} %bitcast.15), channel_id=1, source_target_pairs={{0,8},{4,12},{8,0},{12,4},{16,24},{20,28},{24,16},{28,20},{1,9},{5... | collective-permute-start | bytes 589832 | tf_op jit(solution)/shard_map/ppermute | solution.py:20
  27.7 15.5 %collective-permute-start.4 = (bf16[128,768]{1,0:T(8,128)(2,1)S(1)}, bf16[128,768]{1,0:T(8,128)(2,1)S(1)}, u32[]{:S(2)}, u32[]{:S(2)}) collective-permute-start(bf16[128,768]{1,0:T(8,128)(2,1)S(1)} %bitcast.16), channel_id=1, source_target_pairs={{0,16},{4,20},{8,24},{12,28},{16,0},{20,4},{24,8},{28,12},{1,17},{... | collective-permute-start | bytes 589832 | tf_op jit(solution)/shard_map/ppermute | solution.py:20
  30.8 16.6 %collective-permute-start.5 = (bf16[128,768]{1,0:T(8,128)(2,1)S(1)}, bf16[128,768]{1,0:T(8,128)(2,1)S(1)}, u32[]{:S(2)}, u32[]{:S(2)}) collective-permute-start(bf16[128,768]{1,0:T(8,128)(2,1)S(1)} %bitcast.17), channel_id=1, source_target_pairs={{0,24},{4,28},{8,16},{12,20},{16,8},{20,12},{24,0},{28,4},{1,25},{... | collective-permute-start | bytes 589832 | tf_op jit(solution)/shard_map/ppermute | solution.py:20
  34.2 7.3 %collective-permute-start.11 = (bf16[64,1024]{1,0:T(8,128)(2,1)S(1)}, bf16[64,1024]{1,0:T(8,128)(2,1)S(1)}, u32[]{:S(2)}, u32[]{:S(2)}) collective-permute-start(bf16[64,1024]{1,0:T(8,128)(2,1)S(1)} %collective-permute-done.9.refs_11_), channel_id=1, source_target_pairs={{0,1},{1,0},{2,3},{3,2},{4,5},{5,4},{6,7},{7,6},{8,9},{9,8},{10,11... | collective-permute-start | bytes 393224 | tf_op jit(solution)/shard_map/ppermute | solution.py:24
  35.4 7.3 %collective-permute-start.8 = (bf16[64,1024]{1,0:T(8,128)(2,1)S(1)}, bf16[64,1024]{1,0:T(8,128)(2,1)S(1)}, u32[]{:S(2)}, u32[]{:S(2)}) collective-permute-start(bf16[64,1024]{1,0:T(8,128)(2,1)S(1)} %collective-permute-done.6.refs_7_), channel_id=1, source_target_pairs={{0,2},{1,3},{2,0},{3,1},{4,6},{5,7},{6,4},{7,5},{8,10},{9,11},{10,... | collective-permute-start | bytes 393224 | tf_op jit(solution)/shard_map/ppermute | solution.py:24
  50.2 3.2 %collective-permute-start.12 = (bf16[512,768]{1,0:T(8,128)(2,1)}, bf16[512,768]{1,0:T(8,128)(2,1)}, u32[]{:S(2)}, u32[]{:S(2)}) collective-permute-start(bf16[512,768]{1,0:T(8,128)(2,1)} %constant_dynamic-update-slice_fusion.2.refs_3_), channel_id=1, source_target_pairs={{0,4},{4,0},{8,12},{12,8},{16,20},{20,16},{24,28},{28,24},{1,5},{5... | collective-permute-start | bytes 2359304 | tf_op jit(solution)/shard_map/ppermute | solution.py:20
  51.7 64.4 %copy-start.2 = (f32[2,1024]{1,0:T(2,128)S(1)}, f32[2,1024]{1,0:T(2,128)}, u32[]{:S(2)}) copy-start(f32[2,1024]{1,0:T(2,128)} %gain_ref.1) | copy-start | bytes 24580
  51.7 64.4 %copy-start.3 = (f32[2,1024]{1,0:T(2,128)S(1)}, f32[2,1024]{1,0:T(2,128)}, u32[]{:S(2)}) copy-start(f32[2,1024]{1,0:T(2,128)} %shift_ref.1) | copy-start | bytes 24580
  51.7 64.4 %copy-start.4 = (s32[2]{0:T(128)S(1)}, s32[2]{0:T(128)}, u32[]{:S(2)}) copy-start(s32[2]{0:T(128)} %pad_add_fusion.refs_1_.refs_0_.place_ref) | copy-start | bytes 28
  51.7 30.8 %collective-permute-start.16 = (bf16[64,1024]{1,0:T(8,128)(2,1)S(1)}, bf16[64,1024]{1,0:T(8,128)(2,1)S(1)}, u32[]{:S(2)}, u32[]{:S(2)}) collective-permute-start(bf16[64,1024]{1,0:T(8,128)(2,1)S(1)} %pad_maximum_fusion.1.refs_6_), channel_id=1, source_target_pairs={{0,4},{4,0},{8,12},{12,8},{16,20},{20,16},{24,28},{28,24},{1,5},{5... | collective-permute-start | bytes 393224 | tf_op jit(solution)/shard_map/ppermute | solution.py:20
  51.7 30.8 %collective-permute-start.17 = (bf16[64,1024]{1,0:T(8,128)(2,1)S(1)}, bf16[64,1024]{1,0:T(8,128)(2,1)S(1)}, u32[]{:S(2)}, u32[]{:S(2)}) collective-permute-start(bf16[64,1024]{1,0:T(8,128)(2,1)S(1)} %collective-permute-done.6.refs_7_), channel_id=1, source_target_pairs={{0,4},{4,0},{8,12},{12,8},{16,20},{20,16},{24,28},{28,24},{1,5},{5... | collective-permute-start | bytes 393224 | tf_op jit(solution)/shard_map/ppermute | solution.py:20
  70.5 25.2 %collective-permute-start.13 = (bf16[8,128,256]{2,1,0:T(8,128)(2,1)}, bf16[8,128,256]{2,1,0:T(8,128)(2,1)S(1)}, u32[]{:S(2)}, u32[]{:S(2)}) collective-permute-start(bf16[8,128,256]{2,1,0:T(8,128)(2,1)} %get-tuple-element.29), channel_id=1, source_target_pairs={{0,1},{1,0},{2,3},{3,2},{4,5},{5,4},{6,7},{7,6},{8,9},{9,8},{10,11... | collective-permute-start | bytes 1572872 | tf_op jit(solution)/shard_map/ppermute | solution.py:24
  70.9 45.1 %collective-permute-start.14 = (bf16[8,128,256]{2,1,0:T(8,128)(2,1)}, bf16[8,128,256]{2,1,0:T(8,128)(2,1)S(1)}, u32[]{:S(2)}, u32[]{:S(2)}) collective-permute-start(bf16[8,128,256]{2,1,0:T(8,128)(2,1)} %get-tuple-element.30), channel_id=1, source_target_pairs={{0,2},{1,3},{2,0},{3,1},{4,6},{5,7},{6,4},{7,5},{8,10},{9,11},{10,... | collective-permute-start | bytes 1572872 | tf_op jit(solution)/shard_map/ppermute | solution.py:24
  81.4 34.6 %collective-permute-start.15 = (bf16[8,128,256]{2,1,0:T(8,128)(2,1)}, bf16[8,128,256]{2,1,0:T(8,128)(2,1)S(1)}, u32[]{:S(2)}, u32[]{:S(2)}) collective-permute-start(bf16[8,128,256]{2,1,0:T(8,128)(2,1)} %get-tuple-element.31), channel_id=1, source_target_pairs={{0,3},{1,2},{2,1},{3,0},{4,7},{5,6},{6,5},{7,4},{8,11},{9,10},{10,... | collective-permute-start | bytes 1572872 | tf_op jit(solution)/shard_map/ppermute | solution.py:24
  82.5 1.3 collective-permute-start.18
  82.5 1.5 collective-permute-start.19
  83.8 1.3 collective-permute-start.20
  84.0 1.3 collective-permute-start.21
  85.2 1.3 collective-permute-start.22
  85.4 1.3 collective-permute-start.23
  126.6 1.3 copy-start
  (1 other events, 1.0 us)
Sparse Core Ops, SparseCore 0:
  10.4 135.9 all-gather.1
